TPU v7x, 32 devices: a whole 2x2x4 slice. The times are simulated.
32 devices in a mesh: dp: 8 (over z, core), seq: 4 (over y, x).
Axes of the slice: x: 2, y: 2, z: 4, core: 2. Of those that a mesh axis runs over, the one named last changes fastest.
Arguments:
- queries: bfloat16 [8, 512, 2048], P('dp', 'seq'), may hold values from -8 to 8
- keys: bfloat16 [8, 512, 2048], P('dp', 'seq'), may hold values from -8 to 8
- values: bfloat16 [8, 512, 2048], P('dp', 'seq'), may hold values from -6 to 6
- out_weight: bfloat16 [2048, 2048], P('dp'), may hold values from -0.125 to 0.125
- cotangent: bfloat16 [8, 512, 2048], P('dp', 'seq'), may hold values from -6 to 6
- block_mask: int32 [8, 4, 4], P('dp'), may hold values from 0 to 1, as said below
Outputs:
- mixed: bfloat16 [8, 512, 2048], P('dp', 'seq')
- grad_queries: bfloat16 [8, 512, 2048], P('dp', 'seq')
- grad_keys: bfloat16 [8, 512, 2048], P('dp', 'seq')
- grad_values: bfloat16 [8, 512, 2048], P('dp', 'seq')
- grad_weight: float32 [2048, 2048], P('dp')
Inputs may be any that keep to these rules, and one draw needn't show every extreme that they name: block_mask[b, i, j] is 1 whenever blocks i and j lie in the same view, a view being 8 consecutive blocks (the whole sequence where it has fewer blocks).
All inputs are finite; a program needn't handle non-finite values.
Results may differ from a plain program's by a relative error of at most 0.0075.
Values may be sent and summed in bfloat16 or wider, within the bound.
No kernel may reach another device: no remote copies, remote signals or barrier semaphores. Data moves between devices by JAX's collectives and lax.ppermute only.
A program may use at most 128 MiB of HBM per device.

v0:
```python
import math

import jax
import jax.numpy as jnp
from jax import lax
from jax.experimental import pallas as pl
from jax.experimental.pallas import tpu as pltpu
from jax.sharding import PartitionSpec as P

DH = 128
HALF = DH // 2
LOG2E = 1.4426950408889634
F32 = jnp.float32
BF16 = jnp.bfloat16
VMEM_BYTES = 56 * 1024 * 1024


SMEM = pl.BlockSpec(memory_space=pltpu.SMEM)
VMEM = pl.BlockSpec(memory_space=pltpu.VMEM)
HBM = pl.BlockSpec(memory_space=pl.ANY)


def call(kernel, name, operands, in_specs, out_shape, out_specs, scratch=(), flops=0, after=()):
    extra = len(after)

    def body(*refs):
        kernel(*refs[: len(operands)], *refs[len(operands) + extra :])

    nbytes = sum(x.size * x.dtype.itemsize for x in (*operands, *out_shape))
    return pl.pallas_call(
        body,
        in_specs=list(in_specs) + [HBM] * extra,
        out_specs=list(out_specs),
        out_shape=list(out_shape),
        scratch_shapes=list(scratch),
        compiler_params=pltpu.CompilerParams(vmem_limit_bytes=VMEM_BYTES),
        cost_estimate=pl.CostEstimate(flops=flops, bytes_accessed=nbytes, transcendentals=0),
        name=name,
    )(*operands, *after)


def run_copies(pairs, sems, first=0):
    copies = [pltpu.make_async_copy(s, d, sems.at[first + i]) for i, (s, d) in enumerate(pairs)]
    for copy in copies:
        copy.start()
    return copies


def head_columns(place, block, head):
    column = 4 * jnp.bitwise_xor(place[2], head) + jnp.bitwise_xor(place[0], block)
    return pl.ds(pl.multiple_of(column * DH, DH), DH)


def split_kernel(place, query, key, value, o0, o1, o2, o3):
    for j, out in enumerate((o0, o1, o2, o3)):
        for index, source in enumerate((query, key, value)):
            for h in range(4):
                out[index, :, h * DH : (h + 1) * DH] = source[:, head_columns(place, j, h)]


def split_heads(place, queries, keys, values):
    tokens, width = queries.shape
    out = jax.ShapeDtypeStruct((3, tokens, width // 4), BF16)
    return call(split_kernel, "split_heads", (place, queries, keys, values), [SMEM] + [VMEM] * 3, [out] * 4, [VMEM] * 4)


def merge_kernel(place, b0, b1, b2, b3, *outs):
    for j, block in enumerate((b0, b1, b2, b3)):
        for index, target in enumerate(outs):
            for h in range(4):
                target[:, head_columns(place, j, h)] = block[index, :, h * DH : (h + 1) * DH]


def merge_heads(place, blocks):
    _, tokens, part = blocks[0].shape
    out = jax.ShapeDtypeStruct((tokens, 4 * part), BF16)
    return call(merge_kernel, "merge_heads", (place, *blocks), [SMEM] + [VMEM] * 4, [out] * 3, [VMEM] * 3)


def dot(a, b, a_dim, b_dim):
    return lax.dot_general(a, b, (((a_dim,), (b_dim,)), ((), ())), preferred_element_type=F32)


def load_blocks(blocks, rows, sems, first):
    tokens = blocks[0].shape[1]
    return run_copies([(b, rows.at[:, pl.ds(p * tokens, tokens), :]) for p, b in enumerate(blocks)], sems, first)


def load_cots(blocks, rows, sems, first):
    tokens = blocks[0].shape[0]
    return run_copies([(b, rows.at[pl.ds(p * tokens, tokens), :]) for p, b in enumerate(blocks)], sems, first)


def load_slab(place, mine, other, slab, sems, first):
    pairs = []
    for h in range(4):
        for source, half in ((mine[h], place[1]), (other[h], 1 - place[1])):
            pairs.append((source, slab.at[pl.ds(pl.multiple_of(h * DH + half * HALF, HALF), HALF), :]))
    return run_copies(pairs, sems, first)


def bias_rows(place, mask):
    rows = []
    for r in range(4):
        key_block = jnp.bitwise_xor(place[0], r)
        row = []
        for p in range(4):
            kept = mask[jnp.bitwise_xor(place[0], p) * 4 + key_block] > 0
            row.append(jnp.full((1, DH), jnp.where(kept, 0.0, -1e30), F32))
        rows.append(jnp.concatenate(row, axis=1))
    return rows


def scores_kq(bias, query, key):
    raw = dot(key, query, 1, 1) * (LOG2E / math.sqrt(DH))
    return jnp.concatenate([raw[r * DH : (r + 1) * DH] + bias[r] for r in range(4)], axis=0)


def forward_kernel(place, mask, b0, b1, b2, b3, attended, attended_t, log_total, qkv, sems):
    copies = load_blocks((b0, b1, b2, b3), qkv, sems, 0)
    bias = bias_rows(place, mask)
    for copy in copies:
        copy.wait()
    for h in range(4):
        here = slice(h * DH, (h + 1) * DH)
        scores = scores_kq(bias, qkv[0, :, here], qkv[1, :, here])
        highest = jnp.max(scores, axis=0, keepdims=True)
        weights = jnp.exp2(scores - highest)
        total = jnp.sum(weights, axis=0, keepdims=True)
        rounded = (weights * (1.0 / total)).astype(BF16)
        out_t = dot(qkv[2, :, here], rounded, 0, 0).astype(BF16)
        attended_t[here, :] = out_t
        attended[:, here] = out_t.T
        log_total[h : h + 1, :] = highest + jnp.log2(total)


def forward(place, mask, blocks, after=()):
    _, tokens, part = blocks[0].shape
    length = 4 * tokens
    return call(
        forward_kernel,
        "forward",
        (place, mask, *blocks),
        [SMEM] * 2 + [HBM] * 4,
        [
            jax.ShapeDtypeStruct((length, part), BF16),
            jax.ShapeDtypeStruct((part, length), BF16),
            jax.ShapeDtypeStruct((4, length), F32),
        ],
        [VMEM] * 3,
        [pltpu.VMEM((3, length, part), BF16), pltpu.SemaphoreType.DMA((4,))],
        flops=4 * length * length * part,
        after=after,
    )


def mixed_kernel(place, m0, m1, m2, m3, r0, r1, r2, r3, attended, send_x, send_y, own, x_right, y_left, slab, sems):
    copies = load_slab(place, (m0, m1, m2, m3), (r0, r1, r2, r3), slab, sems, 0)
    for copy in copies:
        copy.wait()
    tokens = attended.shape[0] // 4
    step = slab.shape[1] // 4
    for piece in range(4):
        columns = slice(piece * step, (piece + 1) * step)
        here = slice((piece % 2) * step, (piece % 2 + 1) * step)
        total = dot(attended[...], slab[:, columns], 1, 0)
        parts = [total[p * tokens : (p + 1) * tokens] for p in range(4)]
        own[:, columns] = parts[0].astype(BF16)
        if piece < 2:
            send_x[0, :, here] = parts[1].astype(BF16)
            send_x[1, :, here] = parts[3].astype(BF16)
            y_left[:, here] = parts[2].astype(BF16)
        else:
            send_y[0, :, here] = parts[2].astype(BF16)
            send_y[1, :, here] = parts[3].astype(BF16)
            x_right[:, here] = parts[1].astype(BF16)


def mixed_parts(place, mine, other, attended, after=()):
    length, part = attended.shape
    width = mine[0].shape[1]
    tokens, half = length // 4, width // 2
    return call(
        mixed_kernel,
        "mixed_parts",
        (place, *mine, *other, attended),
        [SMEM] + [HBM] * 8 + [VMEM],
        [
            jax.ShapeDtypeStruct((2, tokens, half), BF16),
            jax.ShapeDtypeStruct((2, tokens, half), BF16),
            jax.ShapeDtypeStruct((tokens, width), BF16),
            jax.ShapeDtypeStruct((tokens, half), BF16),
            jax.ShapeDtypeStruct((tokens, half), BF16),
        ],
        [VMEM] * 5,
        [pltpu.VMEM((part, width), BF16), pltpu.SemaphoreType.DMA((8,))],
        flops=2 * length * width * part,
        after=after,
    )


def weight_kernel(place, attended_t, c0, c1, c2, c3, keep, send, cots, sems):
    copies = load_cots((c0, c1, c2, c3), cots, sems, 0)
    core = place[1]
    rows = []
    for half in (1 - core, core):
        for h in range(4):
            rows.append(attended_t[pl.ds(pl.multiple_of(h * DH + half * HALF, HALF), HALF), :])
    left = jnp.concatenate(rows, axis=0)
    for copy in copies:
        copy.wait()
    step = cots.shape[1] // 4
    for piece in range(4):
        columns = slice(piece * step, (piece + 1) * step)
        total = dot(left, cots[:, columns], 1, 0).astype(BF16)
        for h in range(4):
            send[h, :, columns] = total[h * HALF : (h + 1) * HALF]
            keep[h, :, columns] = total[(4 + h) * HALF : (5 + h) * HALF]


def weight_parts(place, attended_t, cot_blocks, after=()):
    part, length = attended_t.shape
    width = cot_blocks[0].shape[1]
    out = jax.ShapeDtypeStruct((4, HALF, width), BF16)
    return call(
        weight_kernel,
        "weight_parts",
        (place, attended_t, *cot_blocks),
        [SMEM, VMEM] + [HBM] * 4,
        [out] * 2,
        [VMEM] * 2,
        [pltpu.VMEM((length, width), BF16), pltpu.SemaphoreType.DMA((4,))],
        flops=2 * length * width * part,
        after=after,
    )


def add_kernel(keep, got, *outs):
    for h, out in enumerate(outs):
        out[...] = (keep[h].astype(F32) + got[h].astype(F32)).astype(BF16)


def add_cores(keep, got):
    out = jax.ShapeDtypeStruct(keep.shape[1:], BF16)
    return call(add_kernel, "add_cores", (keep, got), [VMEM] * 2, [out] * 4, [VMEM] * 4)


def weight_out_kernel(place, p0, p1, p2, p3, out):
    for k, piece in enumerate((p0, p1, p2, p3)):
        head = jnp.bitwise_xor(place[0] % 2, k % 2)
        half = jnp.bitwise_xor(jnp.bitwise_xor(place[1], place[0] // 2), k // 2)
        start = pl.multiple_of(head * DH + half * HALF, HALF)
        out[pl.ds(start, HALF), :] = piece[...].astype(F32) * 0.125


def weight_out(place, pieces):
    rows, width = pieces[0].shape
    out = jax.ShapeDtypeStruct((4 * rows, width), F32)
    return call(weight_out_kernel, "weight_out", (place, *pieces), [SMEM] + [VMEM] * 4, [out], [VMEM])[0]


def backward_kernel(
    place, mask, m0, m1, m2, m3, r0, r1, r2, r3, log_total, c0, c1, c2, c3, b0, b1, b2, b3,
    o0, o1, o2, o3, slab, cots, qkv, grads, sems,
):
    slab_copies = load_slab(place, (m0, m1, m2, m3), (r0, r1, r2, r3), slab, sems, 0)
    cot_copies = load_cots((c0, c1, c2, c3), cots, sems, 8)
    qkv_copies = load_blocks((b0, b1, b2, b3), qkv, sems, 12)
    outs = (o0, o1, o2, o3)
    tokens = c0.shape[0]
    for copy in slab_copies + cot_copies:
        copy.wait()
    for pair in range(2):
        rows = slice(pair * 2 * DH, (pair + 1) * 2 * DH)
        grads[:, rows] = dot(cots[...], slab[rows, :], 1, 1).astype(BF16)
    for copy in qkv_copies:
        copy.wait()
    scale = 1.0 / math.sqrt(DH)
    bias = bias_rows(place, mask)
    for h in range(4):
        here = slice(h * DH, (h + 1) * DH)
        query, key, value, grad = qkv[0, :, here], qkv[1, :, here], qkv[2, :, here], grads[:, here]
        probs = jnp.exp2(scores_kq(bias, query, key) - log_total[h : h + 1, :])
        grad_value = dot(probs.astype(BF16), grad, 1, 0).astype(BF16)
        grad_probs = dot(value, grad, 1, 1)
        delta = jnp.sum(probs * grad_probs, axis=0, keepdims=True)
        grad_scores = (probs * (grad_probs - delta) * scale).astype(BF16)
        grad_key = dot(grad_scores, query, 1, 0).astype(BF16)
        grad_query = dot(key, grad_scores, 0, 0).astype(BF16).T
        for index, full in enumerate((grad_query, grad_key, grad_value)):
            for p in range(4):
                outs[p][index, :, here] = full[p * tokens : (p + 1) * tokens]


def backward(place, mask, mine, other, log_total, cot_blocks, blocks, after=()):
    _, tokens, part = blocks[0].shape
    width = mine[0].shape[1]
    length = 4 * tokens
    return call(
        backward_kernel,
        "backward",
        (place, mask, *mine, *other, log_total, *cot_blocks, *blocks),
        [SMEM] * 2 + [HBM] * 8 + [VMEM] + [HBM] * 8,
        [jax.ShapeDtypeStruct((3, tokens, part), BF16)] * 4,
        [VMEM] * 4,
        [
            pltpu.VMEM((part, width), BF16),
            pltpu.VMEM((length, width), BF16),
            pltpu.VMEM((3, length, part), BF16),
            pltpu.VMEM((length, part), BF16),
            pltpu.SemaphoreType.DMA((16,)),
        ],
        flops=2 * length * width * part + 10 * length * length * part,
        after=after,
    )


def column_shards(queries, keys, values, out_weight, cotangent, block_mask):
    tokens, width = queries.shape[1:]
    column = lax.axis_index("seq")
    rank = lax.axis_index("dp")
    core, z = rank % 2, rank // 2
    place = jnp.stack([column, core, z]).astype(jnp.int32)
    mask = block_mask.reshape(-1)
    cot = cotangent[0]

    def plane(array, flip):
        return lax.ppermute(array, "seq", [(i, i ^ flip) for i in range(4)])

    def swap(array):
        return lax.ppermute(array, "dp", [(i, i ^ 1) for i in range(8)])

    def along(array, flip):
        return lax.ppermute(array, "dp", [(i, i ^ (2 * flip)) for i in range(8)])

    own, to_x, to_y, to_d = split_heads(place, queries[0], keys[0], values[0])
    blocks = (own, plane(to_x, 1), plane(to_y, 2), plane(to_d, 3))

    cot_x, cot_y = plane(cot, 1), plane(cot, 2)
    half = tokens // 2
    cot_d = jnp.concatenate([plane(cot_y[:half], 1), plane(cot_x[half:], 2)], axis=0)
    cot_blocks = (cot, cot_x, cot_y, cot_d)

    start = (column % 2) * DH
    owner = column // 2 == core
    given = swap(lax.dynamic_slice_in_dim(out_weight, start + HALF * (1 - core), HALF, 0))
    chunk = jnp.where(owner, lax.dynamic_slice_in_dim(out_weight, start + HALF * core, HALF, 0), given)
    mine = (chunk, along(chunk, 1), along(chunk, 2), along(chunk, 3))
    other = tuple(swap(m) for m in mine)

    attended, attended_t, log_total = forward(place, mask, blocks)

    send_x, send_y, mixed_own, x_right, y_left = mixed_parts(place, mine, other, attended)
    got_x, got_y = plane(send_x, 1), plane(send_y, 2)
    got_left = plane((y_left.astype(F32) + got_x[1].astype(F32)).astype(BF16), 2)
    got_right = plane((x_right.astype(F32) + got_y[1].astype(F32)).astype(BF16), 1)
    mixed = jnp.concatenate(
        [
            mixed_own[:, : width // 2].astype(F32) + got_x[0].astype(F32) + got_left.astype(F32),
            mixed_own[:, width // 2 :].astype(F32) + got_y[0].astype(F32) + got_right.astype(F32),
        ],
        axis=1,
    ).astype(BF16)

    keep, send = weight_parts(place, attended_t, cot_blocks, after=(send_x,))
    s0, s1, s2, s3 = add_cores(keep, swap(send))
    got = [along(s, flip).astype(F32) for flip, s in ((1, s1), (2, s2), (3, s3))]
    summed = (s0.astype(F32) + got[0] + got[1] + got[2]).astype(BF16)
    pieces = []
    for k in range(4):
        pairs = []
        for plane_at in range(4):
            for c in range(2):
                for t in range(4):
                    to_core, to_column = t // 2, t ^ (2 * c) ^ k
                    pairs.append(((2 * plane_at + c) * 4 + t, (2 * plane_at + to_core) * 4 + to_column))
        pieces.append(lax.ppermute(summed, ("dp", "seq"), pairs))
    grad_weight = weight_out(place, pieces)

    outs = backward(place, mask, mine, other, log_total, cot_blocks, blocks, after=(keep,))
    grads = merge_heads(place, (outs[0], plane(outs[1], 1), plane(outs[2], 2), plane(outs[3], 3)))
    return (mixed[None],) + tuple(g[None] for g in grads) + (grad_weight,)


def attend(query_heads, key_heads, value_heads, grad_heads, block_mask):
    batch, length, width = query_heads.shape
    heads = width // DH
    shape_split = (batch, length, heads, DH)
    query_split = query_heads.reshape(shape_split)
    key_split = key_heads.reshape(shape_split)
    value_split = value_heads.reshape(shape_split)
    grad_split = grad_heads.reshape(shape_split)
    block = length // block_mask.shape[2]
    rows_step = min(512, length)
    scale = 1.0 / math.sqrt(DH)

    def step(carry, index):
        key_total, value_total = carry
        start = index * rows_step
        query_part = lax.dynamic_slice_in_dim(query_split, start, rows_step, 1)
        grad_part = lax.dynamic_slice_in_dim(grad_split, start, rows_step, 1)
        mask_part = lax.dynamic_slice_in_dim(block_mask, start // block, rows_step // block, 1)
        allowed = jnp.repeat(jnp.repeat(mask_part, block, axis=1), block, axis=2) > 0
        scores = (
            jnp.einsum("bqhd,bkhd->bhqk", query_part, key_split, preferred_element_type=jnp.float32)
            * scale
        )
        scores = jnp.where(allowed[:, None], scores, -1e30)
        highest = jnp.max(scores, axis=3, keepdims=True)
        log_total = highest + jnp.log(jnp.sum(jnp.exp(scores - highest), axis=3, keepdims=True))
        probs = jnp.exp(scores - log_total)
        rounded = probs.astype(jnp.bfloat16)
        attended = jnp.einsum(
            "bhqk,bkhd->bqhd", rounded, value_split, preferred_element_type=jnp.float32
        ).astype(jnp.bfloat16)
        value_total = value_total + jnp.einsum(
            "bhqk,bqhd->bkhd", rounded, grad_part, preferred_element_type=jnp.float32
        )
        grad_probs = jnp.einsum(
            "bqhd,bkhd->bhqk", grad_part, value_split, preferred_element_type=jnp.float32
        )
        delta = jnp.sum(probs * grad_probs, axis=3, keepdims=True)
        grad_scores = (probs * (grad_probs - delta) * scale).astype(jnp.bfloat16)
        grad_query = jnp.einsum(
            "bhqk,bkhd->bqhd", grad_scores, key_split, preferred_element_type=jnp.float32
        ).astype(jnp.bfloat16)
        key_total = key_total + jnp.einsum(
            "bhqk,bqhd->bkhd", grad_scores, query_part, preferred_element_type=jnp.float32
        )
        return ((key_total, value_total), (attended, grad_query))

    zeros = jnp.zeros(shape_split, jnp.float32)
    totals, pieces = lax.scan(
        step, (zeros, zeros), jnp.arange(length // rows_step, dtype=jnp.int32)
    )

    def joined(parts):
        return jnp.moveaxis(parts, 0, 1).reshape(batch, length, width)

    grad_key = totals[0].astype(jnp.bfloat16).reshape(batch, length, width)
    grad_value = totals[1].astype(jnp.bfloat16).reshape(batch, length, width)
    return (joined(pieces[0]), joined(pieces[1]), grad_key, grad_value)


def general_shards(queries, keys, values, out_weight, cotangent, block_mask):
    batch, tokens, width = queries.shape
    query_heads, key_heads, value_heads = (
        lax.all_to_all(queries, "seq", split_axis=2, concat_axis=1, tiled=True),
        lax.all_to_all(keys, "seq", split_axis=2, concat_axis=1, tiled=True),
        lax.all_to_all(values, "seq", split_axis=2, concat_axis=1, tiled=True),
    )
    weight_full = lax.all_gather(out_weight, "dp", axis=0, tiled=True)
    flat_cot = cotangent.reshape(batch * tokens, width)
    grad_attn = lax.dot_general(
        flat_cot, weight_full, (((1,), (1,)), ((), ())), preferred_element_type=jnp.float32
    )
    grad_attn = grad_attn.astype(jnp.bfloat16).reshape(batch, tokens, width)
    grad_heads = lax.all_to_all(grad_attn, "seq", split_axis=2, concat_axis=1, tiled=True)
    attended_heads, grad_q_heads, grad_k_heads, grad_v_heads = attend(
        query_heads, key_heads, value_heads, grad_heads, block_mask
    )
    attended, grad_queries, grad_keys, grad_values = (
        lax.all_to_all(attended_heads, "seq", split_axis=1, concat_axis=2, tiled=True),
        lax.all_to_all(grad_q_heads, "seq", split_axis=1, concat_axis=2, tiled=True),
        lax.all_to_all(grad_k_heads, "seq", split_axis=1, concat_axis=2, tiled=True),
        lax.all_to_all(grad_v_heads, "seq", split_axis=1, concat_axis=2, tiled=True),
    )
    flat_att = attended.reshape(batch * tokens, width)
    mixed = (
        jnp.dot(flat_att, weight_full, preferred_element_type=jnp.float32)
        .astype(jnp.bfloat16)
        .reshape(batch, tokens, width)
    )
    partial_grad = lax.psum_scatter(
        lax.dot_general(
            flat_att, flat_cot, (((0,), (0,)), ((), ())), preferred_element_type=jnp.float32
        ),
        "dp",
        scatter_dimension=0,
        tiled=True,
    )
    summed = lax.psum(partial_grad, "seq")
    grad_weight = summed / (batch * lax.axis_size("dp"))
    return (mixed, grad_queries, grad_keys, grad_values, grad_weight)


def fits_columns(mesh, queries, out_weight, block_mask):
    batch, length, width = queries
    return (
        mesh.shape["dp"] == 8
        and mesh.shape["seq"] == 4
        and batch == 8
        and length == 4 * DH
        and width == 16 * DH
        and out_weight == (width, width)
        and block_mask == (batch, 4, 4)
    )


def solution(mesh):
    placed = (
        P("dp", "seq", None),
        P("dp", "seq", None),
        P("dp", "seq", None),
        P("dp", None),
        P("dp", "seq", None),
        P("dp", None, None),
    )

    def program(queries, keys, values, out_weight, cotangent, block_mask):
        fits = fits_columns(mesh, queries.shape, out_weight.shape, block_mask.shape)
        return jax.shard_map(
            column_shards if fits else general_shards,
            mesh=mesh,
            in_specs=placed,
            out_specs=(
                P("dp", "seq", None),
                P("dp", "seq", None),
                P("dp", "seq", None),
                P("dp", "seq", None),
                P("dp", None),
            ),
            check_vma=False,
        )(queries, keys, values, out_weight, cotangent, block_mask)

    return program
```

profile of v0, /device:TPU:0, one launch (start us, length us, event | category | flops | bytes accessed | tf_op | source)
XLA Modules:
  0.0 148.6 jit_solution(10259491778418901214)
XLA Ops:
  2.2 2.6 %collective-permute-start.16 = (bf16[128,2048]{1,0:T(8,128)(2,1)}, bf16[128,2048]{1,0:T(8,128)(2,1)S(1)}, u32[]{:S(2)}, u32[]{:S(2)}) collective-permute-start(bf16[128,2048]{1,0:T(8,128)(2,1)} %bitcast.37), channel_id=1, source_target_pairs={{0,2},{1,3},{2,0},{3,1},{4,6},{5,7},{6,4},{7,5},{8,10},{9,11},{10,... | collective-permute-start | bytes 1572872 | tf_op jit(solution)/shard_map/ppermute | solution.py:328
  6.9 2.9 %split_heads.1 = (bf16[3,128,512]{2,1,0:T(8,128)(2,1)}, bf16[3,128,512]{2,1,0:T(8,128)(2,1)}, bf16[3,128,512]{2,1,0:T(8,128)(2,1)}, bf16[3,128,512]{2,1,0:T(8,128)(2,1)}) custom-call(s32[3]{0:T(128)} %pad_add_fusion.refs_0_, bf16[128,2048]{1,0:T(8,128)(2,1)} %bitcast.34, bf16[128,2048]{1,0:T(8,128)(2,1)} %bitcast.35, bf16[128,2048]{1,0:T(8,128)(2,1)} %bitcast.36), custom_call_target="tpu_custom_call" | custom-call | bytes 3145740 | tf_op jit(solution)/shard_map/split_heads/pallas_call | solution.py:30
  10.4 2.9 %collective-permute-start.10 = (bf16[3,128,512]{2,1,0:T(8,128)(2,1)}, bf16[3,128,512]{2,1,0:T(8,128)(2,1)S(1)}, u32[]{:S(2)}, u32[]{:S(2)}) collective-permute-start(bf16[3,128,512]{2,1,0:T(8,128)(2,1)} %get-tuple-element.33), channel_id=1, source_target_pairs={{0,3},{1,2},{2,1},{3,0},{4,7},{5,6},{6,5},{7,4},{8,11},{9,10},{10,... | collective-permute-start | bytes 1179656 | tf_op jit(solution)/shard_map/ppermute | solution.py:328
  14.3 3.4 %collective-permute-done.16.refs_4_.refs_13_ = bf16[128,2048]{1,0:T(8,128)(2,1)S(1)} collective-permute-done((bf16[128,2048]{1,0:T(8,128)(2,1)}, bf16[128,2048]{1,0:T(8,128)(2,1)S(1)}, u32[]{:S(2)}, u32[]{:S(2)}) %collective-permute-start.16) | collective-permute-done | bytes 524320 | tf_op jit(solution)/shard_map/ppermute | solution.py:328
  17.8 4.0 %collective-permute-start.3 = (bf16[64,2048]{1,0:T(8,128)(2,1)S(1)}, bf16[64,2048]{1,0:T(8,128)(2,1)S(1)}, u32[]{:S(2)}, u32[]{:S(2)}) collective-permute-start(bf16[64,2048]{1,0:T(8,128)(2,1)S(1)} %dynamic-slice_select_fusion.refs_1_.refs_2_), channel_id=1, source_target_pairs={{0,24},{4,28},{8,16},{12,20},{16,8},{20,12},{24,0},{28,4},{1,25},{... | collective-permute-start | bytes 786440 | tf_op jit(solution)/shard_map/ppermute | solution.py:334
  21.8 6.4 %collective-permute-done.8.refs_3_.refs_16_ = bf16[3,128,512]{2,1,0:T(8,128)(2,1)S(1)} collective-permute-done((bf16[3,128,512]{2,1,0:T(8,128)(2,1)}, bf16[3,128,512]{2,1,0:T(8,128)(2,1)S(1)}, u32[]{:S(2)}, u32[]{:S(2)}) %collective-permute-start.8) | collective-permute-done | bytes 393248 | tf_op jit(solution)/shard_map/ppermute | solution.py:328
  28.2 2.6 %collective-permute-start.2 = (bf16[64,2048]{1,0:T(8,128)(2,1)S(1)}, bf16[64,2048]{1,0:T(8,128)(2,1)S(1)}, u32[]{:S(2)}, u32[]{:S(2)}) collective-permute-start(bf16[64,2048]{1,0:T(8,128)(2,1)S(1)} %dynamic-slice_select_fusion.refs_1_.refs_2_), channel_id=1, source_target_pairs={{0,16},{4,20},{8,24},{12,28},{16,0},{20,4},{24,8},{28,12},{1,17},{... | collective-permute-start | bytes 786440 | tf_op jit(solution)/shard_map/ppermute | solution.py:334
  36.1 2.0 %collective-permute-start.18 = (bf16[64,2048]{1,0:T(8,128)(2,1)S(1)}, bf16[64,2048]{1,0:T(8,128)(2,1)S(1)}, u32[]{:S(2)}, u32[]{:S(2)}) collective-permute-start(bf16[64,2048]{1,0:T(8,128)(2,1)S(1)} %slice.37), channel_id=1, source_target_pairs={{0,2},{1,3},{2,0},{3,1},{4,6},{5,7},{6,4},{7,5},{8,10},{9,11},{10,... | collective-permute-start | bytes 786440 | tf_op jit(solution)/shard_map/ppermute | solution.py:328
  38.1 5.3 %forward.1 = (bf16[512,512]{1,0:T(8,128)(2,1)}, bf16[512,512]{1,0:T(8,128)(2,1)}, f32[4,512]{1,0:T(4,128)}) custom-call(s32[3]{0:T(128)} %pad_add_fusion.refs_0_, s32[16]{0:T(128)} %reshape.52.refs_1_, bf16[3,128,512]{2,1,0:T(8,128)(2,1)} %get-tuple-element.30.refs_2_.refs_15_, bf16[3,128,512]{2,1,0:T(8,128)(2,1)} %copy-done.18, ...), custom_call_target="tpu_custom_call" | custom-call | flops 536870912 | bytes 2629708 | tf_op jit(solution)/shard_map/forward/pallas_call | solution.py:30
  47.1 5.0 %mixed_parts.1 = (bf16[2,128,1024]{2,1,0:T(8,128)(2,1)}, bf16[2,128,1024]{2,1,0:T(8,128)(2,1)}, bf16[128,2048]{1,0:T(8,128)(2,1)}, bf16[128,1024]{1,0:T(8,128)(2,1)}, bf16[128,1024]{1,0:T(8,128)(2,1)}) custom-call(s32[3]{0:T(128)} %pad_add_fusion.refs_0_, bf16[64,2048]{1,0:T(8,128)(2,1)} %copy-done.7, ...), custom_call_target="tpu_custom_call" | custom-call | flops 1073741824 | bytes 4718604 | tf_op jit(solution)/shard_map/mixed_parts/pallas_call | solution.py:30
  52.1 5.1 %weight_parts.1 = (bf16[4,64,2048]{2,1,0:T(8,128)(2,1)}, bf16[4,64,2048]{2,1,0:T(8,128)(2,1)}) custom-call(s32[3]{0:T(128)} %pad_add_fusion.refs_0_, bf16[512,512]{1,0:T(8,128)(2,1)} %get-tuple-element.41.refs_1_, bf16[128,2048]{1,0:T(8,128)(2,1)} %bitcast.39, bf16[128,2048]{1,0:T(8,128)(2,1)} %copy-done.13, bf16[128,2048]{1,0:T(8,128)(2,1)} %copy-done.12, ...), custom_call_target="tpu_custom_call" | custom-call | flops 1073741824 | bytes 4718604 | tf_op jit(solution)/shard_map/weight_parts/pallas_call | solution.py:30
  57.4 8.7 %backward.1 = (bf16[3,128,512]{2,1,0:T(8,128)(2,1)}, bf16[3,128,512]{2,1,0:T(8,128)(2,1)}, bf16[3,128,512]{2,1,0:T(8,128)(2,1)}, bf16[3,128,512]{2,1,0:T(8,128)(2,1)}) custom-call(s32[3]{0:T(128)} %pad_add_fusion.refs_0_, s32[16]{0:T(128)} %reshape.52.refs_1_, bf16[64,2048]{1,0:T(8,128)(2,1)} %copy-done.7, ...), custom_call_target="tpu_custom_call" | custom-call | flops 2415919104 | bytes 7348300 | tf_op jit(solution)/shard_map/backward/pallas_call | solution.py:30
  70.8 7.5 %collective-permute-done.19.refs_2_ = bf16[3,128,512]{2,1,0:T(8,128)(2,1)S(1)} collective-permute-done((bf16[3,128,512]{2,1,0:T(8,128)(2,1)}, bf16[3,128,512]{2,1,0:T(8,128)(2,1)S(1)}, u32[]{:S(2)}, u32[]{:S(2)}) %collective-permute-start.19) | collective-permute-done | bytes 393248 | tf_op jit(solution)/shard_map/ppermute | solution.py:328
  79.8 18.6 %collective-permute-done.20.refs_3_ = bf16[3,128,512]{2,1,0:T(8,128)(2,1)S(1)} collective-permute-done((bf16[3,128,512]{2,1,0:T(8,128)(2,1)}, bf16[3,128,512]{2,1,0:T(8,128)(2,1)S(1)}, u32[]{:S(2)}, u32[]{:S(2)}) %collective-permute-start.20) | collective-permute-done | bytes 393248 | tf_op jit(solution)/shard_map/ppermute | solution.py:328
  99.3 3.0 %merge_heads.1 = (bf16[128,2048]{1,0:T(8,128)(2,1)}, bf16[128,2048]{1,0:T(8,128)(2,1)}, bf16[128,2048]{1,0:T(8,128)(2,1)}) custom-call(s32[3]{0:T(128)} %pad_add_fusion.refs_0_, bf16[3,128,512]{2,1,0:T(8,128)(2,1)} %get-tuple-element.43.refs_1_, bf16[3,128,512]{2,1,0:T(8,128)(2,1)} %copy-done.2, bf16[3,128,512]{2,1,0:T(8,128)(2,1)} %copy-done.3, ...), custom_call_target="tpu_custom_call" | custom-call | bytes 3145740 | tf_op jit(solution)/shard_map/merge_heads/pallas_call | solution.py:30
  103.3 2.6 %add_cores.1 = (bf16[64,2048]{1,0:T(8,128)(2,1)}, bf16[64,2048]{1,0:T(8,128)(2,1)}, bf16[64,2048]{1,0:T(8,128)(2,1)}, bf16[64,2048]{1,0:T(8,128)(2,1)}) custom-call(bf16[4,64,2048]{2,1,0:T(8,128)(2,1)} %get-tuple-element.42.refs_19_.refs_0_, bf16[4,64,2048]{2,1,0:T(8,128)(2,1)} %copy-done), custom_call_target="tpu_custom_call" | custom-call | bytes 3145728 | tf_op jit(solution)/shard_map/add_cores/pallas_call | solution.py:30
  107.5 2.6 %collective-permute-start.24 = (bf16[64,2048]{1,0:T(8,128)(2,1)}, bf16[64,2048]{1,0:T(8,128)(2,1)S(1)}, u32[]{:S(2)}, u32[]{:S(2)}) collective-permute-start(bf16[64,2048]{1,0:T(8,128)(2,1)} %get-tuple-element.53), channel_id=1, source_target_pairs={{0,16},{4,20},{8,24},{12,28},{16,0},{20,4},{24,8},{28,12},{1,17},{... | collective-permute-start | bytes 786440 | tf_op jit(solution)/shard_map/ppermute | solution.py:334
  112.2 5.9 %collective-permute-done.23 = bf16[64,2048]{1,0:T(8,128)(2,1)S(1)} collective-permute-done((bf16[64,2048]{1,0:T(8,128)(2,1)}, bf16[64,2048]{1,0:T(8,128)(2,1)S(1)}, u32[]{:S(2)}, u32[]{:S(2)}) %collective-permute-start.23) | collective-permute-done | bytes 262176 | tf_op jit(solution)/shard_map/ppermute | solution.py:334
  118.1 11.0 %collective-permute-done.24 = bf16[64,2048]{1,0:T(8,128)(2,1)S(1)} collective-permute-done((bf16[64,2048]{1,0:T(8,128)(2,1)}, bf16[64,2048]{1,0:T(8,128)(2,1)S(1)}, u32[]{:S(2)}, u32[]{:S(2)}) %collective-permute-start.24) | collective-permute-done | bytes 262176 | tf_op jit(solution)/shard_map/ppermute | solution.py:334
  131.0 1.9 %collective-permute-start.28 = (bf16[64,2048]{1,0:T(8,128)(2,1)S(1)}, bf16[64,2048]{1,0:T(8,128)(2,1)S(1)}, u32[]{:S(2)}, u32[]{:S(2)}) collective-permute-start(bf16[64,2048]{1,0:T(8,128)(2,1)S(1)} %add_convert_fusion), channel_id=1, source_target_pairs={{0,2},{1,3},{2,4},{3,5},{4,0},{5,1},{6,6},{7,7},{8,10},{9,11},{10,... | collective-permute-start | bytes 786440 | tf_op jit(solution)/shard_map/ppermute | solution.py:377
  136.2 1.9 %collective-permute-done.29.refs_4_ = bf16[64,2048]{1,0:T(8,128)(2,1)S(1)} collective-permute-done((bf16[64,2048]{1,0:T(8,128)(2,1)S(1)}, bf16[64,2048]{1,0:T(8,128)(2,1)S(1)}, u32[]{:S(2)}, u32[]{:S(2)}) %collective-permute-start.29) | collective-permute-done | bytes 262176 | tf_op jit(solution)/shard_map/ppermute | solution.py:377
  138.1 4.6 %collective-permute-done.28.refs_3_ = bf16[64,2048]{1,0:T(8,128)(2,1)S(1)} collective-permute-done((bf16[64,2048]{1,0:T(8,128)(2,1)S(1)}, bf16[64,2048]{1,0:T(8,128)(2,1)S(1)}, u32[]{:S(2)}, u32[]{:S(2)}) %collective-permute-start.28) | collective-permute-done | bytes 262176 | tf_op jit(solution)/shard_map/ppermute | solution.py:377
  142.7 1.8 %collective-permute-done.27.refs_2_ = bf16[64,2048]{1,0:T(8,128)(2,1)S(1)} collective-permute-done((bf16[64,2048]{1,0:T(8,128)(2,1)S(1)}, bf16[64,2048]{1,0:T(8,128)(2,1)S(1)}, u32[]{:S(2)}, u32[]{:S(2)}) %collective-permute-start.27) | collective-permute-done | bytes 262176 | tf_op jit(solution)/shard_map/ppermute | solution.py:377
  145.9 2.7 %weight_out.1 = f32[256,2048]{1,0:T(8,128)} custom-call(s32[3]{0:T(128)} %pad_add_fusion.refs_0_, bf16[64,2048]{1,0:T(8,128)(2,1)} %copy-done.11, bf16[64,2048]{1,0:T(8,128)(2,1)} %copy-done.10, bf16[64,2048]{1,0:T(8,128)(2,1)} %copy-done.9, bf16[64,2048]{1,0:T(8,128)(2,1)} %copy-done.8), custom_call_target="tpu_custom_call" | custom-call | bytes 3145740 | tf_op jit(solution)/shard_map/weight_out/pallas_call | solution.py:30
  (111 shorter events, 32.8 us)
Async XLA Ops:
  1.6 8.8 %collective-permute-start = (bf16[64,2048]{1,0:T(8,128)(2,1)S(1)}, bf16[64,2048]{1,0:T(8,128)(2,1)S(1)}, u32[]{:S(2)}, u32[]{:S(2)}) collective-permute-start(bf16[64,2048]{1,0:T(8,128)(2,1)S(1)} %constant_dynamic-slice_fusion), channel_id=1, source_target_pairs={{0,4},{4,0},{8,12},{12,8},{16,20},{20,16},{24,28},{28,24},{1,5},{5... | collective-permute-start | bytes 786440 | tf_op jit(solution)/shard_map/ppermute | solution.py:331
  2.2 15.6 %collective-permute-start.16 = (bf16[128,2048]{1,0:T(8,128)(2,1)}, bf16[128,2048]{1,0:T(8,128)(2,1)S(1)}, u32[]{:S(2)}, u32[]{:S(2)}) collective-permute-start(bf16[128,2048]{1,0:T(8,128)(2,1)} %bitcast.37), channel_id=1, source_target_pairs={{0,2},{1,3},{2,0},{3,1},{4,6},{5,7},{6,4},{7,5},{8,10},{9,11},{10,... | collective-permute-start | bytes 1572872 | tf_op jit(solution)/shard_map/ppermute | solution.py:328
  4.8 27.6 %collective-permute-start.15 = (bf16[128,2048]{1,0:T(8,128)(2,1)}, bf16[128,2048]{1,0:T(8,128)(2,1)S(1)}, u32[]{:S(2)}, u32[]{:S(2)}) collective-permute-start(bf16[128,2048]{1,0:T(8,128)(2,1)} %bitcast.38), channel_id=1, source_target_pairs={{0,1},{1,0},{2,3},{3,2},{4,5},{5,4},{6,7},{7,6},{8,9},{9,8},{10,11... | collective-permute-start | bytes 1572872 | tf_op jit(solution)/shard_map/ppermute | solution.py:328
  9.8 18.3 %collective-permute-start.8 = (bf16[3,128,512]{2,1,0:T(8,128)(2,1)}, bf16[3,128,512]{2,1,0:T(8,128)(2,1)S(1)}, u32[]{:S(2)}, u32[]{:S(2)}) collective-permute-start(bf16[3,128,512]{2,1,0:T(8,128)(2,1)} %get-tuple-element.31), channel_id=1, source_target_pairs={{0,1},{1,0},{2,3},{3,2},{4,5},{5,4},{6,7},{7,6},{8,9},{9,8},{10,11... | collective-permute-start | bytes 1179656 | tf_op jit(solution)/shard_map/ppermute | solution.py:328
  10.4 20.4 %collective-permute-start.9 = (bf16[3,128,512]{2,1,0:T(8,128)(2,1)}, bf16[3,128,512]{2,1,0:T(8,128)(2,1)S(1)}, u32[]{:S(2)}, u32[]{:S(2)}) collective-permute-start(bf16[3,128,512]{2,1,0:T(8,128)(2,1)} %get-tuple-element.32), channel_id=1, source_target_pairs={{0,2},{1,3},{2,0},{3,1},{4,6},{5,7},{6,4},{7,5},{8,10},{9,11},{10,... | collective-permute-start | bytes 1179656 | tf_op jit(solution)/shard_map/ppermute | solution.py:328
  10.4 25.6 %collective-permute-start.10 = (bf16[3,128,512]{2,1,0:T(8,128)(2,1)}, bf16[3,128,512]{2,1,0:T(8,128)(2,1)S(1)}, u32[]{:S(2)}, u32[]{:S(2)}) collective-permute-start(bf16[3,128,512]{2,1,0:T(8,128)(2,1)} %get-tuple-element.33), channel_id=1, source_target_pairs={{0,3},{1,2},{2,1},{3,0},{4,7},{5,6},{6,5},{7,4},{8,11},{9,10},{10,... | collective-permute-start | bytes 1179656 | tf_op jit(solution)/shard_map/ppermute | solution.py:328
  17.8 25.7 %collective-permute-start.3 = (bf16[64,2048]{1,0:T(8,128)(2,1)S(1)}, bf16[64,2048]{1,0:T(8,128)(2,1)S(1)}, u32[]{:S(2)}, u32[]{:S(2)}) collective-permute-start(bf16[64,2048]{1,0:T(8,128)(2,1)S(1)} %dynamic-slice_select_fusion.refs_1_.refs_2_), channel_id=1, source_target_pairs={{0,24},{4,28},{8,16},{12,20},{16,8},{20,12},{24,0},{28,4},{1,25},{... | collective-permute-start | bytes 786440 | tf_op jit(solution)/shard_map/ppermute | solution.py:334
  28.2 15.4 %collective-permute-start.2 = (bf16[64,2048]{1,0:T(8,128)(2,1)S(1)}, bf16[64,2048]{1,0:T(8,128)(2,1)S(1)}, u32[]{:S(2)}, u32[]{:S(2)}) collective-permute-start(bf16[64,2048]{1,0:T(8,128)(2,1)S(1)} %dynamic-slice_select_fusion.refs_1_.refs_2_), channel_id=1, source_target_pairs={{0,16},{4,20},{8,24},{12,28},{16,0},{20,4},{24,8},{28,12},{1,17},{... | collective-permute-start | bytes 786440 | tf_op jit(solution)/shard_map/ppermute | solution.py:334
  30.8 13.3 %collective-permute-start.1 = (bf16[64,2048]{1,0:T(8,128)(2,1)S(1)}, bf16[64,2048]{1,0:T(8,128)(2,1)}, u32[]{:S(2)}, u32[]{:S(2)}) collective-permute-start(bf16[64,2048]{1,0:T(8,128)(2,1)S(1)} %dynamic-slice_select_fusion.refs_1_.refs_2_), channel_id=1, source_target_pairs={{0,8},{4,12},{8,0},{12,4},{16,24},{20,28},{24,16},{28,20},{1,9},{5... | collective-permute-start | bytes 786440 | tf_op jit(solution)/shard_map/ppermute | solution.py:334
  32.3 11.8 %collective-permute-start.17 = (bf16[64,2048]{1,0:T(8,128)(2,1)S(1)}, bf16[64,2048]{1,0:T(8,128)(2,1)S(1)}, u32[]{:S(2)}, u32[]{:S(2)}) collective-permute-start(bf16[64,2048]{1,0:T(8,128)(2,1)S(1)} %slice.36), channel_id=1, source_target_pairs={{0,1},{1,0},{2,3},{3,2},{4,5},{5,4},{6,7},{7,6},{8,9},{9,8},{10,11... | collective-permute-start | bytes 786440 | tf_op jit(solution)/shard_map/ppermute | solution.py:328
  57.2 45.1 %collective-permute-start.22 = (bf16[4,64,2048]{2,1,0:T(8,128)(2,1)}, bf16[4,64,2048]{2,1,0:T(8,128)(2,1)S(1)}, u32[]{:S(2)}, u32[]{:S(2)}) collective-permute-start(bf16[4,64,2048]{2,1,0:T(8,128)(2,1)} %get-tuple-element.50), channel_id=1, source_target_pairs={{0,4},{4,0},{8,12},{12,8},{16,20},{20,16},{24,28},{28,24},{1,5},{5... | collective-permute-start | bytes 3145736 | tf_op jit(solution)/shard_map/ppermute | solution.py:331
  66.1 12.2 %collective-permute-start.19 = (bf16[3,128,512]{2,1,0:T(8,128)(2,1)}, bf16[3,128,512]{2,1,0:T(8,128)(2,1)S(1)}, u32[]{:S(2)}, u32[]{:S(2)}) collective-permute-start(bf16[3,128,512]{2,1,0:T(8,128)(2,1)} %get-tuple-element.44), channel_id=1, source_target_pairs={{0,1},{1,0},{2,3},{3,2},{4,5},{5,4},{6,7},{7,6},{8,9},{9,8},{10,11... | collective-permute-start | bytes 1179656 | tf_op jit(solution)/shard_map/ppermute | solution.py:328
  67.7 42.6 %collective-permute-start.13 = (bf16[2,128,1024]{2,1,0:T(8,128)(2,1)S(1)}, bf16[2,128,1024]{2,1,0:T(8,128)(2,1)S(1)}, u32[]{:S(2)}, u32[]{:S(2)}) collective-permute-start(bf16[2,128,1024]{2,1,0:T(8,128)(2,1)S(1)} %copy-done.17), channel_id=1, source_target_pairs={{0,2},{1,3},{2,0},{3,1},{4,6},{5,7},{6,4},{7,5},{8,10},{9,11},{10,... | collective-permute-start | bytes 1572872 | tf_op jit(solution)/shard_map/ppermute | solution.py:328
  68.8 29.6 %collective-permute-start.20 = (bf16[3,128,512]{2,1,0:T(8,128)(2,1)}, bf16[3,128,512]{2,1,0:T(8,128)(2,1)S(1)}, u32[]{:S(2)}, u32[]{:S(2)}) collective-permute-start(bf16[3,128,512]{2,1,0:T(8,128)(2,1)} %get-tuple-element.45), channel_id=1, source_target_pairs={{0,2},{1,3},{2,0},{3,1},{4,6},{5,7},{6,4},{7,5},{8,10},{9,11},{10,... | collective-permute-start | bytes 1179656 | tf_op jit(solution)/shard_map/ppermute | solution.py:328
  69.7 28.7 %collective-permute-start.21 = (bf16[3,128,512]{2,1,0:T(8,128)(2,1)}, bf16[3,128,512]{2,1,0:T(8,128)(2,1)S(1)}, u32[]{:S(2)}, u32[]{:S(2)}) collective-permute-start(bf16[3,128,512]{2,1,0:T(8,128)(2,1)} %get-tuple-element.46), channel_id=1, source_target_pairs={{0,3},{1,2},{2,1},{3,0},{4,7},{5,6},{6,5},{7,4},{8,11},{9,10},{10,... | collective-permute-start | bytes 1179656 | tf_op jit(solution)/shard_map/ppermute | solution.py:328
  78.3 32.6 %collective-permute-start.11 = (bf16[2,128,1024]{2,1,0:T(8,128)(2,1)S(1)}, bf16[2,128,1024]{2,1,0:T(8,128)(2,1)S(1)}, u32[]{:S(2)}, u32[]{:S(2)}) collective-permute-start(bf16[2,128,1024]{2,1,0:T(8,128)(2,1)S(1)} %copy-done.16), channel_id=1, source_target_pairs={{0,1},{1,0},{2,3},{3,2},{4,5},{5,4},{6,7},{7,6},{8,9},{9,8},{10,11... | collective-permute-start | bytes 1572872 | tf_op jit(solution)/shard_map/ppermute | solution.py:328
  105.9 12.2 %collective-permute-start.23 = (bf16[64,2048]{1,0:T(8,128)(2,1)}, bf16[64,2048]{1,0:T(8,128)(2,1)S(1)}, u32[]{:S(2)}, u32[]{:S(2)}) collective-permute-start(bf16[64,2048]{1,0:T(8,128)(2,1)} %get-tuple-element.52), channel_id=1, source_target_pairs={{0,8},{4,12},{8,0},{12,4},{16,24},{20,28},{24,16},{28,20},{1,9},{5... | collective-permute-start | bytes 786440 | tf_op jit(solution)/shard_map/ppermute | solution.py:334
  107.5 21.6 %collective-permute-start.24 = (bf16[64,2048]{1,0:T(8,128)(2,1)}, bf16[64,2048]{1,0:T(8,128)(2,1)S(1)}, u32[]{:S(2)}, u32[]{:S(2)}) collective-permute-start(bf16[64,2048]{1,0:T(8,128)(2,1)} %get-tuple-element.53), channel_id=1, source_target_pairs={{0,16},{4,20},{8,24},{12,28},{16,0},{20,4},{24,8},{28,12},{1,17},{... | collective-permute-start | bytes 786440 | tf_op jit(solution)/shard_map/ppermute | solution.py:334
  110.1 19.0 %collective-permute-start.25 = (bf16[64,2048]{1,0:T(8,128)(2,1)}, bf16[64,2048]{1,0:T(8,128)(2,1)S(1)}, u32[]{:S(2)}, u32[]{:S(2)}) collective-permute-start(bf16[64,2048]{1,0:T(8,128)(2,1)} %get-tuple-element.54), channel_id=1, source_target_pairs={{0,24},{4,28},{8,16},{12,20},{16,8},{20,12},{24,0},{28,4},{1,25},{... | collective-permute-start | bytes 786440 | tf_op jit(solution)/shard_map/ppermute | solution.py:334
  110.4 24.1 %collective-permute-start.14 = (bf16[128,1024]{1,0:T(8,128)(2,1)S(1)}, bf16[128,1024]{1,0:T(8,128)(2,1)S(1)}, u32[]{:S(2)}, u32[]{:S(2)}) collective-permute-start(bf16[128,1024]{1,0:T(8,128)(2,1)S(1)} %fusion), channel_id=1, source_target_pairs={{0,1},{1,0},{2,3},{3,2},{4,5},{5,4},{6,7},{7,6},{8,9},{9,8},{10,11... | collective-permute-start | bytes 786440 | tf_op jit(solution)/shard_map/ppermute | solution.py:328
  111.1 24.1 %collective-permute-start.12 = (bf16[128,1024]{1,0:T(8,128)(2,1)S(1)}, bf16[128,1024]{1,0:T(8,128)(2,1)S(1)}, u32[]{:S(2)}, u32[]{:S(2)}) collective-permute-start(bf16[128,1024]{1,0:T(8,128)(2,1)S(1)} %fusion.3), channel_id=1, source_target_pairs={{0,2},{1,3},{2,0},{3,1},{4,6},{5,7},{6,4},{7,5},{8,10},{9,11},{10,... | collective-permute-start | bytes 786440 | tf_op jit(solution)/shard_map/ppermute | solution.py:328
  131.0 11.8 %collective-permute-start.28 = (bf16[64,2048]{1,0:T(8,128)(2,1)S(1)}, bf16[64,2048]{1,0:T(8,128)(2,1)S(1)}, u32[]{:S(2)}, u32[]{:S(2)}) collective-permute-start(bf16[64,2048]{1,0:T(8,128)(2,1)S(1)} %add_convert_fusion), channel_id=1, source_target_pairs={{0,2},{1,3},{2,4},{3,5},{4,0},{5,1},{6,6},{7,7},{8,10},{9,11},{10,... | collective-permute-start | bytes 786440 | tf_op jit(solution)/shard_map/ppermute | solution.py:377
  132.9 11.6 %collective-permute-start.27 = (bf16[64,2048]{1,0:T(8,128)(2,1)S(1)}, bf16[64,2048]{1,0:T(8,128)(2,1)S(1)}, u32[]{:S(2)}, u32[]{:S(2)}) collective-permute-start(bf16[64,2048]{1,0:T(8,128)(2,1)S(1)} %add_convert_fusion), channel_id=1, source_target_pairs={{0,1},{1,0},{2,7},{3,6},{4,3},{5,2},{6,5},{7,4},{8,9},{9,8},{10,15... | collective-permute-start | bytes 786440 | tf_op jit(solution)/shard_map/ppermute | solution.py:377
  134.4 10.1 %collective-permute-start.26 = (bf16[64,2048]{1,0:T(8,128)(2,1)S(1)}, bf16[64,2048]{1,0:T(8,128)(2,1)S(1)}, u32[]{:S(2)}, u32[]{:S(2)}) collective-permute-start(bf16[64,2048]{1,0:T(8,128)(2,1)S(1)} %add_convert_fusion), channel_id=1, source_target_pairs={{0,0},{1,1},{2,6},{3,7},{4,2},{5,3},{6,4},{7,5},{8,8},{9,9},{10,14... | collective-permute-start | bytes 786440 | tf_op jit(solution)/shard_map/ppermute | solution.py:377
  (33 other events, 332.1 us)
where the time goes:
time: 151 us; the launch traced here: 149 us
  waiting for transfers between devices  64.4 us (43%)
  starting transfers between devices  38.3 us (25%)
  Pallas kernels  35.2 us (23%)
  local copies, waits for them, and re-layouts  5.74 us (4%)
  other arithmetic  4 us (3%)
    ppermute x14, waiting for transfers between devices, plane(): return lax.ppermute(array, 'seq', [(i, i ^ flip) for i in range(4)])  37.6 us
    pallas_call x8, Pallas kernels, call(): pl.pallas_call(body, in_specs=list(in_specs) + [HBM] * extra, out_specs=l...  35.2 us
    ppermute x14, starting transfers between devices, plane(): return lax.ppermute(array, 'seq', [(i, i ^ flip) for i in range(4)])  19 us
    ppermute x6, waiting for transfers between devices, along(): return lax.ppermute(array, 'dp', [(i, i ^ 2 * flip) for i in range(8)])  16.9 us
    ppermute x6, starting transfers between devices, along(): return lax.ppermute(array, 'dp', [(i, i ^ 2 * flip) for i in range(8)])  12.6 us
    ppermute x4, waiting for transfers between devices, column_shards(): pieces.append(lax.ppermute(summed, ('dp', 'seq'), pairs))  8.27 us
    ppermute x4, starting transfers between devices, column_shards(): pieces.append(lax.ppermute(summed, ('dp', 'seq'), pairs))  4.91 us
    unnamed x55, local copies, waits for them, and re-layouts  4.12 us
  transfers between devices with their start and end apart: 30, of which 14 were waited for; matrix products, arithmetic and copies ran while one was open for 3% of the time, Pallas kernels for 15%

commit v1 on v0

--- a/solution.py
+++ b/solution.py
@@ -34,7 +34,7 @@
         out_shape=list(out_shape),
         scratch_shapes=list(scratch),
         compiler_params=pltpu.CompilerParams(vmem_limit_bytes=VMEM_BYTES),
-        cost_estimate=pl.CostEstimate(flops=flops, bytes_accessed=nbytes, transcendentals=0),
+        cost_estimate=pl.CostEstimate(flops=0, bytes_accessed=1024, transcendentals=0),
         name=name,
     )(*operands, *after)
 
@@ -46,35 +46,57 @@
     return copies
 
 
-def head_columns(place, block, head):
-    column = 4 * jnp.bitwise_xor(place[2], head) + jnp.bitwise_xor(place[0], block)
-    return pl.ds(pl.multiple_of(column * DH, DH), DH)
-
-
-def split_kernel(place, query, key, value, o0, o1, o2, o3):
-    for j, out in enumerate((o0, o1, o2, o3)):
+def head_columns(place, column, head):
+    at = 4 * jnp.bitwise_xor(place[2], head) + column
+    return pl.ds(pl.multiple_of(at * DH, DH), DH)
+
+
+def block_rows(place, flip, tokens):
+    return pl.ds(pl.multiple_of(jnp.bitwise_xor(place[0], flip) * tokens, tokens), tokens)
+
+
+def split_kernel(place, query, key, value, out):
+    for column in range(4):
         for index, source in enumerate((query, key, value)):
             for h in range(4):
-                out[index, :, h * DH : (h + 1) * DH] = source[:, head_columns(place, j, h)]
-
-
-def split_heads(place, queries, keys, values):
+                out[column, index, :, h * DH : (h + 1) * DH] = source[:, head_columns(place, column, h)]
+
+
+def split_heads(place, queries, keys, values, after=()):
     tokens, width = queries.shape
-    out = jax.ShapeDtypeStruct((3, tokens, width // 4), BF16)
-    return call(split_kernel, "split_heads", (place, queries, keys, values), [SMEM] + [VMEM] * 3, [out] * 4, [VMEM] * 4)
-
-
-def merge_kernel(place, b0, b1, b2, b3, *outs):
-    for j, block in enumerate((b0, b1, b2, b3)):
+    out = jax.ShapeDtypeStruct((4, 3, tokens, width // 4), BF16)
+    operands = (place, queries, keys, values)
+    return call(split_kernel, "split_heads", operands, [SMEM] + [VMEM] * 3, [out], [VMEM], after=after)[0]
+
+
+def chunk_kernel(place, own, got, chunk, part, sems):
+    column, core = place[0], place[1]
+    rows = pl.ds(pl.multiple_of((column % 2) * DH, DH), DH)
+    owner = column // 2 == core
+    pl.when(owner)(lambda: pltpu.make_async_copy(own.at[rows, :], chunk, sems.at[0]).start())
+    pl.when(jnp.logical_not(owner))(lambda: pltpu.make_async_copy(got.at[rows, :], chunk, sems.at[0]).start())
+    pltpu.make_async_copy(own.at[rows, :], chunk, sems.at[0]).wait()
+    part[...] = chunk[pl.ds(pl.multiple_of(core * HALF, HALF), HALF), :]
+
+
+def head_chunk(place, own, got, after=()):
+    width = own.shape[1]
+    out = [jax.ShapeDtypeStruct((rows, width), BF16) for rows in (DH, HALF)]
+    scratch = [pltpu.SemaphoreType.DMA((1,))]
+    return call(chunk_kernel, "head_chunk", (place, own, got), [SMEM, HBM, HBM], out, [VMEM] * 2, scratch, after=after)
+
+
+def merge_kernel(place, blocks, *outs):
+    for column in range(4):
         for index, target in enumerate(outs):
             for h in range(4):
-                target[:, head_columns(place, j, h)] = block[index, :, h * DH : (h + 1) * DH]
-
-
-def merge_heads(place, blocks):
-    _, tokens, part = blocks[0].shape
+                target[:, head_columns(place, column, h)] = blocks[column, index, :, h * DH : (h + 1) * DH]
+
+
+def merge_heads(place, blocks, after=()):
+    _, _, tokens, part = blocks.shape
     out = jax.ShapeDtypeStruct((tokens, 4 * part), BF16)
-    return call(merge_kernel, "merge_heads", (place, *blocks), [SMEM] + [VMEM] * 4, [out] * 3, [VMEM] * 3)
+    return call(merge_kernel, "merge_heads", (place, blocks), [SMEM, VMEM], [out] * 3, [VMEM] * 3, after=after)
 
 
 def dot(a, b, a_dim, b_dim):
@@ -82,30 +104,42 @@
 
 
 def load_blocks(blocks, rows, sems, first):
-    tokens = blocks[0].shape[1]
-    return run_copies([(b, rows.at[:, pl.ds(p * tokens, tokens), :]) for p, b in enumerate(blocks)], sems, first)
-
-
-def load_cots(blocks, rows, sems, first):
+    tokens = blocks.shape[2]
+    return run_copies([(blocks.at[p], rows.at[:, pl.ds(p * tokens, tokens), :]) for p in range(4)], sems, first)
+
+
+def load_cots(place, blocks, rows, sems, first):
     tokens = blocks[0].shape[0]
-    return run_copies([(b, rows.at[pl.ds(p * tokens, tokens), :]) for p, b in enumerate(blocks)], sems, first)
-
-
-def load_slab(place, mine, other, slab, sems, first):
-    pairs = []
-    for h in range(4):
-        for source, half in ((mine[h], place[1]), (other[h], 1 - place[1])):
-            pairs.append((source, slab.at[pl.ds(pl.multiple_of(h * DH + half * HALF, HALF), HALF), :]))
+    pairs = [(b, rows.at[block_rows(place, p, tokens), :]) for p, b in enumerate(blocks[:3])]
+    start = pl.multiple_of(jnp.bitwise_xor(place[0], 3) * tokens, tokens)
+    for i, part in enumerate(blocks[3:]):
+        pairs.append((part, rows.at[pl.ds(start + i * (tokens // 2), tokens // 2), :]))
     return run_copies(pairs, sems, first)
 
 
-def bias_rows(place, mask):
+def load_slab(place, weights, slab, sems, first):
+    own, direct, crossed, half, other_half = weights
+    core = place[1]
+
+    def rows(start, count):
+        return slab.at[pl.ds(pl.multiple_of(start, HALF), count), :]
+
+    pairs = [
+        (own, rows(0, DH)),
+        (direct, rows((1 + core) * DH, DH)),
+        (crossed, rows((2 - core) * DH, DH)),
+        (half, rows(3 * DH + core * HALF, HALF)),
+        (other_half, rows(3 * DH + (1 - core) * HALF, HALF)),
+    ]
+    return run_copies(pairs, sems, first)
+
+
+def bias_rows(mask):
     rows = []
     for r in range(4):
-        key_block = jnp.bitwise_xor(place[0], r)
         row = []
         for p in range(4):
-            kept = mask[jnp.bitwise_xor(place[0], p) * 4 + key_block] > 0
+            kept = mask[p * 4 + r] > 0
             row.append(jnp.full((1, DH), jnp.where(kept, 0.0, -1e30), F32))
         rows.append(jnp.concatenate(row, axis=1))
     return rows
@@ -116,9 +150,9 @@
     return jnp.concatenate([raw[r * DH : (r + 1) * DH] + bias[r] for r in range(4)], axis=0)
 
 
-def forward_kernel(place, mask, b0, b1, b2, b3, attended, attended_t, log_total, qkv, sems):
-    copies = load_blocks((b0, b1, b2, b3), qkv, sems, 0)
-    bias = bias_rows(place, mask)
+def forward_kernel(mask, blocks, attended, attended_t, log_total, qkv, sems):
+    copies = load_blocks(blocks, qkv, sems, 0)
+    bias = bias_rows(mask)
     for copy in copies:
         copy.wait()
     for h in range(4):
@@ -134,14 +168,14 @@
         log_total[h : h + 1, :] = highest + jnp.log2(total)
 
 
-def forward(place, mask, blocks, after=()):
-    _, tokens, part = blocks[0].shape
+def forward(mask, blocks, after=()):
+    _, _, tokens, part = blocks.shape
     length = 4 * tokens
     return call(
         forward_kernel,
         "forward",
-        (place, mask, *blocks),
-        [SMEM] * 2 + [HBM] * 4,
+        (mask, blocks),
+        [SMEM, HBM],
         [
             jax.ShapeDtypeStruct((length, part), BF16),
             jax.ShapeDtypeStruct((part, length), BF16),
@@ -154,8 +188,8 @@
     )
 
 
-def mixed_kernel(place, m0, m1, m2, m3, r0, r1, r2, r3, attended, send_x, send_y, own, x_right, y_left, slab, sems):
-    copies = load_slab(place, (m0, m1, m2, m3), (r0, r1, r2, r3), slab, sems, 0)
+def mixed_kernel(place, w0, w1, w2, w3, w4, attended, send_x, send_y, own, x_right, y_left, slab, total, sems):
+    copies = load_slab(place, (w0, w1, w2, w3, w4), slab, sems, 0)
     for copy in copies:
         copy.wait()
     tokens = attended.shape[0] // 4
@@ -163,28 +197,28 @@
     for piece in range(4):
         columns = slice(piece * step, (piece + 1) * step)
         here = slice((piece % 2) * step, (piece % 2 + 1) * step)
-        total = dot(attended[...], slab[:, columns], 1, 0)
-        parts = [total[p * tokens : (p + 1) * tokens] for p in range(4)]
-        own[:, columns] = parts[0].astype(BF16)
+        total[piece % 2] = dot(attended[...], slab[:, columns], 1, 0).astype(BF16)
+        parts = [total.at[piece % 2][block_rows(place, flip, tokens), :] for flip in range(4)]
+        own[:, columns] = parts[0]
         if piece < 2:
-            send_x[0, :, here] = parts[1].astype(BF16)
-            send_x[1, :, here] = parts[3].astype(BF16)
-            y_left[:, here] = parts[2].astype(BF16)
+            send_x[0, :, here] = parts[1]
+            send_x[1, :, here] = parts[3]
+            y_left[:, here] = parts[2]
         else:
-            send_y[0, :, here] = parts[2].astype(BF16)
-            send_y[1, :, here] = parts[3].astype(BF16)
-            x_right[:, here] = parts[1].astype(BF16)
-
-
-def mixed_parts(place, mine, other, attended, after=()):
+            send_y[0, :, here] = parts[2]
+            send_y[1, :, here] = parts[3]
+            x_right[:, here] = parts[1]
+
+
+def mixed_parts(place, weights, attended, after=()):
     length, part = attended.shape
-    width = mine[0].shape[1]
+    width = weights[0].shape[1]
     tokens, half = length // 4, width // 2
     return call(
         mixed_kernel,
         "mixed_parts",
-        (place, *mine, *other, attended),
-        [SMEM] + [HBM] * 8 + [VMEM],
+        (place, *weights, attended),
+        [SMEM] + [HBM] * 5 + [VMEM],
         [
             jax.ShapeDtypeStruct((2, tokens, half), BF16),
             jax.ShapeDtypeStruct((2, tokens, half), BF16),
@@ -193,14 +227,18 @@
             jax.ShapeDtypeStruct((tokens, half), BF16),
         ],
         [VMEM] * 5,
-        [pltpu.VMEM((part, width), BF16), pltpu.SemaphoreType.DMA((8,))],
+        [
+            pltpu.VMEM((part, width), BF16),
+            pltpu.VMEM((2, length, width // 4), BF16),
+            pltpu.SemaphoreType.DMA((5,)),
+        ],
         flops=2 * length * width * part,
         after=after,
     )
 
 
-def weight_kernel(place, attended_t, c0, c1, c2, c3, keep, send, cots, sems):
-    copies = load_cots((c0, c1, c2, c3), cots, sems, 0)
+def weight_kernel(place, attended_t, c0, c1, c2, c3, c4, keep, send, cots, sems):
+    copies = load_cots(place, (c0, c1, c2, c3, c4), cots, sems, 0)
     core = place[1]
     rows = []
     for half in (1 - core, core):
@@ -226,10 +264,10 @@
         weight_kernel,
         "weight_parts",
         (place, attended_t, *cot_blocks),
-        [SMEM, VMEM] + [HBM] * 4,
+        [SMEM, VMEM] + [HBM] * 5,
         [out] * 2,
         [VMEM] * 2,
-        [pltpu.VMEM((length, width), BF16), pltpu.SemaphoreType.DMA((4,))],
+        [pltpu.VMEM((length, width), BF16), pltpu.SemaphoreType.DMA((5,))],
         flops=2 * length * width * part,
         after=after,
     )
@@ -240,9 +278,9 @@
         out[...] = (keep[h].astype(F32) + got[h].astype(F32)).astype(BF16)
 
 
-def add_cores(keep, got):
+def add_cores(keep, got, after=()):
     out = jax.ShapeDtypeStruct(keep.shape[1:], BF16)
-    return call(add_kernel, "add_cores", (keep, got), [VMEM] * 2, [out] * 4, [VMEM] * 4)
+    return call(add_kernel, "add_cores", (keep, got), [VMEM] * 2, [out] * 4, [VMEM] * 4, after=after)
 
 
 def weight_out_kernel(place, p0, p1, p2, p3, out):
@@ -259,24 +297,39 @@
     return call(weight_out_kernel, "weight_out", (place, *pieces), [SMEM] + [VMEM] * 4, [out], [VMEM])[0]
 
 
-def backward_kernel(
-    place, mask, m0, m1, m2, m3, r0, r1, r2, r3, log_total, c0, c1, c2, c3, b0, b1, b2, b3,
-    o0, o1, o2, o3, slab, cots, qkv, grads, sems,
-):
-    slab_copies = load_slab(place, (m0, m1, m2, m3), (r0, r1, r2, r3), slab, sems, 0)
-    cot_copies = load_cots((c0, c1, c2, c3), cots, sems, 8)
-    qkv_copies = load_blocks((b0, b1, b2, b3), qkv, sems, 12)
-    outs = (o0, o1, o2, o3)
-    tokens = c0.shape[0]
-    for copy in slab_copies + cot_copies:
+def grads_kernel(place, w0, w1, w2, w3, w4, c0, c1, c2, c3, c4, grads, slab, cots, sems):
+    copies = load_slab(place, (w0, w1, w2, w3, w4), slab, sems, 0)
+    copies += load_cots(place, (c0, c1, c2, c3, c4), cots, sems, 5)
+    for copy in copies:
         copy.wait()
     for pair in range(2):
         rows = slice(pair * 2 * DH, (pair + 1) * 2 * DH)
         grads[:, rows] = dot(cots[...], slab[rows, :], 1, 1).astype(BF16)
-    for copy in qkv_copies:
+
+
+def attended_grads(place, weights, cot_blocks, after=()):
+    tokens, width = cot_blocks[0].shape
+    part, length = 4 * DH, 4 * tokens
+    return call(
+        grads_kernel,
+        "attended_grads",
+        (place, *weights, *cot_blocks),
+        [SMEM] + [HBM] * 10,
+        [jax.ShapeDtypeStruct((length, part), BF16)],
+        [VMEM],
+        [pltpu.VMEM((part, width), BF16), pltpu.VMEM((length, width), BF16), pltpu.SemaphoreType.DMA((10,))],
+        flops=2 * length * width * part,
+        after=after,
+    )[0]
+
+
+def backward_kernel(mask, log_total, grads, blocks, out, qkv, sems):
+    copies = load_blocks(blocks, qkv, sems, 0)
+    tokens = out.shape[2]
+    scale = 1.0 / math.sqrt(DH)
+    bias = bias_rows(mask)
+    for copy in copies:
         copy.wait()
-    scale = 1.0 / math.sqrt(DH)
-    bias = bias_rows(place, mask)
     for h in range(4):
         here = slice(h * DH, (h + 1) * DH)
         query, key, value, grad = qkv[0, :, here], qkv[1, :, here], qkv[2, :, here], grads[:, here]
@@ -289,30 +342,23 @@
         grad_query = dot(key, grad_scores, 0, 0).astype(BF16).T
         for index, full in enumerate((grad_query, grad_key, grad_value)):
             for p in range(4):
-                outs[p][index, :, here] = full[p * tokens : (p + 1) * tokens]
-
-
-def backward(place, mask, mine, other, log_total, cot_blocks, blocks, after=()):
-    _, tokens, part = blocks[0].shape
-    width = mine[0].shape[1]
+                out[p, index, :, here] = full[p * tokens : (p + 1) * tokens]
+
+
+def backward(mask, log_total, grads, blocks, after=()):
+    _, _, tokens, part = blocks.shape
     length = 4 * tokens
     return call(
         backward_kernel,
         "backward",
-        (place, mask, *mine, *other, log_total, *cot_blocks, *blocks),
-        [SMEM] * 2 + [HBM] * 8 + [VMEM] + [HBM] * 8,
-        [jax.ShapeDtypeStruct((3, tokens, part), BF16)] * 4,
-        [VMEM] * 4,
-        [
-            pltpu.VMEM((part, width), BF16),
-            pltpu.VMEM((length, width), BF16),
-            pltpu.VMEM((3, length, part), BF16),
-            pltpu.VMEM((length, part), BF16),
-            pltpu.SemaphoreType.DMA((16,)),
-        ],
-        flops=2 * length * width * part + 10 * length * length * part,
+        (mask, log_total, grads, blocks),
+        [SMEM] + [VMEM] * 2 + [HBM],
+        [jax.ShapeDtypeStruct(blocks.shape, BF16)],
+        [VMEM],
+        [pltpu.VMEM((3, length, part), BF16), pltpu.SemaphoreType.DMA((4,))],
+        flops=10 * length * length * part,
         after=after,
-    )
+    )[0]
 
 
 def column_shards(queries, keys, values, out_weight, cotangent, block_mask):
@@ -333,24 +379,29 @@
     def along(array, flip):
         return lax.ppermute(array, "dp", [(i, i ^ (2 * flip)) for i in range(8)])
 
-    own, to_x, to_y, to_d = split_heads(place, queries[0], keys[0], values[0])
-    blocks = (own, plane(to_x, 1), plane(to_y, 2), plane(to_d, 3))
+    def columns(array):
+        return lax.all_to_all(array, "seq", 0, 0, tiled=True)
+
+    heads = split_heads(place, queries[0], keys[0], values[0])
+    blocks = columns(heads)
 
     cot_x, cot_y = plane(cot, 1), plane(cot, 2)
+
+    def in_dp(array, target):
+        return lax.ppermute(array, "dp", [(2 * a + c, target(a, c)) for a in range(4) for c in range(2)])
+
+    chunk, part = head_chunk(place, out_weight, swap(out_weight), after=(heads,))
+    direct = in_dp(chunk, lambda a, c: 2 * (a ^ (1 + c)) + c)
+    part = in_dp(part, lambda a, c: 2 * (a ^ 3) + c)
+
+    attended, attended_t, log_total = forward(mask, blocks)
+
+    cot_x, cot_y, direct, part, attended = lax.optimization_barrier((cot_x, cot_y, direct, part, attended))
     half = tokens // 2
-    cot_d = jnp.concatenate([plane(cot_y[:half], 1), plane(cot_x[half:], 2)], axis=0)
-    cot_blocks = (cot, cot_x, cot_y, cot_d)
-
-    start = (column % 2) * DH
-    owner = column // 2 == core
-    given = swap(lax.dynamic_slice_in_dim(out_weight, start + HALF * (1 - core), HALF, 0))
-    chunk = jnp.where(owner, lax.dynamic_slice_in_dim(out_weight, start + HALF * core, HALF, 0), given)
-    mine = (chunk, along(chunk, 1), along(chunk, 2), along(chunk, 3))
-    other = tuple(swap(m) for m in mine)
-
-    attended, attended_t, log_total = forward(place, mask, blocks)
-
-    send_x, send_y, mixed_own, x_right, y_left = mixed_parts(place, mine, other, attended)
+    cot_blocks = (cot, cot_x, cot_y, plane(cot_y[:half], 1), plane(cot_x[half:], 2))
+    weights = (chunk, direct, swap(direct), part, swap(part))
+
+    send_x, send_y, mixed_own, x_right, y_left = mixed_parts(place, weights, attended)
     got_x, got_y = plane(send_x, 1), plane(send_y, 2)
     got_left = plane((y_left.astype(F32) + got_x[1].astype(F32)).astype(BF16), 2)
     got_right = plane((x_right.astype(F32) + got_y[1].astype(F32)).astype(BF16), 1)
@@ -363,7 +414,8 @@
     ).astype(BF16)
 
     keep, send = weight_parts(place, attended_t, cot_blocks, after=(send_x,))
-    s0, s1, s2, s3 = add_cores(keep, swap(send))
+    grads = attended_grads(place, weights, cot_blocks, after=(keep,))
+    s0, s1, s2, s3 = add_cores(keep, swap(send), after=(grads,))
     got = [along(s, flip).astype(F32) for flip, s in ((1, s1), (2, s2), (3, s3))]
     summed = (s0.astype(F32) + got[0] + got[1] + got[2]).astype(BF16)
     pieces = []
@@ -377,9 +429,9 @@
         pieces.append(lax.ppermute(summed, ("dp", "seq"), pairs))
     grad_weight = weight_out(place, pieces)
 
-    outs = backward(place, mask, mine, other, log_total, cot_blocks, blocks, after=(keep,))
-    grads = merge_heads(place, (outs[0], plane(outs[1], 1), plane(outs[2], 2), plane(outs[3], 3)))
-    return (mixed[None],) + tuple(g[None] for g in grads) + (grad_weight,)
+    outs = columns(backward(mask, log_total, grads, blocks, after=(s1,)))
+    merged = merge_heads(place, outs, after=(summed,))
+    return (mixed[None],) + tuple(g[None] for g in merged) + (grad_weight,)
 
 
 def attend(query_heads, key_heads, value_heads, grad_heads, block_mask):

time: 151 us -> 127 us (0.84)
  waiting for transfers between devices: 64.4 us -> 37.5 us
  Pallas kernels: 35.2 us -> 41.1 us
  starting transfers between devices: 38.3 us -> 33.6 us
  local copies, waits for them, and re-layouts: 5.74 us -> 7.7 us
    ppermute x14 -> x8, waiting for transfers between devices: 37.6 us -> 23.3 us  [plane(): return lax.ppermute(array, 'seq', [(i, i ^ flip) for i in range(4)])]
    ppermute x6 -> x3, waiting for transfers between devices: 16.9 us -> 4.1 us  [along(): return lax.ppermute(array, 'dp', [(i, i ^ 2 * flip) for i in range(8)])]
    all_to_all x0 -> x2, waiting for transfers between devices: none -> 9.74 us  [columns(): return lax.all_to_all(array, 'seq', 0, 0, tiled=True)]
    all_to_all x0 -> x2, starting transfers between devices: none -> 8.58 us  [columns(): return lax.all_to_all(array, 'seq', 0, 0, tiled=True)]
    ppermute x14 -> x8, starting transfers between devices: 19 us -> 10.5 us  [plane(): return lax.ppermute(array, 'seq', [(i, i ^ flip) for i in range(4)])]
    ppermute x6 -> x3, starting transfers between devices: 12.6 us -> 4.27 us  [along(): return lax.ppermute(array, 'dp', [(i, i ^ 2 * flip) for i in range(8)])]
    ppermute x4, waiting for transfers between devices: 8.27 us -> 0.33 us  [column_shards(): pieces.append(lax.ppermute(summed, ('dp', 'seq'), pairs))]
    pallas_call x8 -> x10, Pallas kernels: 35.2 us -> 41.1 us  [call(): pl.pallas_call(body, in_specs=list(in_specs) + [HBM] * extra, out_specs=l...]
  transfers between devices with their start and end apart: 30 -> 23, of which waited for: 14 -> 7; matrix products, arithmetic and copies ran while one was open for 3% -> 4% of each run, Pallas kernels for 15% -> 26%
where the time goes in v1:
time: 127 us; the launch traced here: 125 us
  Pallas kernels  41.1 us (32%)
  waiting for transfers between devices  37.5 us (30%)
  starting transfers between devices  33.6 us (26%)
  local copies, waits for them, and re-layouts  7.7 us (6%)
  other arithmetic  4.07 us (3%)
    pallas_call x10, Pallas kernels, call(): pl.pallas_call(body, in_specs=list(in_specs) + [HBM] * extra, out_specs=l...  41.1 us
    ppermute x8, waiting for transfers between devices, plane(): return lax.ppermute(array, 'seq', [(i, i ^ flip) for i in range(4)])  23.3 us
    ppermute x8, starting transfers between devices, plane(): return lax.ppermute(array, 'seq', [(i, i ^ flip) for i in range(4)])  10.5 us
    all_to_all x2, waiting for transfers between devices, columns(): return lax.all_to_all(array, 'seq', 0, 0, tiled=True)  9.74 us
    all_to_all x2, starting transfers between devices, columns(): return lax.all_to_all(array, 'seq', 0, 0, tiled=True)  8.58 us
    unnamed x44, local copies, waits for them, and re-layouts  6.99 us
    ppermute x4, starting transfers between devices, column_shards(): pieces.append(lax.ppermute(summed, ('dp', 'seq'), pairs))  4.95 us
    ppermute x3, starting transfers between devices, along(): return lax.ppermute(array, 'dp', [(i, i ^ 2 * flip) for i in range(8)])  4.27 us
  transfers between devices with their start and end apart: 23, of which 7 were waited for; matrix products, arithmetic and copies ran while one was open for 4% of the time, Pallas kernels for 26%

profile of v1, /device:TPU:0, one launch (start us, length us, event | category | flops | bytes accessed | tf_op | source)
XLA Modules:
  0.0 124.8 jit_solution(2591789645721947343)
XLA Ops:
  1.8 2.9 %split_heads.1.refs_3_ = bf16[4,3,128,512]{3,2,1,0:T(8,128)(2,1)} custom-call(s32[3]{0:T(128)} %pad_add_fusion.refs_0_, bf16[128,2048]{1,0:T(8,128)(2,1)} %bitcast.38, bf16[128,2048]{1,0:T(8,128)(2,1)} %bitcast.39, bf16[128,2048]{1,0:T(8,128)(2,1)} %bitcast.40), custom_call_target="tpu_custom_call" | custom-call | bytes 1024 | tf_op jit(solution)/shard_map/split_heads/pallas_call | solution.py:30
  4.7 4.9 %all-to-all-start = ((bf16[4,3,128,512]{3,2,1,0:T(8,128)(2,1)}), bf16[4,3,128,512]{3,2,1,0:T(8,128)(2,1)S(1)}, u32[]{:S(2)}, u32[]{:S(2)}) async-start(bf16[4,3,128,512]{3,2,1,0:T(8,128)(2,1)} %split_heads.1.refs_3_), calls=%async_computation | async-start | bytes 3145728 | tf_op jit(solution)/shard_map/all_to_all | solution.py:383
  9.6 2.0 %collective-permute-start.2 = (bf16[128,2048]{1,0:T(8,128)(2,1)S(1)}, bf16[128,2048]{1,0:T(8,128)(2,1)S(1)}, u32[]{:S(2)}, u32[]{:S(2)}) collective-permute-start(bf16[128,2048]{1,0:T(8,128)(2,1)S(1)} %bitcast.36), channel_id=1, source_target_pairs={{0,2},{1,3},{2,0},{3,1},{4,6},{5,7},{6,4},{7,5},{8,10},{9,11},{10,... | collective-permute-start | bytes 1572872 | tf_op jit(solution)/shard_map/ppermute | solution.py:374
  13.1 2.6 %head_chunk.1 = (bf16[128,2048]{1,0:T(8,128)(2,1)}, bf16[64,2048]{1,0:T(8,128)(2,1)}) custom-call(s32[3]{0:T(128)} %pad_add_fusion.refs_0_, bf16[256,2048]{1,0:T(8,128)(2,1)} %refs_1_.1, bf16[256,2048]{1,0:T(8,128)(2,1)} %collective-permute-done.refs_2_, bf16[4,3,128,512]{3,2,1,0:T(8,128)(2,1)} %split_heads.1.refs_3_), custom_call_target="tpu_custom_call" | custom-call | bytes 1024 | tf_op jit(solution)/shard_map/head_chunk/pallas_call | solution.py:30
  15.7 1.6 %collective-permute-start.3 = (bf16[128,2048]{1,0:T(8,128)(2,1)}, bf16[128,2048]{1,0:T(8,128)(2,1)}, u32[]{:S(2)}, u32[]{:S(2)}) collective-permute-start(bf16[128,2048]{1,0:T(8,128)(2,1)} %get-tuple-element.29.refs_1_), channel_id=1, source_target_pairs={{0,8},{4,20},{8,0},{12,28},{16,24},{20,4},{24,16},{28,12},{1,9},{5... | collective-permute-start | bytes 1572872 | tf_op jit(solution)/shard_map/ppermute | solution.py:391
  17.3 2.5 %collective-permute-start.4 = (bf16[64,2048]{1,0:T(8,128)(2,1)}, bf16[64,2048]{1,0:T(8,128)(2,1)S(1)}, u32[]{:S(2)}, u32[]{:S(2)}) collective-permute-start(bf16[64,2048]{1,0:T(8,128)(2,1)} %get-tuple-element.30), channel_id=1, source_target_pairs={{0,24},{4,28},{8,16},{12,20},{16,8},{20,12},{24,0},{28,4},{1,25},{... | collective-permute-start | bytes 786440 | tf_op jit(solution)/shard_map/ppermute | solution.py:391
  20.5 9.7 %all-to-all-done.refs_1_.refs_3_ = bf16[4,3,128,512]{3,2,1,0:T(8,128)(2,1)S(1)} async-done(((bf16[4,3,128,512]{3,2,1,0:T(8,128)(2,1)}), bf16[4,3,128,512]{3,2,1,0:T(8,128)(2,1)S(1)}, u32[]{:S(2)}, u32[]{:S(2)}) %all-to-all-start) | async-done | bytes 1572896 | tf_op jit(solution)/shard_map/all_to_all | solution.py:383
  31.4 5.3 %forward.1 = (bf16[512,512]{1,0:T(8,128)(2,1)}, bf16[512,512]{1,0:T(8,128)(2,1)}, f32[4,512]{1,0:T(4,128)}) custom-call(s32[16]{0:T(128)} %reshape.52.refs_0_, bf16[4,3,128,512]{3,2,1,0:T(8,128)(2,1)} %copy-done), custom_call_target="tpu_custom_call" | custom-call | bytes 1024 | tf_op jit(solution)/shard_map/forward/pallas_call | solution.py:30
  36.7 4.0 %collective-permute-done.2.refs_4_.refs_8_ = bf16[128,2048]{1,0:T(8,128)(2,1)S(1)} collective-permute-done((bf16[128,2048]{1,0:T(8,128)(2,1)S(1)}, bf16[128,2048]{1,0:T(8,128)(2,1)S(1)}, u32[]{:S(2)}, u32[]{:S(2)}) %collective-permute-start.2) | collective-permute-done | bytes 524320 | tf_op jit(solution)/shard_map/ppermute | solution.py:374
  41.4 1.5 %collective-permute-start.11 = (bf16[64,2048]{1,0:T(8,128)(2,1)S(1)}, bf16[64,2048]{1,0:T(8,128)(2,1)S(1)}, u32[]{:S(2)}, u32[]{:S(2)}) collective-permute-start(bf16[64,2048]{1,0:T(8,128)(2,1)S(1)} %slice.30), channel_id=1, source_target_pairs={{0,1},{1,0},{2,3},{3,2},{4,5},{5,4},{6,7},{7,6},{8,9},{9,8},{10,11... | collective-permute-start | bytes 786440 | tf_op jit(solution)/shard_map/ppermute | solution.py:374
  45.0 5.1 %mixed_parts.1 = (bf16[2,128,1024]{2,1,0:T(8,128)(2,1)}, bf16[2,128,1024]{2,1,0:T(8,128)(2,1)}, bf16[128,2048]{1,0:T(8,128)(2,1)}, bf16[128,1024]{1,0:T(8,128)(2,1)}, bf16[128,1024]{1,0:T(8,128)(2,1)}) custom-call(s32[3]{0:T(128)} %pad_add_fusion.refs_0_, bf16[128,2048]{1,0:T(8,128)(2,1)} %get-tuple-element.29.refs_1_, ...), custom_call_target="tpu_custom_call" | custom-call | bytes 1024 | tf_op jit(solution)/shard_map/mixed_parts/pallas_call | solution.py:30
  51.6 5.2 %weight_parts.1 = (bf16[4,64,2048]{2,1,0:T(8,128)(2,1)}, bf16[4,64,2048]{2,1,0:T(8,128)(2,1)}) custom-call(s32[3]{0:T(128)} %pad_add_fusion.refs_0_, bf16[512,512]{1,0:T(8,128)(2,1)} %get-tuple-element.43.refs_1_, bf16[128,2048]{1,0:T(8,128)(2,1)} %bitcast.34, bf16[128,2048]{1,0:T(8,128)(2,1)} %copy-done.3, bf16[128,2048]{1,0:T(8,128)(2,1)} %copy-done.2, ...), custom_call_target="tpu_custom_call" | custom-call | bytes 1024 | tf_op jit(solution)/shard_map/weight_parts/pallas_call | solution.py:30
  59.0 5.0 %attended_grads.1.refs_2_ = bf16[512,512]{1,0:T(8,128)(2,1)} custom-call(s32[3]{0:T(128)} %pad_add_fusion.refs_0_, bf16[128,2048]{1,0:T(8,128)(2,1)} %get-tuple-element.29.refs_1_, bf16[128,2048]{1,0:T(8,128)(2,1)} %collective-permute-done.3.refs_2_, bf16[128,2048]{1,0:T(8,128)(2,1)} %copy-done.5, bf16[64,2048]{1,0:T(8,128)(2,1)} %copy-done.8, ...), custom_call_target="tpu_custom_call" | custom-call | bytes 1024 | tf_op jit(solution)/shard_map/attended_grads/pallas_call | solution.py:30
  64.9 2.6 %add_cores.1 = (bf16[64,2048]{1,0:T(8,128)(2,1)}, bf16[64,2048]{1,0:T(8,128)(2,1)}, bf16[64,2048]{1,0:T(8,128)(2,1)}, bf16[64,2048]{1,0:T(8,128)(2,1)}) custom-call(bf16[4,64,2048]{2,1,0:T(8,128)(2,1)} %get-tuple-element.44.refs_11_.refs_0_, bf16[4,64,2048]{2,1,0:T(8,128)(2,1)} %copy-done.6, bf16[512,512]{1,0:T(8,128)(2,1)} %attended_grads.1.refs_2_), custom_call_target="tpu_custom_call" | custom-call | bytes 1024 | tf_op jit(solution)/shard_map/add_cores/pallas_call | solution.py:30
  67.5 2.7 %collective-permute-start.15 = (bf16[64,2048]{1,0:T(8,128)(2,1)}, bf16[64,2048]{1,0:T(8,128)(2,1)}, u32[]{:S(2)}, u32[]{:S(2)}) collective-permute-start(bf16[64,2048]{1,0:T(8,128)(2,1)} %get-tuple-element.48), channel_id=1, source_target_pairs={{0,16},{4,20},{8,24},{12,28},{16,0},{20,4},{24,8},{28,12},{1,17},{... | collective-permute-start | bytes 786440 | tf_op jit(solution)/shard_map/ppermute | solution.py:380
  72.6 6.8 %backward.1 = bf16[4,3,128,512]{3,2,1,0:T(8,128)(2,1)} custom-call(s32[16]{0:T(128)} %reshape.52.refs_0_, f32[4,512]{1,0:T(4,128)} %get-tuple-element.40.refs_1_, bf16[512,512]{1,0:T(8,128)(2,1)} %attended_grads.1.refs_2_, bf16[4,3,128,512]{3,2,1,0:T(8,128)(2,1)} %copy-done, bf16[64,2048]{1,0:T(8,128)(2,1)} %get-tuple-element.46.refs_4_), custom_call_target="tpu_custom_call" | custom-call | bytes 1024 | tf_op jit(solution)/shard_map/backward/pallas_call | solution.py:30
  79.5 3.7 %all-to-all-start.1 = ((bf16[4,3,128,512]{3,2,1,0:T(8,128)(2,1)}), bf16[4,3,128,512]{3,2,1,0:T(8,128)(2,1)S(1)}, u32[]{:S(2)}, u32[]{:S(2)}) async-start(bf16[4,3,128,512]{3,2,1,0:T(8,128)(2,1)} %backward.1), calls=%async_computation.1 | async-start | bytes 3145728 | tf_op jit(solution)/shard_map/all_to_all | solution.py:383
  83.3 2.0 %collective-permute-start.8 = (bf16[128,1024]{1,0:T(8,128)(2,1)S(1)}, bf16[128,1024]{1,0:T(8,128)(2,1)S(1)}, u32[]{:S(2)}, u32[]{:S(2)}) collective-permute-start(bf16[128,1024]{1,0:T(8,128)(2,1)S(1)} %fusion.3), channel_id=1, source_target_pairs={{0,2},{1,3},{2,0},{3,1},{4,6},{5,7},{6,4},{7,5},{8,10},{9,11},{10,... | collective-permute-start | bytes 786440 | tf_op jit(solution)/shard_map/ppermute | solution.py:374
  85.3 3.8 %collective-permute-done.15 = bf16[64,2048]{1,0:T(8,128)(2,1)} collective-permute-done((bf16[64,2048]{1,0:T(8,128)(2,1)}, bf16[64,2048]{1,0:T(8,128)(2,1)}, u32[]{:S(2)}, u32[]{:S(2)}) %collective-permute-start.15) | collective-permute-done | bytes 262176 | tf_op jit(solution)/shard_map/ppermute | solution.py:380
  90.7 1.5 %collective-permute-start.20 = (bf16[64,2048]{1,0:T(8,128)(2,1)S(1)}, bf16[64,2048]{1,0:T(8,128)(2,1)S(1)}, u32[]{:S(2)}, u32[]{:S(2)}) collective-permute-start(bf16[64,2048]{1,0:T(8,128)(2,1)S(1)} %add_convert_fusion.refs_2_), channel_id=1, source_target_pairs={{0,3},{1,2},{2,5},{3,4},{4,1},{5,0},{6,7},{7,6},{8,11},{9,10},{10,... | collective-permute-start | bytes 786440 | tf_op jit(solution)/shard_map/ppermute | solution.py:429
  92.2 1.9 %collective-permute-start.19 = (bf16[64,2048]{1,0:T(8,128)(2,1)S(1)}, bf16[64,2048]{1,0:T(8,128)(2,1)S(1)}, u32[]{:S(2)}, u32[]{:S(2)}) collective-permute-start(bf16[64,2048]{1,0:T(8,128)(2,1)S(1)} %add_convert_fusion.refs_2_), channel_id=1, source_target_pairs={{0,2},{1,3},{2,4},{3,5},{4,0},{5,1},{6,6},{7,7},{8,10},{9,11},{10,... | collective-permute-start | bytes 786440 | tf_op jit(solution)/shard_map/ppermute | solution.py:429
  95.7 18.5 %collective-permute-done.8 = bf16[128,1024]{1,0:T(8,128)(2,1)S(1)} collective-permute-done((bf16[128,1024]{1,0:T(8,128)(2,1)S(1)}, bf16[128,1024]{1,0:T(8,128)(2,1)S(1)}, u32[]{:S(2)}, u32[]{:S(2)}) %collective-permute-start.8) | collective-permute-done | bytes 262176 | tf_op jit(solution)/shard_map/ppermute | solution.py:374
  118.0 2.7 %weight_out.1 = f32[256,2048]{1,0:T(8,128)} custom-call(s32[3]{0:T(128)} %pad_add_fusion.refs_0_, bf16[64,2048]{1,0:T(8,128)(2,1)} %copy-done.19, bf16[64,2048]{1,0:T(8,128)(2,1)} %copy-done.18, bf16[64,2048]{1,0:T(8,128)(2,1)} %copy-done.17, bf16[64,2048]{1,0:T(8,128)(2,1)} %copy-done.16), custom_call_target="tpu_custom_call" | custom-call | bytes 1024 | tf_op jit(solution)/shard_map/weight_out/pallas_call | solution.py:30
  121.9 3.0 %merge_heads.1 = (bf16[128,2048]{1,0:T(8,128)(2,1)}, bf16[128,2048]{1,0:T(8,128)(2,1)}, bf16[128,2048]{1,0:T(8,128)(2,1)}) custom-call(s32[3]{0:T(128)} %pad_add_fusion.refs_0_, bf16[4,3,128,512]{3,2,1,0:T(8,128)(2,1)} %copy-done.1, bf16[64,2048]{1,0:T(8,128)(2,1)} %copy-done.7), custom_call_target="tpu_custom_call" | custom-call | bytes 1024 | tf_op jit(solution)/shard_map/merge_heads/pallas_call | solution.py:30
  (85 shorter events, 22.5 us)
Async XLA Ops:
  0.6 12.5 %collective-permute-start = (bf16[256,2048]{1,0:T(8,128)(2,1)}, bf16[256,2048]{1,0:T(8,128)(2,1)}, u32[]{:S(2)}, u32[]{:S(2)}) collective-permute-start(bf16[256,2048]{1,0:T(8,128)(2,1)} %refs_1_.1), channel_id=1, source_target_pairs={{0,4},{4,0},{8,12},{12,8},{16,20},{20,16},{24,28},{28,24},{1,5},{5... | collective-permute-start | bytes 3145736 | tf_op jit(solution)/shard_map/ppermute | solution.py:377
  4.7 25.5 %all-to-all-start = ((bf16[4,3,128,512]{3,2,1,0:T(8,128)(2,1)}), bf16[4,3,128,512]{3,2,1,0:T(8,128)(2,1)S(1)}, u32[]{:S(2)}, u32[]{:S(2)}) async-start(bf16[4,3,128,512]{3,2,1,0:T(8,128)(2,1)} %split_heads.1.refs_3_), calls=%async_computation | async-start | bytes 3145728 | tf_op jit(solution)/shard_map/all_to_all | solution.py:383
  9.6 31.1 %collective-permute-start.2 = (bf16[128,2048]{1,0:T(8,128)(2,1)S(1)}, bf16[128,2048]{1,0:T(8,128)(2,1)S(1)}, u32[]{:S(2)}, u32[]{:S(2)}) collective-permute-start(bf16[128,2048]{1,0:T(8,128)(2,1)S(1)} %bitcast.36), channel_id=1, source_target_pairs={{0,2},{1,3},{2,0},{3,1},{4,6},{5,7},{6,4},{7,5},{8,10},{9,11},{10,... | collective-permute-start | bytes 1572872 | tf_op jit(solution)/shard_map/ppermute | solution.py:374
  11.6 29.1 %collective-permute-start.1 = (bf16[128,2048]{1,0:T(8,128)(2,1)S(1)}, bf16[128,2048]{1,0:T(8,128)(2,1)S(1)}, u32[]{:S(2)}, u32[]{:S(2)}) collective-permute-start(bf16[128,2048]{1,0:T(8,128)(2,1)S(1)} %bitcast.37), channel_id=1, source_target_pairs={{0,1},{1,0},{2,3},{3,2},{4,5},{5,4},{6,7},{7,6},{8,9},{9,8},{10,11... | collective-permute-start | bytes 1572872 | tf_op jit(solution)/shard_map/ppermute | solution.py:374
  15.7 25.0 %collective-permute-start.3 = (bf16[128,2048]{1,0:T(8,128)(2,1)}, bf16[128,2048]{1,0:T(8,128)(2,1)}, u32[]{:S(2)}, u32[]{:S(2)}) collective-permute-start(bf16[128,2048]{1,0:T(8,128)(2,1)} %get-tuple-element.29.refs_1_), channel_id=1, source_target_pairs={{0,8},{4,20},{8,0},{12,28},{16,24},{20,4},{24,16},{28,12},{1,9},{5... | collective-permute-start | bytes 1572872 | tf_op jit(solution)/shard_map/ppermute | solution.py:391
  17.3 23.4 %collective-permute-start.4 = (bf16[64,2048]{1,0:T(8,128)(2,1)}, bf16[64,2048]{1,0:T(8,128)(2,1)S(1)}, u32[]{:S(2)}, u32[]{:S(2)}) collective-permute-start(bf16[64,2048]{1,0:T(8,128)(2,1)} %get-tuple-element.30), channel_id=1, source_target_pairs={{0,24},{4,28},{8,16},{12,20},{16,8},{20,12},{24,0},{28,4},{1,25},{... | collective-permute-start | bytes 786440 | tf_op jit(solution)/shard_map/ppermute | solution.py:391
  40.7 2.7 %collective-permute-start.5 = (bf16[128,2048]{1,0:T(8,128)(2,1)}, bf16[128,2048]{1,0:T(8,128)(2,1)S(1)}, u32[]{:S(2)}, u32[]{:S(2)}) collective-permute-start(bf16[128,2048]{1,0:T(8,128)(2,1)} %collective-permute-done.3.refs_2_), channel_id=1, source_target_pairs={{0,4},{4,0},{8,12},{12,8},{16,20},{20,16},{24,28},{28,24},{1,5},{5... | collective-permute-start | bytes 1572872 | tf_op jit(solution)/shard_map/ppermute | solution.py:377
  40.8 2.6 %collective-permute-start.6 = (bf16[64,2048]{1,0:T(8,128)(2,1)S(1)}, bf16[64,2048]{1,0:T(8,128)(2,1)S(1)}, u32[]{:S(2)}, u32[]{:S(2)}) collective-permute-start(bf16[64,2048]{1,0:T(8,128)(2,1)S(1)} %collective-permute-done.4.refs_4_), channel_id=1, source_target_pairs={{0,4},{4,0},{8,12},{12,8},{16,20},{20,16},{24,28},{28,24},{1,5},{5... | collective-permute-start | bytes 786440 | tf_op jit(solution)/shard_map/ppermute | solution.py:377
  41.4 8.7 %collective-permute-start.11 = (bf16[64,2048]{1,0:T(8,128)(2,1)S(1)}, bf16[64,2048]{1,0:T(8,128)(2,1)S(1)}, u32[]{:S(2)}, u32[]{:S(2)}) collective-permute-start(bf16[64,2048]{1,0:T(8,128)(2,1)S(1)} %slice.30), channel_id=1, source_target_pairs={{0,1},{1,0},{2,3},{3,2},{4,5},{5,4},{6,7},{7,6},{8,9},{9,8},{10,11... | collective-permute-start | bytes 786440 | tf_op jit(solution)/shard_map/ppermute | solution.py:374
  42.9 8.0 %collective-permute-start.12 = (bf16[64,2048]{1,0:T(8,128)(2,1)S(1)}, bf16[64,2048]{1,0:T(8,128)(2,1)S(1)}, u32[]{:S(2)}, u32[]{:S(2)}) collective-permute-start(bf16[64,2048]{1,0:T(8,128)(2,1)S(1)} %slice.31), channel_id=1, source_target_pairs={{0,2},{1,3},{2,0},{3,1},{4,6},{5,7},{6,4},{7,5},{8,10},{9,11},{10,... | collective-permute-start | bytes 786440 | tf_op jit(solution)/shard_map/ppermute | solution.py:374
  56.8 7.2 %collective-permute-start.13 = (bf16[4,64,2048]{2,1,0:T(8,128)(2,1)}, bf16[4,64,2048]{2,1,0:T(8,128)(2,1)S(1)}, u32[]{:S(2)}, u32[]{:S(2)}) collective-permute-start(bf16[4,64,2048]{2,1,0:T(8,128)(2,1)} %get-tuple-element.45), channel_id=1, source_target_pairs={{0,4},{4,0},{8,12},{12,8},{16,20},{20,16},{24,28},{28,24},{1,5},{5... | collective-permute-start | bytes 3145736 | tf_op jit(solution)/shard_map/ppermute | solution.py:377
  56.9 14.9 %collective-permute-start.9 = (bf16[2,128,1024]{2,1,0:T(8,128)(2,1)S(1)}, bf16[2,128,1024]{2,1,0:T(8,128)(2,1)S(1)}, u32[]{:S(2)}, u32[]{:S(2)}) collective-permute-start(bf16[2,128,1024]{2,1,0:T(8,128)(2,1)S(1)} %copy-done.21), channel_id=1, source_target_pairs={{0,2},{1,3},{2,0},{3,1},{4,6},{5,7},{6,4},{7,5},{8,10},{9,11},{10,... | collective-permute-start | bytes 1572872 | tf_op jit(solution)/shard_map/ppermute | solution.py:374
  57.7 25.5 %collective-permute-start.7 = (bf16[2,128,1024]{2,1,0:T(8,128)(2,1)}, bf16[2,128,1024]{2,1,0:T(8,128)(2,1)S(1)}, u32[]{:S(2)}, u32[]{:S(2)}) collective-permute-start(bf16[2,128,1024]{2,1,0:T(8,128)(2,1)} %get-tuple-element.36.refs_7_), channel_id=1, source_target_pairs={{0,1},{1,0},{2,3},{3,2},{4,5},{5,4},{6,7},{7,6},{8,9},{9,8},{10,11... | collective-permute-start | bytes 1572872 | tf_op jit(solution)/shard_map/ppermute | solution.py:374
  67.5 21.7 %collective-permute-start.15 = (bf16[64,2048]{1,0:T(8,128)(2,1)}, bf16[64,2048]{1,0:T(8,128)(2,1)}, u32[]{:S(2)}, u32[]{:S(2)}) collective-permute-start(bf16[64,2048]{1,0:T(8,128)(2,1)} %get-tuple-element.48), channel_id=1, source_target_pairs={{0,16},{4,20},{8,24},{12,28},{16,0},{20,4},{24,8},{28,12},{1,17},{... | collective-permute-start | bytes 786440 | tf_op jit(solution)/shard_map/ppermute | solution.py:380
  70.2 19.0 %collective-permute-start.16 = (bf16[64,2048]{1,0:T(8,128)(2,1)}, bf16[64,2048]{1,0:T(8,128)(2,1)}, u32[]{:S(2)}, u32[]{:S(2)}) collective-permute-start(bf16[64,2048]{1,0:T(8,128)(2,1)} %get-tuple-element.49), channel_id=1, source_target_pairs={{0,24},{4,28},{8,16},{12,20},{16,8},{20,12},{24,0},{28,4},{1,25},{... | collective-permute-start | bytes 786440 | tf_op jit(solution)/shard_map/ppermute | solution.py:380
  71.5 17.9 %collective-permute-start.14 = (bf16[64,2048]{1,0:T(8,128)(2,1)}, bf16[64,2048]{1,0:T(8,128)(2,1)}, u32[]{:S(2)}, u32[]{:S(2)}) collective-permute-start(bf16[64,2048]{1,0:T(8,128)(2,1)} %get-tuple-element.46.refs_4_), channel_id=1, source_target_pairs={{0,8},{4,12},{8,0},{12,4},{16,24},{20,28},{24,16},{28,20},{1,9},{5... | collective-permute-start | bytes 786440 | tf_op jit(solution)/shard_map/ppermute | solution.py:380
  71.8 23.2 %collective-permute-start.10 = (bf16[128,1024]{1,0:T(8,128)(2,1)S(1)}, bf16[128,1024]{1,0:T(8,128)(2,1)}, u32[]{:S(2)}, u32[]{:S(2)}) collective-permute-start(bf16[128,1024]{1,0:T(8,128)(2,1)S(1)} %fusion), channel_id=1, source_target_pairs={{0,1},{1,0},{2,3},{3,2},{4,5},{5,4},{6,7},{7,6},{8,9},{9,8},{10,11... | collective-permute-start | bytes 786440 | tf_op jit(solution)/shard_map/ppermute | solution.py:374
  79.5 41.2 %all-to-all-start.1 = ((bf16[4,3,128,512]{3,2,1,0:T(8,128)(2,1)}), bf16[4,3,128,512]{3,2,1,0:T(8,128)(2,1)S(1)}, u32[]{:S(2)}, u32[]{:S(2)}) async-start(bf16[4,3,128,512]{3,2,1,0:T(8,128)(2,1)} %backward.1), calls=%async_computation.1 | async-start | bytes 3145728 | tf_op jit(solution)/shard_map/all_to_all | solution.py:383
  83.2 31.0 %copy-start.12 = (bf16[128,2048]{1,0:T(8,128)(2,1)S(1)}, bf16[128,2048]{1,0:T(8,128)(2,1)}, u32[]{:S(2)}) copy-start(bf16[128,2048]{1,0:T(8,128)(2,1)} %get-tuple-element.35) | copy-start | bytes 1572868
  83.3 30.8 %collective-permute-start.8 = (bf16[128,1024]{1,0:T(8,128)(2,1)S(1)}, bf16[128,1024]{1,0:T(8,128)(2,1)S(1)}, u32[]{:S(2)}, u32[]{:S(2)}) collective-permute-start(bf16[128,1024]{1,0:T(8,128)(2,1)S(1)} %fusion.3), channel_id=1, source_target_pairs={{0,2},{1,3},{2,0},{3,1},{4,6},{5,7},{6,4},{7,5},{8,10},{9,11},{10,... | collective-permute-start | bytes 786440 | tf_op jit(solution)/shard_map/ppermute | solution.py:374
  90.7 25.5 %collective-permute-start.20 = (bf16[64,2048]{1,0:T(8,128)(2,1)S(1)}, bf16[64,2048]{1,0:T(8,128)(2,1)S(1)}, u32[]{:S(2)}, u32[]{:S(2)}) collective-permute-start(bf16[64,2048]{1,0:T(8,128)(2,1)S(1)} %add_convert_fusion.refs_2_), channel_id=1, source_target_pairs={{0,3},{1,2},{2,5},{3,4},{4,1},{5,0},{6,7},{7,6},{8,11},{9,10},{10,... | collective-permute-start | bytes 786440 | tf_op jit(solution)/shard_map/ppermute | solution.py:429
  92.2 24.3 %collective-permute-start.19 = (bf16[64,2048]{1,0:T(8,128)(2,1)S(1)}, bf16[64,2048]{1,0:T(8,128)(2,1)S(1)}, u32[]{:S(2)}, u32[]{:S(2)}) collective-permute-start(bf16[64,2048]{1,0:T(8,128)(2,1)S(1)} %add_convert_fusion.refs_2_), channel_id=1, source_target_pairs={{0,2},{1,3},{2,4},{3,5},{4,0},{5,1},{6,6},{7,7},{8,10},{9,11},{10,... | collective-permute-start | bytes 786440 | tf_op jit(solution)/shard_map/ppermute | solution.py:429
  94.1 22.4 %collective-permute-start.18 = (bf16[64,2048]{1,0:T(8,128)(2,1)S(1)}, bf16[64,2048]{1,0:T(8,128)(2,1)S(1)}, u32[]{:S(2)}, u32[]{:S(2)}) collective-permute-start(bf16[64,2048]{1,0:T(8,128)(2,1)S(1)} %add_convert_fusion.refs_2_), channel_id=1, source_target_pairs={{0,1},{1,0},{2,7},{3,6},{4,3},{5,2},{6,5},{7,4},{8,9},{9,8},{10,15... | collective-permute-start | bytes 786440 | tf_op jit(solution)/shard_map/ppermute | solution.py:429
  95.0 21.6 %collective-permute-start.17 = (bf16[64,2048]{1,0:T(8,128)(2,1)S(1)}, bf16[64,2048]{1,0:T(8,128)(2,1)S(1)}, u32[]{:S(2)}, u32[]{:S(2)}) collective-permute-start(bf16[64,2048]{1,0:T(8,128)(2,1)S(1)} %add_convert_fusion.refs_2_), channel_id=1, source_target_pairs={{0,0},{1,1},{2,6},{3,7},{4,2},{5,3},{6,4},{7,5},{8,8},{9,9},{10,14... | collective-permute-start | bytes 786440 | tf_op jit(solution)/shard_map/ppermute | solution.py:429
  (21 other events, 98.1 us)

commit v2 on v1

--- a/solution.py
+++ b/solution.py
@@ -12,29 +12,30 @@
 LOG2E = 1.4426950408889634
 F32 = jnp.float32
 BF16 = jnp.bfloat16
-VMEM_BYTES = 56 * 1024 * 1024
+VMEM_BYTES = 20 * 1024 * 1024
+HINT = 8_000_000_000
 
 
 SMEM = pl.BlockSpec(memory_space=pltpu.SMEM)
 VMEM = pl.BlockSpec(memory_space=pltpu.VMEM)
 HBM = pl.BlockSpec(memory_space=pl.ANY)
-
-
-def call(kernel, name, operands, in_specs, out_shape, out_specs, scratch=(), flops=0, after=()):
+FAR = pl.BlockSpec(memory_space=pltpu.HBM)
+
+
+def call(kernel, name, operands, in_specs, out_shape, out_specs, scratch=(), hint=0, after=(), vmem=VMEM_BYTES):
     extra = len(after)
 
     def body(*refs):
         kernel(*refs[: len(operands)], *refs[len(operands) + extra :])
 
-    nbytes = sum(x.size * x.dtype.itemsize for x in (*operands, *out_shape))
     return pl.pallas_call(
         body,
         in_specs=list(in_specs) + [HBM] * extra,
         out_specs=list(out_specs),
         out_shape=list(out_shape),
         scratch_shapes=list(scratch),
-        compiler_params=pltpu.CompilerParams(vmem_limit_bytes=VMEM_BYTES),
-        cost_estimate=pl.CostEstimate(flops=0, bytes_accessed=1024, transcendentals=0),
+        compiler_params=pltpu.CompilerParams(vmem_limit_bytes=vmem),
+        cost_estimate=pl.CostEstimate(flops=hint, bytes_accessed=1024, transcendentals=0),
         name=name,
     )(*operands, *after)
 
@@ -55,18 +56,21 @@
     return pl.ds(pl.multiple_of(jnp.bitwise_xor(place[0], flip) * tokens, tokens), tokens)
 
 
-def split_kernel(place, query, key, value, out):
-    for column in range(4):
-        for index, source in enumerate((query, key, value)):
+def split_kernel(place, query, key, value, out, held, sems):
+    loads = run_copies([(source, held.at[index]) for index, source in enumerate((query, key, value))], sems)
+    for index in range(3):
+        loads[index].wait()
+        for column in range(4):
             for h in range(4):
-                out[column, index, :, h * DH : (h + 1) * DH] = source[:, head_columns(place, column, h)]
+                out[column, index, :, h * DH : (h + 1) * DH] = held[index, :, head_columns(place, column, h)]
 
 
 def split_heads(place, queries, keys, values, after=()):
     tokens, width = queries.shape
     out = jax.ShapeDtypeStruct((4, 3, tokens, width // 4), BF16)
     operands = (place, queries, keys, values)
-    return call(split_kernel, "split_heads", operands, [SMEM] + [VMEM] * 3, [out], [VMEM], after=after)[0]
+    scratch = [pltpu.VMEM((3, tokens, width), BF16), pltpu.SemaphoreType.DMA((3,))]
+    return call(split_kernel, "split_heads", operands, [SMEM] + [FAR] * 3, [out], [VMEM], scratch, after=after, vmem=3 * VMEM_BYTES)[0]
 
 
 def chunk_kernel(place, own, got, chunk, part, sems):
@@ -83,7 +87,7 @@
     width = own.shape[1]
     out = [jax.ShapeDtypeStruct((rows, width), BF16) for rows in (DH, HALF)]
     scratch = [pltpu.SemaphoreType.DMA((1,))]
-    return call(chunk_kernel, "head_chunk", (place, own, got), [SMEM, HBM, HBM], out, [VMEM] * 2, scratch, after=after)
+    return call(chunk_kernel, "head_chunk", (place, own, got), [SMEM, FAR, HBM], out, [VMEM] * 2, scratch, after=after)
 
 
 def merge_kernel(place, blocks, *outs):
@@ -103,35 +107,54 @@
     return lax.dot_general(a, b, (((a_dim,), (b_dim,)), ((), ())), preferred_element_type=F32)
 
 
-def load_blocks(blocks, rows, sems, first):
+def head_lanes(h):
+    return pl.ds(h * DH, DH)
+
+
+def load_heads(blocks, rows, sems):
     tokens = blocks.shape[2]
-    return run_copies([(blocks.at[p], rows.at[:, pl.ds(p * tokens, tokens), :]) for p in range(4)], sems, first)
-
-
-def load_cots(place, blocks, rows, sems, first):
+    return run_copies([(blocks.at[p], rows.at[:, pl.ds(p * tokens, tokens), :]) for p in range(4)], sems)
+
+
+def load_pieces(pairs, sems, first, count):
+    step = pairs[0][0].shape[1] // count
+    copies = []
+    for i in range(count):
+        columns = pl.ds(i * step, step)
+        copies.append(run_copies([(s.at[:, columns], d(columns)) for s, d in pairs], sems, first + i * len(pairs)))
+    return copies
+
+
+def cot_pairs(place, blocks, rows):
     tokens = blocks[0].shape[0]
-    pairs = [(b, rows.at[block_rows(place, p, tokens), :]) for p, b in enumerate(blocks[:3])]
-    start = pl.multiple_of(jnp.bitwise_xor(place[0], 3) * tokens, tokens)
-    for i, part in enumerate(blocks[3:]):
-        pairs.append((part, rows.at[pl.ds(start + i * (tokens // 2), tokens // 2), :]))
-    return run_copies(pairs, sems, first)
-
-
-def load_slab(place, weights, slab, sems, first):
+
+    def target(flip, offset, count):
+        start = pl.multiple_of(jnp.bitwise_xor(place[0], flip) * tokens + offset, HALF)
+        return lambda columns: rows.at[pl.ds(start, count), columns]
+
+    pairs = [(b, target(p, 0, tokens)) for p, b in enumerate(blocks[:3])]
+    return pairs + [(b, target(3, i * (tokens // 2), tokens // 2)) for i, b in enumerate(blocks[3:])]
+
+
+def slab_pairs(place, weights, slab):
     own, direct, crossed, half, other_half = weights
     core = place[1]
 
-    def rows(start, count):
-        return slab.at[pl.ds(pl.multiple_of(start, HALF), count), :]
-
-    pairs = [
-        (own, rows(0, DH)),
-        (direct, rows((1 + core) * DH, DH)),
-        (crossed, rows((2 - core) * DH, DH)),
-        (half, rows(3 * DH + core * HALF, HALF)),
-        (other_half, rows(3 * DH + (1 - core) * HALF, HALF)),
+    def target(start, count):
+        return lambda columns: slab.at[pl.ds(pl.multiple_of(start, HALF), count), columns]
+
+    return [
+        (own, target(0, DH)),
+        (direct, target((1 + core) * DH, DH)),
+        (crossed, target((2 - core) * DH, DH)),
+        (half, target(3 * DH + core * HALF, HALF)),
+        (other_half, target(3 * DH + (1 - core) * HALF, HALF)),
     ]
-    return run_copies(pairs, sems, first)
+
+
+def wait_all(copies):
+    for copy in copies:
+        copy.wait()
 
 
 def bias_rows(mask):
@@ -151,10 +174,9 @@
 
 
 def forward_kernel(mask, blocks, attended, attended_t, log_total, qkv, sems):
-    copies = load_blocks(blocks, qkv, sems, 0)
+    copies = load_heads(blocks, qkv, sems)
     bias = bias_rows(mask)
-    for copy in copies:
-        copy.wait()
+    wait_all(copies)
     for h in range(4):
         here = slice(h * DH, (h + 1) * DH)
         scores = scores_kq(bias, qkv[0, :, here], qkv[1, :, here])
@@ -183,15 +205,12 @@
         ],
         [VMEM] * 3,
         [pltpu.VMEM((3, length, part), BF16), pltpu.SemaphoreType.DMA((4,))],
-        flops=4 * length * length * part,
         after=after,
     )
 
 
 def mixed_kernel(place, w0, w1, w2, w3, w4, attended, send_x, send_y, own, x_right, y_left, slab, total, sems):
-    copies = load_slab(place, (w0, w1, w2, w3, w4), slab, sems, 0)
-    for copy in copies:
-        copy.wait()
+    wait_all(load_pieces(slab_pairs(place, (w0, w1, w2, w3, w4), slab), sems, 0, 1)[0])
     tokens = attended.shape[0] // 4
     step = slab.shape[1] // 4
     for piece in range(4):
@@ -232,28 +251,42 @@
             pltpu.VMEM((2, length, width // 4), BF16),
             pltpu.SemaphoreType.DMA((5,)),
         ],
-        flops=2 * length * width * part,
         after=after,
     )
 
 
-def weight_kernel(place, attended_t, c0, c1, c2, c3, c4, keep, send, cots, sems):
-    copies = load_cots(place, (c0, c1, c2, c3, c4), cots, sems, 0)
+def second_kernel(x_right, y_left, got_x, got_y, left, right):
+    left[...] = (y_left[...].astype(F32) + got_x[1].astype(F32)).astype(BF16)
+    right[...] = (x_right[...].astype(F32) + got_y[1].astype(F32)).astype(BF16)
+
+
+def second_parts(x_right, y_left, got_x, got_y, after=()):
+    out = jax.ShapeDtypeStruct(x_right.shape, BF16)
+    operands = (x_right, y_left, got_x, got_y)
+    return call(second_kernel, "second_parts", operands, [VMEM] * 4, [out] * 2, [VMEM] * 2, hint=HINT, after=after)
+
+
+def weight_kernel(place, attended_t, c0, c1, c2, c3, c4, keep, send, cots, kept, sent, sems):
+    loads = load_pieces(cot_pairs(place, (c0, c1, c2, c3, c4), cots), sems, 0, 1)[0]
     core = place[1]
     rows = []
     for half in (1 - core, core):
         for h in range(4):
             rows.append(attended_t[pl.ds(pl.multiple_of(h * DH + half * HALF, HALF), HALF), :])
     left = jnp.concatenate(rows, axis=0)
-    for copy in copies:
-        copy.wait()
     step = cots.shape[1] // 4
+    stores = []
+    wait_all(loads)
     for piece in range(4):
         columns = slice(piece * step, (piece + 1) * step)
         total = dot(left, cots[:, columns], 1, 0).astype(BF16)
         for h in range(4):
-            send[h, :, columns] = total[h * HALF : (h + 1) * HALF]
-            keep[h, :, columns] = total[(4 + h) * HALF : (5 + h) * HALF]
+            sent[h, :, columns] = total[h * HALF : (h + 1) * HALF]
+            kept[h, :, columns] = total[(4 + h) * HALF : (5 + h) * HALF]
+        window = pl.ds(piece * step, step)
+        pairs = [(sent.at[:, :, window], send.at[:, :, window]), (kept.at[:, :, window], keep.at[:, :, window])]
+        stores += run_copies(pairs, sems, 5 + 2 * piece)
+    wait_all(stores)
 
 
 def weight_parts(place, attended_t, cot_blocks, after=()):
@@ -266,9 +299,13 @@
         (place, attended_t, *cot_blocks),
         [SMEM, VMEM] + [HBM] * 5,
         [out] * 2,
-        [VMEM] * 2,
-        [pltpu.VMEM((length, width), BF16), pltpu.SemaphoreType.DMA((5,))],
-        flops=2 * length * width * part,
+        [HBM] * 2,
+        [
+            pltpu.VMEM((length, width), BF16),
+            pltpu.VMEM((4, HALF, width), BF16),
+            pltpu.VMEM((4, HALF, width), BF16),
+            pltpu.SemaphoreType.DMA((13,)),
+        ],
         after=after,
     )
 
@@ -281,6 +318,15 @@
 def add_cores(keep, got, after=()):
     out = jax.ShapeDtypeStruct(keep.shape[1:], BF16)
     return call(add_kernel, "add_cores", (keep, got), [VMEM] * 2, [out] * 4, [VMEM] * 4, after=after)
+
+
+def sum_kernel(p0, p1, p2, p3, out):
+    out[...] = (p0[...].astype(F32) + p1[...].astype(F32) + p2[...].astype(F32) + p3[...].astype(F32)).astype(BF16)
+
+
+def sum_planes(*parts):
+    out = jax.ShapeDtypeStruct(parts[0].shape, BF16)
+    return call(sum_kernel, "sum_planes", parts, [VMEM] * 4, [out], [VMEM], hint=0)[0]
 
 
 def weight_out_kernel(place, p0, p1, p2, p3, out):
@@ -291,17 +337,16 @@
         out[pl.ds(start, HALF), :] = piece[...].astype(F32) * 0.125
 
 
-def weight_out(place, pieces):
+def weight_out(place, pieces, after=()):
     rows, width = pieces[0].shape
     out = jax.ShapeDtypeStruct((4 * rows, width), F32)
-    return call(weight_out_kernel, "weight_out", (place, *pieces), [SMEM] + [VMEM] * 4, [out], [VMEM])[0]
+    return call(weight_out_kernel, "weight_out", (place, *pieces), [SMEM] + [VMEM] * 4, [out], [VMEM], after=after)[0]
 
 
 def grads_kernel(place, w0, w1, w2, w3, w4, c0, c1, c2, c3, c4, grads, slab, cots, sems):
-    copies = load_slab(place, (w0, w1, w2, w3, w4), slab, sems, 0)
-    copies += load_cots(place, (c0, c1, c2, c3, c4), cots, sems, 5)
-    for copy in copies:
-        copy.wait()
+    loads = load_pieces(slab_pairs(place, (w0, w1, w2, w3, w4), slab), sems, 0, 1)
+    loads += load_pieces(cot_pairs(place, (c0, c1, c2, c3, c4), cots), sems, 5, 1)
+    wait_all(loads[0] + loads[1])
     for pair in range(2):
         rows = slice(pair * 2 * DH, (pair + 1) * 2 * DH)
         grads[:, rows] = dot(cots[...], slab[rows, :], 1, 1).astype(BF16)
@@ -317,19 +362,22 @@
         [SMEM] + [HBM] * 10,
         [jax.ShapeDtypeStruct((length, part), BF16)],
         [VMEM],
-        [pltpu.VMEM((part, width), BF16), pltpu.VMEM((length, width), BF16), pltpu.SemaphoreType.DMA((10,))],
-        flops=2 * length * width * part,
+        [
+            pltpu.VMEM((part, width), BF16),
+            pltpu.VMEM((length, width), BF16),
+            pltpu.SemaphoreType.DMA((10,)),
+        ],
         after=after,
     )[0]
 
 
-def backward_kernel(mask, log_total, grads, blocks, out, qkv, sems):
-    copies = load_blocks(blocks, qkv, sems, 0)
+def backward_kernel(mask, log_total, grads, blocks, out, qkv, made, sems):
+    loads = load_heads(blocks, qkv, sems)
     tokens = out.shape[2]
     scale = 1.0 / math.sqrt(DH)
     bias = bias_rows(mask)
-    for copy in copies:
-        copy.wait()
+    stores = []
+    wait_all(loads)
     for h in range(4):
         here = slice(h * DH, (h + 1) * DH)
         query, key, value, grad = qkv[0, :, here], qkv[1, :, here], qkv[2, :, here], grads[:, here]
@@ -342,7 +390,9 @@
         grad_query = dot(key, grad_scores, 0, 0).astype(BF16).T
         for index, full in enumerate((grad_query, grad_key, grad_value)):
             for p in range(4):
-                out[p, index, :, here] = full[p * tokens : (p + 1) * tokens]
+                made[p, index, :, here] = full[p * tokens : (p + 1) * tokens]
+        stores += run_copies([(made.at[:, :, :, head_lanes(h)], out.at[:, :, :, head_lanes(h)])], sems, 4 + h)
+    wait_all(stores)
 
 
 def backward(mask, log_total, grads, blocks, after=()):
@@ -354,9 +404,8 @@
         (mask, log_total, grads, blocks),
         [SMEM] + [VMEM] * 2 + [HBM],
         [jax.ShapeDtypeStruct(blocks.shape, BF16)],
-        [VMEM],
-        [pltpu.VMEM((3, length, part), BF16), pltpu.SemaphoreType.DMA((4,))],
-        flops=10 * length * length * part,
+        [HBM],
+        [pltpu.VMEM((3, length, part), BF16), pltpu.VMEM(blocks.shape, BF16), pltpu.SemaphoreType.DMA((8,))],
         after=after,
     )[0]
 
@@ -396,15 +445,23 @@
 
     attended, attended_t, log_total = forward(mask, blocks)
 
-    cot_x, cot_y, direct, part, attended = lax.optimization_barrier((cot_x, cot_y, direct, part, attended))
+    direct, part, attended = lax.optimization_barrier((direct, part, attended))
+    weights = (chunk, direct, swap(direct), part, swap(part))
+
+    send_x, send_y, mixed_own, x_right, y_left = mixed_parts(place, weights, attended)
+    got_x, got_y = plane(send_x, 1), plane(send_y, 2)
+    cot_x, cot_y, attended_t = lax.optimization_barrier((cot_x, cot_y, attended_t))
     half = tokens // 2
     cot_blocks = (cot, cot_x, cot_y, plane(cot_y[:half], 1), plane(cot_x[half:], 2))
-    weights = (chunk, direct, swap(direct), part, swap(part))
-
-    send_x, send_y, mixed_own, x_right, y_left = mixed_parts(place, weights, attended)
-    got_x, got_y = plane(send_x, 1), plane(send_y, 2)
-    got_left = plane((y_left.astype(F32) + got_x[1].astype(F32)).astype(BF16), 2)
-    got_right = plane((x_right.astype(F32) + got_y[1].astype(F32)).astype(BF16), 1)
+
+    keep, send = weight_parts(place, attended_t, cot_blocks, after=(send_x,))
+    grads = attended_grads(place, weights, cot_blocks, after=(keep,))
+    s0, s1, s2, s3 = add_cores(keep, swap(send), after=(grads,))
+    got = [along(s, flip).astype(F32) for flip, s in ((1, s1), (2, s2), (3, s3))]
+    summed = (s0.astype(F32) + got[0] + got[1] + got[2]).astype(BF16)
+    left, right = second_parts(x_right, y_left, got_x, got_y, after=(s1,))
+    got_left, got_right = plane(left, 2), plane(right, 1)
+    outs = columns(backward(mask, log_total, grads, blocks, after=(left,)))
     mixed = jnp.concatenate(
         [
             mixed_own[:, : width // 2].astype(F32) + got_x[0].astype(F32) + got_left.astype(F32),
@@ -413,11 +470,6 @@
         axis=1,
     ).astype(BF16)
 
-    keep, send = weight_parts(place, attended_t, cot_blocks, after=(send_x,))
-    grads = attended_grads(place, weights, cot_blocks, after=(keep,))
-    s0, s1, s2, s3 = add_cores(keep, swap(send), after=(grads,))
-    got = [along(s, flip).astype(F32) for flip, s in ((1, s1), (2, s2), (3, s3))]
-    summed = (s0.astype(F32) + got[0] + got[1] + got[2]).astype(BF16)
     pieces = []
     for k in range(4):
         pairs = []
@@ -427,10 +479,8 @@
                     to_core, to_column = t // 2, t ^ (2 * c) ^ k
                     pairs.append(((2 * plane_at + c) * 4 + t, (2 * plane_at + to_core) * 4 + to_column))
         pieces.append(lax.ppermute(summed, ("dp", "seq"), pairs))
-    grad_weight = weight_out(place, pieces)
-
-    outs = columns(backward(mask, log_total, grads, blocks, after=(s1,)))
-    merged = merge_heads(place, outs, after=(summed,))
+    merged = merge_heads(place, outs, after=(summed, mixed))
+    grad_weight = weight_out(place, pieces, after=(merged[0],))
     return (mixed[None],) + tuple(g[None] for g in merged) + (grad_weight,)
 
 

time: 127 us -> 115 us (0.906)
  the two profiles are of different devices: /device:TPU:0 before, /device:TPU:1 now
where the time goes in v2:
time: 115 us; the launch traced here: 114 us
  waiting for transfers between devices  43.8 us (38%)
  starting transfers between devices  33.3 us (29%)
  Pallas kernels  28.9 us (25%)
  other arithmetic  4.15 us (4%)
  local copies, waits for them, and re-layouts  3.35 us (3%)
    pallas_call x11, Pallas kernels, call(): pl.pallas_call(body, in_specs=list(in_specs) + [HBM] * extra, out_specs=l...  28.9 us
    all_to_all x2, waiting for transfers between devices, columns(): return lax.all_to_all(array, 'seq', 0, 0, tiled=True)  15.4 us
    ppermute x8, waiting for transfers between devices, plane(): return lax.ppermute(array, 'seq', [(i, i ^ flip) for i in range(4)])  12.2 us
    ppermute x4, waiting for transfers between devices, column_shards(): pieces.append(lax.ppermute(summed, ('dp', 'seq'), pairs))  10.9 us
    all_to_all x2, starting transfers between devices, columns(): return lax.all_to_all(array, 'seq', 0, 0, tiled=True)  8.73 us
    ppermute x4, starting transfers between devices, column_shards(): pieces.append(lax.ppermute(summed, ('dp', 'seq'), pairs))  8.67 us
    ppermute x8, starting transfers between devices, plane(): return lax.ppermute(array, 'seq', [(i, i ^ flip) for i in range(4)])  6.04 us
    ppermute x2, waiting for transfers between devices, in_dp(): lax.ppermute(array, 'dp', [(2 * a + c, target(a, c)) for a in range(4) fo...  4.38 us
  transfers between devices with their start and end apart: 23, of which 12 were waited for; matrix products, arithmetic and copies ran while one was open for 4% of the time, Pallas kernels for 20%

profile of v2, /device:TPU:1, one launch (start us, length us, event | category | flops | bytes accessed | tf_op | source)
XLA Modules:
  0.0 114.3 jit_solution(6517214214850112543)
XLA Ops:
  1.3 3.3 %split_heads.1.refs_3_ = bf16[4,3,128,512]{3,2,1,0:T(8,128)(2,1)} custom-call(s32[3]{0:T(128)} %pad_add_fusion.refs_0_, bf16[128,2048]{1,0:T(8,128)(2,1)} %bitcast.25, bf16[128,2048]{1,0:T(8,128)(2,1)} %bitcast.26, bf16[128,2048]{1,0:T(8,128)(2,1)} %bitcast.27), custom_call_target="tpu_custom_call" | custom-call | bytes 1024 | tf_op jit(solution)/shard_map/split_heads/pallas_call | solution.py:31
  4.7 5.0 %all-to-all-start = ((bf16[4,3,128,512]{3,2,1,0:T(8,128)(2,1)}), bf16[4,3,128,512]{3,2,1,0:T(8,128)(2,1)S(1)}, u32[]{:S(2)}, u32[]{:S(2)}) async-start(bf16[4,3,128,512]{3,2,1,0:T(8,128)(2,1)} %split_heads.1.refs_3_), calls=%async_computation | async-start | bytes 3145728 | tf_op jit(solution)/shard_map/all_to_all | solution.py:432
  11.0 2.5 %head_chunk.1 = (bf16[128,2048]{1,0:T(8,128)(2,1)}, bf16[64,2048]{1,0:T(8,128)(2,1)}) custom-call(s32[3]{0:T(128)S(1)} %copy-done.7, bf16[256,2048]{1,0:T(8,128)(2,1)S(1)} %copy-done.1, bf16[256,2048]{1,0:T(8,128)(2,1)} %collective-permute-done.refs_2_, bf16[4,3,128,512]{3,2,1,0:T(8,128)(2,1)S(1)} %copy-done), custom_call_target="tpu_custom_call" | custom-call | bytes 1024 | tf_op jit(solution)/shard_map/head_chunk/pallas_call | solution.py:31
  13.5 2.5 %collective-permute-start.1 = (bf16[128,2048]{1,0:T(8,128)(2,1)}, bf16[128,2048]{1,0:T(8,128)(2,1)S(1)}, u32[]{:S(2)}, u32[]{:S(2)}) collective-permute-start(bf16[128,2048]{1,0:T(8,128)(2,1)} %get-tuple-element.32.refs_1_), channel_id=1, source_target_pairs={{0,8},{4,20},{8,0},{12,28},{16,24},{20,4},{24,16},{28,12},{1,9},{5... | collective-permute-start | bytes 1572872 | tf_op jit(solution)/shard_map/ppermute | solution.py:440
  18.7 10.0 %all-to-all-done.refs_1_.refs_3_ = bf16[4,3,128,512]{3,2,1,0:T(8,128)(2,1)S(1)} async-done(((bf16[4,3,128,512]{3,2,1,0:T(8,128)(2,1)}), bf16[4,3,128,512]{3,2,1,0:T(8,128)(2,1)S(1)}, u32[]{:S(2)}, u32[]{:S(2)}) %all-to-all-start) | async-done | bytes 1572896 | tf_op jit(solution)/shard_map/all_to_all | solution.py:432
  28.8 3.2 %forward.1 = (bf16[512,512]{1,0:T(8,128)(2,1)S(1)}, bf16[512,512]{1,0:T(8,128)(2,1)S(1)}, f32[4,512]{1,0:T(4,128)S(1)}) custom-call(s32[16]{0:T(128)S(1)} %reshape.48.refs_0_, bf16[4,3,128,512]{3,2,1,0:T(8,128)(2,1)S(1)} %all-to-all-done.refs_1_.refs_3_), custom_call_target="tpu_custom_call" | custom-call | bytes 1024 | tf_op jit(solution)/shard_map/forward/pallas_call | solution.py:31
  32.0 2.9 %collective-permute-done.2.refs_4_ = bf16[64,2048]{1,0:T(8,128)(2,1)S(1)} collective-permute-done((bf16[64,2048]{1,0:T(8,128)(2,1)}, bf16[64,2048]{1,0:T(8,128)(2,1)S(1)}, u32[]{:S(2)}, u32[]{:S(2)}) %collective-permute-start.2) | collective-permute-done | bytes 262176 | tf_op jit(solution)/shard_map/ppermute | solution.py:440
  34.9 1.5 %collective-permute-done.1.refs_2_ = bf16[128,2048]{1,0:T(8,128)(2,1)S(1)} collective-permute-done((bf16[128,2048]{1,0:T(8,128)(2,1)}, bf16[128,2048]{1,0:T(8,128)(2,1)S(1)}, u32[]{:S(2)}, u32[]{:S(2)}) %collective-permute-start.1) | collective-permute-done | bytes 524320 | tf_op jit(solution)/shard_map/ppermute | solution.py:440
  36.4 3.6 %collective-permute-done.7.refs_3_.refs_7_ = bf16[128,2048]{1,0:T(8,128)(2,1)S(1)} collective-permute-done((bf16[128,2048]{1,0:T(8,128)(2,1)}, bf16[128,2048]{1,0:T(8,128)(2,1)S(1)}, u32[]{:S(2)}, u32[]{:S(2)}) %collective-permute-start.7) | collective-permute-done | bytes 524320 | tf_op jit(solution)/shard_map/ppermute | solution.py:423
  42.8 3.0 %mixed_parts.1 = (bf16[2,128,1024]{2,1,0:T(8,128)(2,1)S(1)}, bf16[2,128,1024]{2,1,0:T(8,128)(2,1)S(1)}, bf16[128,2048]{1,0:T(8,128)(2,1)S(1)}, bf16[128,1024]{1,0:T(8,128)(2,1)S(1)}, bf16[128,1024]{1,0:T(8,128)(2,1)S(1)}) custom-call(s32[3]{0:T(128)S(1)} %copy-done.7, bf16[128,2048]{1,0:T(8,128)(2,1)} %get-tuple-element.32.refs_1_, ...), custom_call_target="tpu_custom_call" | custom-call | bytes 1024 | tf_op jit(solution)/shard_map/mixed_parts/pallas_call | solution.py:31
  46.6 2.6 %collective-permute-done.10.refs_6_.refs_10_ = bf16[64,2048]{1,0:T(8,128)(2,1)S(1)} collective-permute-done((bf16[64,2048]{1,0:T(8,128)(2,1)S(1)}, bf16[64,2048]{1,0:T(8,128)(2,1)S(1)}, u32[]{:S(2)}, u32[]{:S(2)}) %collective-permute-start.10) | collective-permute-done | bytes 262176 | tf_op jit(solution)/shard_map/ppermute | solution.py:423
  50.1 3.7 %weight_parts.1 = (bf16[4,64,2048]{2,1,0:T(8,128)(2,1)S(1)}, bf16[4,64,2048]{2,1,0:T(8,128)(2,1)S(1)}) custom-call(s32[3]{0:T(128)S(1)} %copy-done.7, bf16[512,512]{1,0:T(8,128)(2,1)S(1)} %get-tuple-element.44.refs_1_, bf16[128,2048]{1,0:T(8,128)(2,1)} %bitcast.7.refs_2_.refs_6_, bf16[128,2048]{1,0:T(8,128)(2,1)S(1)} %collective-permute-done.7.refs_3_.refs_7_, ...), custom_call_target="tpu_custom_call" | custom-call | bytes 1024 | tf_op jit(solution)/shard_map/weight_parts/pallas_call | solution.py:31
  56.4 3.1 %attended_grads.1.refs_2_ = bf16[512,512]{1,0:T(8,128)(2,1)S(1)} custom-call(s32[3]{0:T(128)S(1)} %copy-done.7, bf16[128,2048]{1,0:T(8,128)(2,1)} %get-tuple-element.32.refs_1_, bf16[128,2048]{1,0:T(8,128)(2,1)S(1)} %collective-permute-done.1.refs_2_, bf16[128,2048]{1,0:T(8,128)(2,1)S(1)} %collective-permute-done.3.refs_3_, ...), custom_call_target="tpu_custom_call" | custom-call | bytes 1024 | tf_op jit(solution)/shard_map/attended_grads/pallas_call | solution.py:31
  61.3 2.3 %collective-permute-start.15 = (bf16[64,2048]{1,0:T(8,128)(2,1)S(1)}, bf16[64,2048]{1,0:T(8,128)(2,1)}, u32[]{:S(2)}, u32[]{:S(2)}) collective-permute-start(bf16[64,2048]{1,0:T(8,128)(2,1)S(1)} %get-tuple-element.54), channel_id=1, source_target_pairs={{0,16},{4,20},{8,24},{12,28},{16,0},{20,4},{24,8},{28,12},{1,17},{... | collective-permute-start | bytes 786440 | tf_op jit(solution)/shard_map/ppermute | solution.py:429
  63.6 5.0 %collective-permute-done.5.refs_2_ = bf16[2,128,1024]{2,1,0:T(8,128)(2,1)S(1)} collective-permute-done((bf16[2,128,1024]{2,1,0:T(8,128)(2,1)S(1)}, bf16[2,128,1024]{2,1,0:T(8,128)(2,1)S(1)}, u32[]{:S(2)}, u32[]{:S(2)}) %collective-permute-start.5) | collective-permute-done | bytes 524320 | tf_op jit(solution)/shard_map/ppermute | solution.py:423
  71.1 4.8 %backward.1 = bf16[4,3,128,512]{3,2,1,0:T(8,128)(2,1)} custom-call(s32[16]{0:T(128)S(1)} %reshape.48.refs_0_, f32[4,512]{1,0:T(4,128)S(1)} %get-tuple-element.52.refs_1_, bf16[512,512]{1,0:T(8,128)(2,1)S(1)} %attended_grads.1.refs_2_, bf16[4,3,128,512]{3,2,1,0:T(8,128)(2,1)S(1)} %all-to-all-done.refs_1_.refs_3_, bf16[128,1024]{1,0:T(8,128)(2,1)S(1)} %get-tuple-element.50.refs_4_), custom_call_target="tpu_custom_call" | custom-call | bytes 1024 | tf_op jit(solution)/shard_map/backward/pallas_call | solution.py:31
  75.9 3.7 %all-to-all-start.1 = ((bf16[4,3,128,512]{3,2,1,0:T(8,128)(2,1)}), bf16[4,3,128,512]{3,2,1,0:T(8,128)(2,1)S(1)}, u32[]{:S(2)}, u32[]{:S(2)}) async-start(bf16[4,3,128,512]{3,2,1,0:T(8,128)(2,1)} %backward.1), calls=%async_computation.1 | async-start | bytes 3145728 | tf_op jit(solution)/shard_map/all_to_all | solution.py:432
  81.9 5.2 %collective-permute-start.17 = (bf16[64,2048]{1,0:T(8,128)(2,1)S(1)}, bf16[64,2048]{1,0:T(8,128)(2,1)S(1)}, u32[]{:S(2)}, u32[]{:S(2)}) collective-permute-start(bf16[64,2048]{1,0:T(8,128)(2,1)S(1)} %add_convert_fusion.refs_2_), channel_id=1, source_target_pairs={{0,0},{1,1},{2,6},{3,7},{4,2},{5,3},{6,4},{7,5},{8,8},{9,9},{10,14... | collective-permute-start | bytes 786440 | tf_op jit(solution)/shard_map/ppermute | solution.py:481
  88.0 1.9 %collective-permute-start.19 = (bf16[64,2048]{1,0:T(8,128)(2,1)S(1)}, bf16[64,2048]{1,0:T(8,128)(2,1)S(1)}, u32[]{:S(2)}, u32[]{:S(2)}) collective-permute-start(bf16[64,2048]{1,0:T(8,128)(2,1)S(1)} %add_convert_fusion.refs_2_), channel_id=1, source_target_pairs={{0,2},{1,3},{2,4},{3,5},{4,0},{5,1},{6,6},{7,7},{8,10},{9,11},{10,... | collective-permute-start | bytes 786440 | tf_op jit(solution)/shard_map/ppermute | solution.py:481
  92.9 5.4 %all-to-all-done.1.refs_1_ = bf16[4,3,128,512]{3,2,1,0:T(8,128)(2,1)S(1)} async-done(((bf16[4,3,128,512]{3,2,1,0:T(8,128)(2,1)}), bf16[4,3,128,512]{3,2,1,0:T(8,128)(2,1)S(1)}, u32[]{:S(2)}, u32[]{:S(2)}) %all-to-all-start.1) | async-done | bytes 1572896 | tf_op jit(solution)/shard_map/all_to_all | solution.py:432
  98.3 2.1 %merge_heads.1 = (bf16[128,2048]{1,0:T(8,128)(2,1)}, bf16[128,2048]{1,0:T(8,128)(2,1)}, bf16[128,2048]{1,0:T(8,128)(2,1)}) custom-call(s32[3]{0:T(128)S(1)} %copy-done.7, bf16[4,3,128,512]{3,2,1,0:T(8,128)(2,1)S(1)} %all-to-all-done.1.refs_1_, bf16[64,2048]{1,0:T(8,128)(2,1)S(1)} %add_convert_fusion.refs_2_, bf16[128,2048]{1,0:T(8,128)(2,1)S(1)} %pad_maximum_fusion.1.refs_3_), custom_call_target="tpu_custom_call" | custom-call | bytes 1024 | tf_op jit(solution)/shard_map/merge_heads/pallas_call | solution.py:31
  100.4 6.3 %collective-permute-done.17.refs_1_ = bf16[64,2048]{1,0:T(8,128)(2,1)S(1)} collective-permute-done((bf16[64,2048]{1,0:T(8,128)(2,1)S(1)}, bf16[64,2048]{1,0:T(8,128)(2,1)S(1)}, u32[]{:S(2)}, u32[]{:S(2)}) %collective-permute-start.17) | collective-permute-done | bytes 262176 | tf_op jit(solution)/shard_map/ppermute | solution.py:481
  107.8 3.5 %collective-permute-done.20.refs_4_ = bf16[64,2048]{1,0:T(8,128)(2,1)S(1)} collective-permute-done((bf16[64,2048]{1,0:T(8,128)(2,1)S(1)}, bf16[64,2048]{1,0:T(8,128)(2,1)S(1)}, u32[]{:S(2)}, u32[]{:S(2)}) %collective-permute-start.20) | collective-permute-done | bytes 262176 | tf_op jit(solution)/shard_map/ppermute | solution.py:481
  112.3 2.0 %weight_out.1 = f32[256,2048]{1,0:T(8,128)} custom-call(s32[3]{0:T(128)S(1)} %copy-done.7, bf16[64,2048]{1,0:T(8,128)(2,1)S(1)} %collective-permute-done.17.refs_1_, bf16[64,2048]{1,0:T(8,128)(2,1)S(1)} %collective-permute-done.18.refs_2_, bf16[64,2048]{1,0:T(8,128)(2,1)S(1)} %collective-permute-done.19.refs_3_, ...), custom_call_target="tpu_custom_call" | custom-call | bytes 1024 | tf_op jit(solution)/shard_map/weight_out/pallas_call | solution.py:31
  (59 shorter events, 24.3 us)
Async XLA Ops:
  0.6 9.1 %collective-permute-start = (bf16[256,2048]{1,0:T(8,128)(2,1)}, bf16[256,2048]{1,0:T(8,128)(2,1)}, u32[]{:S(2)}, u32[]{:S(2)}) collective-permute-start(bf16[256,2048]{1,0:T(8,128)(2,1)} %refs_1_.1), channel_id=1, source_target_pairs={{0,4},{4,0},{8,12},{12,8},{16,20},{20,16},{24,28},{28,24},{1,5},{5... | collective-permute-start | bytes 3145736 | tf_op jit(solution)/shard_map/ppermute | solution.py:426
  4.7 24.1 %all-to-all-start = ((bf16[4,3,128,512]{3,2,1,0:T(8,128)(2,1)}), bf16[4,3,128,512]{3,2,1,0:T(8,128)(2,1)S(1)}, u32[]{:S(2)}, u32[]{:S(2)}) async-start(bf16[4,3,128,512]{3,2,1,0:T(8,128)(2,1)} %split_heads.1.refs_3_), calls=%async_computation | async-start | bytes 3145728 | tf_op jit(solution)/shard_map/all_to_all | solution.py:432
  13.5 22.9 %collective-permute-start.1 = (bf16[128,2048]{1,0:T(8,128)(2,1)}, bf16[128,2048]{1,0:T(8,128)(2,1)S(1)}, u32[]{:S(2)}, u32[]{:S(2)}) collective-permute-start(bf16[128,2048]{1,0:T(8,128)(2,1)} %get-tuple-element.32.refs_1_), channel_id=1, source_target_pairs={{0,8},{4,20},{8,0},{12,28},{16,24},{20,4},{24,16},{28,12},{1,9},{5... | collective-permute-start | bytes 1572872 | tf_op jit(solution)/shard_map/ppermute | solution.py:440
  16.0 24.0 %collective-permute-start.7 = (bf16[128,2048]{1,0:T(8,128)(2,1)}, bf16[128,2048]{1,0:T(8,128)(2,1)S(1)}, u32[]{:S(2)}, u32[]{:S(2)}) collective-permute-start(bf16[128,2048]{1,0:T(8,128)(2,1)} %bitcast.7.refs_2_.refs_6_), channel_id=1, source_target_pairs={{0,1},{1,0},{2,3},{3,2},{4,5},{5,4},{6,7},{7,6},{8,9},{9,8},{10,11... | collective-permute-start | bytes 1572872 | tf_op jit(solution)/shard_map/ppermute | solution.py:423
  17.4 22.6 %collective-permute-start.8 = (bf16[128,2048]{1,0:T(8,128)(2,1)}, bf16[128,2048]{1,0:T(8,128)(2,1)S(1)}, u32[]{:S(2)}, u32[]{:S(2)}) collective-permute-start(bf16[128,2048]{1,0:T(8,128)(2,1)} %bitcast.7.refs_2_.refs_6_), channel_id=1, source_target_pairs={{0,2},{1,3},{2,0},{3,1},{4,6},{5,7},{6,4},{7,5},{8,10},{9,11},{10,... | collective-permute-start | bytes 1572872 | tf_op jit(solution)/shard_map/ppermute | solution.py:423
  17.6 17.3 %collective-permute-start.2 = (bf16[64,2048]{1,0:T(8,128)(2,1)}, bf16[64,2048]{1,0:T(8,128)(2,1)S(1)}, u32[]{:S(2)}, u32[]{:S(2)}) collective-permute-start(bf16[64,2048]{1,0:T(8,128)(2,1)} %get-tuple-element.33), channel_id=1, source_target_pairs={{0,24},{4,28},{8,16},{12,20},{16,8},{20,12},{24,0},{28,4},{1,25},{... | collective-permute-start | bytes 786440 | tf_op jit(solution)/shard_map/ppermute | solution.py:440
  36.4 6.4 %collective-permute-start.3 = (bf16[128,2048]{1,0:T(8,128)(2,1)S(1)}, bf16[128,2048]{1,0:T(8,128)(2,1)S(1)}, u32[]{:S(2)}, u32[]{:S(2)}) collective-permute-start(bf16[128,2048]{1,0:T(8,128)(2,1)S(1)} %collective-permute-done.1.refs_2_), channel_id=1, source_target_pairs={{0,4},{4,0},{8,12},{12,8},{16,20},{20,16},{24,28},{28,24},{1,5},{5... | collective-permute-start | bytes 1572872 | tf_op jit(solution)/shard_map/ppermute | solution.py:426
  40.0 2.8 %collective-permute-start.4 = (bf16[64,2048]{1,0:T(8,128)(2,1)S(1)}, bf16[64,2048]{1,0:T(8,128)(2,1)S(1)}, u32[]{:S(2)}, u32[]{:S(2)}) collective-permute-start(bf16[64,2048]{1,0:T(8,128)(2,1)S(1)} %collective-permute-done.2.refs_4_), channel_id=1, source_target_pairs={{0,4},{4,0},{8,12},{12,8},{16,20},{20,16},{24,28},{28,24},{1,5},{5... | collective-permute-start | bytes 786440 | tf_op jit(solution)/shard_map/ppermute | solution.py:426
  41.2 8.0 %collective-permute-start.10 = (bf16[64,2048]{1,0:T(8,128)(2,1)S(1)}, bf16[64,2048]{1,0:T(8,128)(2,1)S(1)}, u32[]{:S(2)}, u32[]{:S(2)}) collective-permute-start(bf16[64,2048]{1,0:T(8,128)(2,1)S(1)} %slice.21), channel_id=1, source_target_pairs={{0,2},{1,3},{2,0},{3,1},{4,6},{5,7},{6,4},{7,5},{8,10},{9,11},{10,... | collective-permute-start | bytes 786440 | tf_op jit(solution)/shard_map/ppermute | solution.py:423
  42.5 7.7 %collective-permute-start.9 = (bf16[64,2048]{1,0:T(8,128)(2,1)S(1)}, bf16[64,2048]{1,0:T(8,128)(2,1)S(1)}, u32[]{:S(2)}, u32[]{:S(2)}) collective-permute-start(bf16[64,2048]{1,0:T(8,128)(2,1)S(1)} %slice.20), channel_id=1, source_target_pairs={{0,1},{1,0},{2,3},{3,2},{4,5},{5,4},{6,7},{7,6},{8,9},{9,8},{10,11... | collective-permute-start | bytes 786440 | tf_op jit(solution)/shard_map/ppermute | solution.py:423
  53.8 5.8 %collective-permute-start.11 = (bf16[4,64,2048]{2,1,0:T(8,128)(2,1)S(1)}, bf16[4,64,2048]{2,1,0:T(8,128)(2,1)S(1)}, u32[]{:S(2)}, u32[]{:S(2)}) collective-permute-start(bf16[4,64,2048]{2,1,0:T(8,128)(2,1)S(1)} %get-tuple-element.48), channel_id=1, source_target_pairs={{0,4},{4,0},{8,12},{12,8},{16,20},{20,16},{24,28},{28,24},{1,5},{5... | collective-permute-start | bytes 3145736 | tf_op jit(solution)/shard_map/ppermute | solution.py:426
  55.0 13.6 %collective-permute-start.5 = (bf16[2,128,1024]{2,1,0:T(8,128)(2,1)S(1)}, bf16[2,128,1024]{2,1,0:T(8,128)(2,1)S(1)}, u32[]{:S(2)}, u32[]{:S(2)}) collective-permute-start(bf16[2,128,1024]{2,1,0:T(8,128)(2,1)S(1)} %get-tuple-element.39.refs_7_), channel_id=1, source_target_pairs={{0,1},{1,0},{2,3},{3,2},{4,5},{5,4},{6,7},{7,6},{8,9},{9,8},{10,11... | collective-permute-start | bytes 1572872 | tf_op jit(solution)/shard_map/ppermute | solution.py:423
  55.3 13.3 %collective-permute-start.6 = (bf16[2,128,1024]{2,1,0:T(8,128)(2,1)S(1)}, bf16[2,128,1024]{2,1,0:T(8,128)(2,1)S(1)}, u32[]{:S(2)}, u32[]{:S(2)}) collective-permute-start(bf16[2,128,1024]{2,1,0:T(8,128)(2,1)S(1)} %get-tuple-element.42), channel_id=1, source_target_pairs={{0,2},{1,3},{2,0},{3,1},{4,6},{5,7},{6,4},{7,5},{8,10},{9,11},{10,... | collective-permute-start | bytes 1572872 | tf_op jit(solution)/shard_map/ppermute | solution.py:423
  59.8 19.8 %collective-permute-start.14 = (bf16[64,2048]{1,0:T(8,128)(2,1)S(1)}, bf16[64,2048]{1,0:T(8,128)(2,1)}, u32[]{:S(2)}, u32[]{:S(2)}) collective-permute-start(bf16[64,2048]{1,0:T(8,128)(2,1)S(1)} %get-tuple-element.49.refs_4_), channel_id=1, source_target_pairs={{0,8},{4,12},{8,0},{12,4},{16,24},{20,28},{24,16},{28,20},{1,9},{5... | collective-permute-start | bytes 786440 | tf_op jit(solution)/shard_map/ppermute | solution.py:429
  61.3 18.3 %collective-permute-start.15 = (bf16[64,2048]{1,0:T(8,128)(2,1)S(1)}, bf16[64,2048]{1,0:T(8,128)(2,1)}, u32[]{:S(2)}, u32[]{:S(2)}) collective-permute-start(bf16[64,2048]{1,0:T(8,128)(2,1)S(1)} %get-tuple-element.54), channel_id=1, source_target_pairs={{0,16},{4,20},{8,24},{12,28},{16,0},{20,4},{24,8},{28,12},{1,17},{... | collective-permute-start | bytes 786440 | tf_op jit(solution)/shard_map/ppermute | solution.py:429
  63.6 17.0 %collective-permute-start.16 = (bf16[64,2048]{1,0:T(8,128)(2,1)S(1)}, bf16[64,2048]{1,0:T(8,128)(2,1)}, u32[]{:S(2)}, u32[]{:S(2)}) collective-permute-start(bf16[64,2048]{1,0:T(8,128)(2,1)S(1)} %get-tuple-element.55), channel_id=1, source_target_pairs={{0,24},{4,28},{8,16},{12,20},{16,8},{20,12},{24,0},{28,4},{1,25},{... | collective-permute-start | bytes 786440 | tf_op jit(solution)/shard_map/ppermute | solution.py:429
  69.7 20.3 %collective-permute-start.12 = (bf16[128,1024]{1,0:T(8,128)(2,1)S(1)}, bf16[128,1024]{1,0:T(8,128)(2,1)}, u32[]{:S(2)}, u32[]{:S(2)}) collective-permute-start(bf16[128,1024]{1,0:T(8,128)(2,1)S(1)} %get-tuple-element.50.refs_4_), channel_id=1, source_target_pairs={{0,2},{1,3},{2,0},{3,1},{4,6},{5,7},{6,4},{7,5},{8,10},{9,11},{10,... | collective-permute-start | bytes 786440 | tf_op jit(solution)/shard_map/ppermute | solution.py:423
  70.6 20.0 %collective-permute-start.13 = (bf16[128,1024]{1,0:T(8,128)(2,1)}, bf16[128,1024]{1,0:T(8,128)(2,1)}, u32[]{:S(2)}, u32[]{:S(2)}) collective-permute-start(bf16[128,1024]{1,0:T(8,128)(2,1)} %get-tuple-element.51), channel_id=1, source_target_pairs={{0,1},{1,0},{2,3},{3,2},{4,5},{5,4},{6,7},{7,6},{8,9},{9,8},{10,11... | collective-permute-start | bytes 786440 | tf_op jit(solution)/shard_map/ppermute | solution.py:423
  75.9 14.7 %copy-start.3 = (bf16[128,2048]{1,0:T(8,128)(2,1)S(1)}, bf16[128,2048]{1,0:T(8,128)(2,1)}, u32[]{:S(2)}) copy-start(bf16[128,2048]{1,0:T(8,128)(2,1)} %copy-done.2) | copy-start | bytes 1572868
  75.9 22.4 %all-to-all-start.1 = ((bf16[4,3,128,512]{3,2,1,0:T(8,128)(2,1)}), bf16[4,3,128,512]{3,2,1,0:T(8,128)(2,1)S(1)}, u32[]{:S(2)}, u32[]{:S(2)}) async-start(bf16[4,3,128,512]{3,2,1,0:T(8,128)(2,1)} %backward.1), calls=%async_computation.1 | async-start | bytes 3145728 | tf_op jit(solution)/shard_map/all_to_all | solution.py:432
  81.9 24.8 %collective-permute-start.17 = (bf16[64,2048]{1,0:T(8,128)(2,1)S(1)}, bf16[64,2048]{1,0:T(8,128)(2,1)S(1)}, u32[]{:S(2)}, u32[]{:S(2)}) collective-permute-start(bf16[64,2048]{1,0:T(8,128)(2,1)S(1)} %add_convert_fusion.refs_2_), channel_id=1, source_target_pairs={{0,0},{1,1},{2,6},{3,7},{4,2},{5,3},{6,4},{7,5},{8,8},{9,9},{10,14... | collective-permute-start | bytes 786440 | tf_op jit(solution)/shard_map/ppermute | solution.py:481
  87.1 19.7 %collective-permute-start.18 = (bf16[64,2048]{1,0:T(8,128)(2,1)S(1)}, bf16[64,2048]{1,0:T(8,128)(2,1)S(1)}, u32[]{:S(2)}, u32[]{:S(2)}) collective-permute-start(bf16[64,2048]{1,0:T(8,128)(2,1)S(1)} %add_convert_fusion.refs_2_), channel_id=1, source_target_pairs={{0,1},{1,0},{2,7},{3,6},{4,3},{5,2},{6,5},{7,4},{8,9},{9,8},{10,15... | collective-permute-start | bytes 786440 | tf_op jit(solution)/shard_map/ppermute | solution.py:481
  88.0 19.8 %collective-permute-start.19 = (bf16[64,2048]{1,0:T(8,128)(2,1)S(1)}, bf16[64,2048]{1,0:T(8,128)(2,1)S(1)}, u32[]{:S(2)}, u32[]{:S(2)}) collective-permute-start(bf16[64,2048]{1,0:T(8,128)(2,1)S(1)} %add_convert_fusion.refs_2_), channel_id=1, source_target_pairs={{0,2},{1,3},{2,4},{3,5},{4,0},{5,1},{6,6},{7,7},{8,10},{9,11},{10,... | collective-permute-start | bytes 786440 | tf_op jit(solution)/shard_map/ppermute | solution.py:481
  90.0 21.3 %collective-permute-start.20 = (bf16[64,2048]{1,0:T(8,128)(2,1)S(1)}, bf16[64,2048]{1,0:T(8,128)(2,1)S(1)}, u32[]{:S(2)}, u32[]{:S(2)}) collective-permute-start(bf16[64,2048]{1,0:T(8,128)(2,1)S(1)} %add_convert_fusion.refs_2_), channel_id=1, source_target_pairs={{0,3},{1,2},{2,5},{3,4},{4,1},{5,0},{6,7},{7,6},{8,11},{9,10},{10,... | collective-permute-start | bytes 786440 | tf_op jit(solution)/shard_map/ppermute | solution.py:481
  (8 other events, 22.8 us)

commit v3 on v2

--- a/solution.py
+++ b/solution.py
@@ -13,7 +13,7 @@
 F32 = jnp.float32
 BF16 = jnp.bfloat16
 VMEM_BYTES = 20 * 1024 * 1024
-HINT = 8_000_000_000
+HINT = 0
 
 
 SMEM = pl.BlockSpec(memory_space=pltpu.SMEM)
@@ -171,6 +171,15 @@
 def scores_kq(bias, query, key):
     raw = dot(key, query, 1, 1) * (LOG2E / math.sqrt(DH))
     return jnp.concatenate([raw[r * DH : (r + 1) * DH] + bias[r] for r in range(4)], axis=0)
+
+
+def arrived_kernel(*refs):
+    refs[-1][...] = jnp.zeros_like(refs[-1])
+
+
+def arrived(arrays):
+    out = jax.ShapeDtypeStruct((8, DH), F32)
+    return call(arrived_kernel, "arrived", arrays, [HBM] * len(arrays), [out], [VMEM], hint=12_000_000_000)[0]
 
 
 def forward_kernel(mask, blocks, attended, attended_t, log_total, qkv, sems):
@@ -443,25 +452,26 @@
     direct = in_dp(chunk, lambda a, c: 2 * (a ^ (1 + c)) + c)
     part = in_dp(part, lambda a, c: 2 * (a ^ 3) + c)
 
-    attended, attended_t, log_total = forward(mask, blocks)
-
-    direct, part, attended = lax.optimization_barrier((direct, part, attended))
-    weights = (chunk, direct, swap(direct), part, swap(part))
+    half = tokens // 2
+    cot_blocks = (cot, cot_x, cot_y, plane(cot_y[:half], 1), plane(cot_x[half:], 2))
+    attended, attended_t, log_total = forward(mask, blocks, after=(arrived((cot_x, cot_y)),))
+
+    crossed, other, attended, far_y, far_x = lax.optimization_barrier((swap(direct), swap(part), attended, *cot_blocks[3:]))
+    cot_blocks = (*cot_blocks[:3], far_y, far_x)
+    weights = (chunk, direct, crossed, part, other)
 
     send_x, send_y, mixed_own, x_right, y_left = mixed_parts(place, weights, attended)
     got_x, got_y = plane(send_x, 1), plane(send_y, 2)
-    cot_x, cot_y, attended_t = lax.optimization_barrier((cot_x, cot_y, attended_t))
-    half = tokens // 2
-    cot_blocks = (cot, cot_x, cot_y, plane(cot_y[:half], 1), plane(cot_x[half:], 2))
 
     keep, send = weight_parts(place, attended_t, cot_blocks, after=(send_x,))
     grads = attended_grads(place, weights, cot_blocks, after=(keep,))
     s0, s1, s2, s3 = add_cores(keep, swap(send), after=(grads,))
     got = [along(s, flip).astype(F32) for flip, s in ((1, s1), (2, s2), (3, s3))]
     summed = (s0.astype(F32) + got[0] + got[1] + got[2]).astype(BF16)
-    left, right = second_parts(x_right, y_left, got_x, got_y, after=(s1,))
+    made = backward(mask, log_total, grads, blocks, after=(s1,))
+    outs = columns(made)
+    left, right = second_parts(x_right, y_left, got_x, got_y, after=(made,))
     got_left, got_right = plane(left, 2), plane(right, 1)
-    outs = columns(backward(mask, log_total, grads, blocks, after=(left,)))
     mixed = jnp.concatenate(
         [
             mixed_own[:, : width // 2].astype(F32) + got_x[0].astype(F32) + got_left.astype(F32),

time: 115 us -> 109 us (0.948)
  the two profiles are of different devices: /device:TPU:1 before, /device:TPU:0 now
where the time goes in v3:
time: 109 us
  starting transfers between devices  35.8 us (33%)
  waiting for transfers between devices  34.3 us (31%)
  Pallas kernels  30.5 us (28%)
  other arithmetic  3.99 us (4%)
  local copies, waits for them, and re-layouts  3.31 us (3%)
    pallas_call x12, Pallas kernels, call(): pl.pallas_call(body, in_specs=list(in_specs) + [HBM] * extra, out_specs=l...  30.5 us
    ppermute x8, starting transfers between devices, plane(): return lax.ppermute(array, 'seq', [(i, i ^ flip) for i in range(4)])  13.1 us
    ppermute x8, waiting for transfers between devices, plane(): return lax.ppermute(array, 'seq', [(i, i ^ flip) for i in range(4)])  10.5 us
    ppermute x2, waiting for transfers between devices, in_dp(): lax.ppermute(array, 'dp', [(2 * a + c, target(a, c)) for a in range(4) fo...  8.67 us
    all_to_all x2, starting transfers between devices, columns(): return lax.all_to_all(array, 'seq', 0, 0, tiled=True)  7.27 us
    ppermute x4, starting transfers between devices, column_shards(): pieces.append(lax.ppermute(summed, ('dp', 'seq'), pairs))  5.57 us
    all_to_all x2, waiting for transfers between devices, columns(): return lax.all_to_all(array, 'seq', 0, 0, tiled=True)  5.31 us
    ppermute x4, waiting for transfers between devices, column_shards(): pieces.append(lax.ppermute(summed, ('dp', 'seq'), pairs))  5.06 us
  transfers between devices with their start and end apart: 23, of which 8 were waited for; matrix products, arithmetic and copies ran while one was open for 5% of the time, Pallas kernels for 19%

profile of v3, /device:TPU:0, one launch (start us, length us, event | category | flops | bytes accessed | tf_op | source)
XLA Modules:
  0.0 108.8 jit_solution(15071693151553989624)
XLA Ops:
  1.1 2.6 %collective-permute-start.6 = (bf16[128,2048]{1,0:T(8,128)(2,1)}, bf16[128,2048]{1,0:T(8,128)(2,1)S(1)}, u32[]{:S(2)}, u32[]{:S(2)}) collective-permute-start(bf16[128,2048]{1,0:T(8,128)(2,1)} %bitcast.22), channel_id=1, source_target_pairs={{0,2},{1,3},{2,0},{3,1},{4,6},{5,7},{6,4},{7,5},{8,10},{9,11},{10,... | collective-permute-start | bytes 1572872 | tf_op jit(solution)/shard_map/ppermute | solution.py:432
  5.8 3.5 %split_heads.1.refs_3_ = bf16[4,3,128,512]{3,2,1,0:T(8,128)(2,1)} custom-call(s32[3]{0:T(128)} %pad_add_fusion.refs_0_, bf16[128,2048]{1,0:T(8,128)(2,1)} %bitcast.29, bf16[128,2048]{1,0:T(8,128)(2,1)} %bitcast.30, bf16[128,2048]{1,0:T(8,128)(2,1)} %bitcast.31), custom_call_target="tpu_custom_call" | custom-call | bytes 1024 | tf_op jit(solution)/shard_map/split_heads/pallas_call | solution.py:31
  10.7 1.6 %collective-permute-start.1 = (bf16[128,2048]{1,0:T(8,128)(2,1)S(1)}, bf16[128,2048]{1,0:T(8,128)(2,1)}, u32[]{:S(2)}, u32[]{:S(2)}) collective-permute-start(bf16[128,2048]{1,0:T(8,128)(2,1)S(1)} %get-tuple-element.31.refs_1_), channel_id=1, source_target_pairs={{0,8},{4,20},{8,0},{12,28},{16,24},{20,4},{24,16},{28,12},{1,9},{5... | collective-permute-start | bytes 1572872 | tf_op jit(solution)/shard_map/ppermute | solution.py:449
  12.3 2.5 %collective-permute-start.3 = (bf16[64,2048]{1,0:T(8,128)(2,1)}, bf16[64,2048]{1,0:T(8,128)(2,1)S(1)}, u32[]{:S(2)}, u32[]{:S(2)}) collective-permute-start(bf16[64,2048]{1,0:T(8,128)(2,1)} %get-tuple-element.32), channel_id=1, source_target_pairs={{0,24},{4,28},{8,16},{12,20},{16,8},{20,12},{24,0},{28,4},{1,25},{... | collective-permute-start | bytes 786440 | tf_op jit(solution)/shard_map/ppermute | solution.py:449
  14.8 3.6 %all-to-all-start = ((bf16[4,3,128,512]{3,2,1,0:T(8,128)(2,1)}), bf16[4,3,128,512]{3,2,1,0:T(8,128)(2,1)S(1)}, u32[]{:S(2)}, u32[]{:S(2)}) async-start(bf16[4,3,128,512]{3,2,1,0:T(8,128)(2,1)} %split_heads.1.refs_3_), calls=%async_computation | async-start | bytes 3145728 | tf_op jit(solution)/shard_map/all_to_all | solution.py:441
  19.2 2.0 %collective-permute-start.7 = (bf16[64,2048]{1,0:T(8,128)(2,1)}, bf16[64,2048]{1,0:T(8,128)(2,1)}, u32[]{:S(2)}, u32[]{:S(2)}) collective-permute-start(bf16[64,2048]{1,0:T(8,128)(2,1)} %slice.24), channel_id=1, source_target_pairs={{0,1},{1,0},{2,3},{3,2},{4,5},{5,4},{6,7},{7,6},{8,9},{9,8},{10,11... | collective-permute-start | bytes 786440 | tf_op jit(solution)/shard_map/ppermute | solution.py:432
  23.3 8.7 %collective-permute-done.3.refs_4_ = bf16[64,2048]{1,0:T(8,128)(2,1)S(1)} collective-permute-done((bf16[64,2048]{1,0:T(8,128)(2,1)}, bf16[64,2048]{1,0:T(8,128)(2,1)S(1)}, u32[]{:S(2)}, u32[]{:S(2)}) %collective-permute-start.3) | collective-permute-done | bytes 262176 | tf_op jit(solution)/shard_map/ppermute | solution.py:449
  32.0 1.7 %collective-permute-start.2 = (bf16[128,2048]{1,0:T(8,128)(2,1)}, bf16[128,2048]{1,0:T(8,128)(2,1)}, u32[]{:S(2)}, u32[]{:S(2)}) collective-permute-start(bf16[128,2048]{1,0:T(8,128)(2,1)} %collective-permute-done.1.refs_2_), channel_id=1, source_target_pairs={{0,4},{4,0},{8,12},{12,8},{16,20},{20,16},{24,28},{28,24},{1,5},{5... | collective-permute-start | bytes 1572872 | tf_op jit(solution)/shard_map/ppermute | solution.py:435
  33.7 5.3 %all-to-all-done.refs_1_.refs_3_ = bf16[4,3,128,512]{3,2,1,0:T(8,128)(2,1)S(1)} async-done(((bf16[4,3,128,512]{3,2,1,0:T(8,128)(2,1)}), bf16[4,3,128,512]{3,2,1,0:T(8,128)(2,1)S(1)}, u32[]{:S(2)}, u32[]{:S(2)}) %all-to-all-start) | async-done | bytes 1572896 | tf_op jit(solution)/shard_map/all_to_all | solution.py:441
  39.0 3.2 %forward.1 = (bf16[512,512]{1,0:T(8,128)(2,1)S(1)}, bf16[512,512]{1,0:T(8,128)(2,1)S(1)}, f32[4,512]{1,0:T(4,128)S(1)}) custom-call(s32[16]{0:T(128)S(1)} %reshape.48.refs_0_, bf16[4,3,128,512]{3,2,1,0:T(8,128)(2,1)S(1)} %all-to-all-done.refs_1_.refs_3_, f32[8,128]{1,0:T(8,128)S(1)} %arrived.1.refs_2_), custom_call_target="tpu_custom_call" | custom-call | bytes 1024 | tf_op jit(solution)/shard_map/forward/pallas_call | solution.py:31
  43.0 4.0 %mixed_parts.1 = (bf16[2,128,1024]{2,1,0:T(8,128)(2,1)}, bf16[2,128,1024]{2,1,0:T(8,128)(2,1)}, bf16[128,2048]{1,0:T(8,128)(2,1)S(1)}, bf16[128,1024]{1,0:T(8,128)(2,1)S(1)}, bf16[128,1024]{1,0:T(8,128)(2,1)S(1)}) custom-call(s32[3]{0:T(128)S(1)} %copy-done.9, bf16[128,2048]{1,0:T(8,128)(2,1)S(1)} %get-tuple-element.31.refs_1_, ...), custom_call_target="tpu_custom_call" | custom-call | bytes 1024 | tf_op jit(solution)/shard_map/mixed_parts/pallas_call | solution.py:31
  47.8 3.8 %weight_parts.1 = (bf16[4,64,2048]{2,1,0:T(8,128)(2,1)S(1)}, bf16[4,64,2048]{2,1,0:T(8,128)(2,1)S(1)}) custom-call(s32[3]{0:T(128)S(1)} %copy-done.9, bf16[512,512]{1,0:T(8,128)(2,1)S(1)} %get-tuple-element.45.refs_1_, bf16[128,2048]{1,0:T(8,128)(2,1)S(1)} %bitcast.24, bf16[128,2048]{1,0:T(8,128)(2,1)S(1)} %collective-permute-done.5.refs_0_.refs_3_.refs_7_, ...), custom_call_target="tpu_custom_call" | custom-call | bytes 1024 | tf_op jit(solution)/shard_map/weight_parts/pallas_call | solution.py:31
  51.7 1.5 %collective-permute-start.10 = (bf16[2,128,1024]{2,1,0:T(8,128)(2,1)}, bf16[2,128,1024]{2,1,0:T(8,128)(2,1)}, u32[]{:S(2)}, u32[]{:S(2)}) collective-permute-start(bf16[2,128,1024]{2,1,0:T(8,128)(2,1)} %get-tuple-element.41), channel_id=1, source_target_pairs={{0,2},{1,3},{2,0},{3,1},{4,6},{5,7},{6,4},{7,5},{8,10},{9,11},{10,... | collective-permute-start | bytes 1572872 | tf_op jit(solution)/shard_map/ppermute | solution.py:432
  53.8 3.4 %attended_grads.1.refs_2_ = bf16[512,512]{1,0:T(8,128)(2,1)S(1)} custom-call(s32[3]{0:T(128)S(1)} %copy-done.9, bf16[128,2048]{1,0:T(8,128)(2,1)S(1)} %get-tuple-element.31.refs_1_, bf16[128,2048]{1,0:T(8,128)(2,1)} %collective-permute-done.1.refs_2_, bf16[128,2048]{1,0:T(8,128)(2,1)} %collective-permute-done.2.refs_3_, ...), custom_call_target="tpu_custom_call" | custom-call | bytes 1024 | tf_op jit(solution)/shard_map/attended_grads/pallas_call | solution.py:31
  58.1 1.7 %collective-permute-start.15 = (bf16[64,2048]{1,0:T(8,128)(2,1)}, bf16[64,2048]{1,0:T(8,128)(2,1)}, u32[]{:S(2)}, u32[]{:S(2)}) collective-permute-start(bf16[64,2048]{1,0:T(8,128)(2,1)} %get-tuple-element.52), channel_id=1, source_target_pairs={{0,16},{4,20},{8,24},{12,28},{16,0},{20,4},{24,8},{28,12},{1,17},{... | collective-permute-start | bytes 786440 | tf_op jit(solution)/shard_map/ppermute | solution.py:438
  61.6 4.8 %backward.1.refs_4_ = bf16[4,3,128,512]{3,2,1,0:T(8,128)(2,1)} custom-call(s32[16]{0:T(128)S(1)} %reshape.48.refs_0_, f32[4,512]{1,0:T(4,128)S(1)} %get-tuple-element.42.refs_1_, bf16[512,512]{1,0:T(8,128)(2,1)S(1)} %attended_grads.1.refs_2_, bf16[4,3,128,512]{3,2,1,0:T(8,128)(2,1)S(1)} %all-to-all-done.refs_1_.refs_3_, ...), custom_call_target="tpu_custom_call" | custom-call | bytes 1024 | tf_op jit(solution)/shard_map/backward/pallas_call | solution.py:31
  66.4 3.7 %all-to-all-start.1 = ((bf16[4,3,128,512]{3,2,1,0:T(8,128)(2,1)}), bf16[4,3,128,512]{3,2,1,0:T(8,128)(2,1)S(1)}, u32[]{:S(2)}, u32[]{:S(2)}) async-start(bf16[4,3,128,512]{3,2,1,0:T(8,128)(2,1)} %backward.1.refs_4_), calls=%async_computation.1 | async-start | bytes 3145728 | tf_op jit(solution)/shard_map/all_to_all | solution.py:441
  71.6 2.0 %collective-permute-start.12 = (bf16[128,1024]{1,0:T(8,128)(2,1)S(1)}, bf16[128,1024]{1,0:T(8,128)(2,1)S(1)}, u32[]{:S(2)}, u32[]{:S(2)}) collective-permute-start(bf16[128,1024]{1,0:T(8,128)(2,1)S(1)} %get-tuple-element.49), channel_id=1, source_target_pairs={{0,2},{1,3},{2,0},{3,1},{4,6},{5,7},{6,4},{7,5},{8,10},{9,11},{10,... | collective-permute-start | bytes 786440 | tf_op jit(solution)/shard_map/ppermute | solution.py:432
  75.1 3.7 %collective-permute-done.15 = bf16[64,2048]{1,0:T(8,128)(2,1)} collective-permute-done((bf16[64,2048]{1,0:T(8,128)(2,1)}, bf16[64,2048]{1,0:T(8,128)(2,1)}, u32[]{:S(2)}, u32[]{:S(2)}) %collective-permute-start.15) | collective-permute-done | bytes 262176 | tf_op jit(solution)/shard_map/ppermute | solution.py:438
  82.5 1.9 %collective-permute-start.19 = (bf16[64,2048]{1,0:T(8,128)(2,1)S(1)}, bf16[64,2048]{1,0:T(8,128)(2,1)S(1)}, u32[]{:S(2)}, u32[]{:S(2)}) collective-permute-start(bf16[64,2048]{1,0:T(8,128)(2,1)S(1)} %add_convert_fusion.refs_2_), channel_id=1, source_target_pairs={{0,2},{1,3},{2,4},{3,5},{4,0},{5,1},{6,6},{7,7},{8,10},{9,11},{10,... | collective-permute-start | bytes 786440 | tf_op jit(solution)/shard_map/ppermute | solution.py:491
  85.9 8.5 %collective-permute-done.12 = bf16[128,1024]{1,0:T(8,128)(2,1)S(1)} collective-permute-done((bf16[128,1024]{1,0:T(8,128)(2,1)S(1)}, bf16[128,1024]{1,0:T(8,128)(2,1)S(1)}, u32[]{:S(2)}, u32[]{:S(2)}) %collective-permute-start.12) | collective-permute-done | bytes 262176 | tf_op jit(solution)/shard_map/ppermute | solution.py:432
  98.6 2.1 %merge_heads.1 = (bf16[128,2048]{1,0:T(8,128)(2,1)}, bf16[128,2048]{1,0:T(8,128)(2,1)}, bf16[128,2048]{1,0:T(8,128)(2,1)}) custom-call(s32[3]{0:T(128)S(1)} %copy-done.9, bf16[4,3,128,512]{3,2,1,0:T(8,128)(2,1)S(1)} %all-to-all-done.1.refs_1_, bf16[64,2048]{1,0:T(8,128)(2,1)S(1)} %add_convert_fusion.refs_2_, bf16[128,2048]{1,0:T(8,128)(2,1)S(1)} %pad_maximum_fusion.1.refs_3_), custom_call_target="tpu_custom_call" | custom-call | bytes 1024 | tf_op jit(solution)/shard_map/merge_heads/pallas_call | solution.py:31
  100.7 5.0 %collective-permute-done.18.refs_2_ = bf16[64,2048]{1,0:T(8,128)(2,1)S(1)} collective-permute-done((bf16[64,2048]{1,0:T(8,128)(2,1)S(1)}, bf16[64,2048]{1,0:T(8,128)(2,1)S(1)}, u32[]{:S(2)}, u32[]{:S(2)}) %collective-permute-start.18) | collective-permute-done | bytes 262176 | tf_op jit(solution)/shard_map/ppermute | solution.py:491
  106.8 2.0 %weight_out.1 = f32[256,2048]{1,0:T(8,128)} custom-call(s32[3]{0:T(128)S(1)} %copy-done.9, bf16[64,2048]{1,0:T(8,128)(2,1)S(1)} %collective-permute-done.17.refs_1_, bf16[64,2048]{1,0:T(8,128)(2,1)S(1)} %collective-permute-done.18.refs_2_, bf16[64,2048]{1,0:T(8,128)(2,1)S(1)} %collective-permute-done.19.refs_3_, ...), custom_call_target="tpu_custom_call" | custom-call | bytes 1024 | tf_op jit(solution)/shard_map/weight_out/pallas_call | solution.py:31
  (64 shorter events, 25.0 us)
Async XLA Ops:
  0.6 8.7 %collective-permute-start = (bf16[256,2048]{1,0:T(8,128)(2,1)}, bf16[256,2048]{1,0:T(8,128)(2,1)S(1)}, u32[]{:S(2)}, u32[]{:S(2)}) collective-permute-start(bf16[256,2048]{1,0:T(8,128)(2,1)} %refs_1_.1), channel_id=1, source_target_pairs={{0,4},{4,0},{8,12},{12,8},{16,20},{20,16},{24,28},{28,24},{1,5},{5... | collective-permute-start | bytes 3145736 | tf_op jit(solution)/shard_map/ppermute | solution.py:435
  1.1 17.3 %collective-permute-start.6 = (bf16[128,2048]{1,0:T(8,128)(2,1)}, bf16[128,2048]{1,0:T(8,128)(2,1)S(1)}, u32[]{:S(2)}, u32[]{:S(2)}) collective-permute-start(bf16[128,2048]{1,0:T(8,128)(2,1)} %bitcast.22), channel_id=1, source_target_pairs={{0,2},{1,3},{2,0},{3,1},{4,6},{5,7},{6,4},{7,5},{8,10},{9,11},{10,... | collective-permute-start | bytes 1572872 | tf_op jit(solution)/shard_map/ppermute | solution.py:432
  3.7 17.4 %collective-permute-start.5 = (bf16[128,2048]{1,0:T(8,128)(2,1)}, bf16[128,2048]{1,0:T(8,128)(2,1)S(1)}, u32[]{:S(2)}, u32[]{:S(2)}) collective-permute-start(bf16[128,2048]{1,0:T(8,128)(2,1)} %bitcast.23), channel_id=1, source_target_pairs={{0,1},{1,0},{2,3},{3,2},{4,5},{5,4},{6,7},{7,6},{8,9},{9,8},{10,11... | collective-permute-start | bytes 1572872 | tf_op jit(solution)/shard_map/ppermute | solution.py:432
  10.7 21.4 %collective-permute-start.1 = (bf16[128,2048]{1,0:T(8,128)(2,1)S(1)}, bf16[128,2048]{1,0:T(8,128)(2,1)}, u32[]{:S(2)}, u32[]{:S(2)}) collective-permute-start(bf16[128,2048]{1,0:T(8,128)(2,1)S(1)} %get-tuple-element.31.refs_1_), channel_id=1, source_target_pairs={{0,8},{4,20},{8,0},{12,28},{16,24},{20,4},{24,16},{28,12},{1,9},{5... | collective-permute-start | bytes 1572872 | tf_op jit(solution)/shard_map/ppermute | solution.py:449
  12.3 19.7 %collective-permute-start.3 = (bf16[64,2048]{1,0:T(8,128)(2,1)}, bf16[64,2048]{1,0:T(8,128)(2,1)S(1)}, u32[]{:S(2)}, u32[]{:S(2)}) collective-permute-start(bf16[64,2048]{1,0:T(8,128)(2,1)} %get-tuple-element.32), channel_id=1, source_target_pairs={{0,24},{4,28},{8,16},{12,20},{16,8},{20,12},{24,0},{28,4},{1,25},{... | collective-permute-start | bytes 786440 | tf_op jit(solution)/shard_map/ppermute | solution.py:449
  14.8 24.2 %all-to-all-start = ((bf16[4,3,128,512]{3,2,1,0:T(8,128)(2,1)}), bf16[4,3,128,512]{3,2,1,0:T(8,128)(2,1)S(1)}, u32[]{:S(2)}, u32[]{:S(2)}) async-start(bf16[4,3,128,512]{3,2,1,0:T(8,128)(2,1)} %split_heads.1.refs_3_), calls=%async_computation | async-start | bytes 3145728 | tf_op jit(solution)/shard_map/all_to_all | solution.py:441
  19.2 23.8 %collective-permute-start.7 = (bf16[64,2048]{1,0:T(8,128)(2,1)}, bf16[64,2048]{1,0:T(8,128)(2,1)}, u32[]{:S(2)}, u32[]{:S(2)}) collective-permute-start(bf16[64,2048]{1,0:T(8,128)(2,1)} %slice.24), channel_id=1, source_target_pairs={{0,1},{1,0},{2,3},{3,2},{4,5},{5,4},{6,7},{7,6},{8,9},{9,8},{10,11... | collective-permute-start | bytes 786440 | tf_op jit(solution)/shard_map/ppermute | solution.py:432
  21.9 21.1 %collective-permute-start.8 = (bf16[64,2048]{1,0:T(8,128)(2,1)}, bf16[64,2048]{1,0:T(8,128)(2,1)}, u32[]{:S(2)}, u32[]{:S(2)}) collective-permute-start(bf16[64,2048]{1,0:T(8,128)(2,1)} %slice.25), channel_id=1, source_target_pairs={{0,2},{1,3},{2,0},{3,1},{4,6},{5,7},{6,4},{7,5},{8,10},{9,11},{10,... | collective-permute-start | bytes 786440 | tf_op jit(solution)/shard_map/ppermute | solution.py:432
  32.0 11.0 %collective-permute-start.4 = (bf16[64,2048]{1,0:T(8,128)(2,1)S(1)}, bf16[64,2048]{1,0:T(8,128)(2,1)}, u32[]{:S(2)}, u32[]{:S(2)}) collective-permute-start(bf16[64,2048]{1,0:T(8,128)(2,1)S(1)} %collective-permute-done.3.refs_4_), channel_id=1, source_target_pairs={{0,4},{4,0},{8,12},{12,8},{16,20},{20,16},{24,28},{28,24},{1,5},{5... | collective-permute-start | bytes 786440 | tf_op jit(solution)/shard_map/ppermute | solution.py:435
  32.0 11.0 %collective-permute-start.2 = (bf16[128,2048]{1,0:T(8,128)(2,1)}, bf16[128,2048]{1,0:T(8,128)(2,1)}, u32[]{:S(2)}, u32[]{:S(2)}) collective-permute-start(bf16[128,2048]{1,0:T(8,128)(2,1)} %collective-permute-done.1.refs_2_), channel_id=1, source_target_pairs={{0,4},{4,0},{8,12},{12,8},{16,20},{20,16},{24,28},{28,24},{1,5},{5... | collective-permute-start | bytes 1572872 | tf_op jit(solution)/shard_map/ppermute | solution.py:435
  51.6 5.6 %collective-permute-start.11 = (bf16[4,64,2048]{2,1,0:T(8,128)(2,1)S(1)}, bf16[4,64,2048]{2,1,0:T(8,128)(2,1)S(1)}, u32[]{:S(2)}, u32[]{:S(2)}) collective-permute-start(bf16[4,64,2048]{2,1,0:T(8,128)(2,1)S(1)} %get-tuple-element.47), channel_id=1, source_target_pairs={{0,4},{4,0},{8,12},{12,8},{16,20},{20,16},{24,28},{28,24},{1,5},{5... | collective-permute-start | bytes 3145736 | tf_op jit(solution)/shard_map/ppermute | solution.py:435
  51.7 18.4 %collective-permute-start.10 = (bf16[2,128,1024]{2,1,0:T(8,128)(2,1)}, bf16[2,128,1024]{2,1,0:T(8,128)(2,1)}, u32[]{:S(2)}, u32[]{:S(2)}) collective-permute-start(bf16[2,128,1024]{2,1,0:T(8,128)(2,1)} %get-tuple-element.41), channel_id=1, source_target_pairs={{0,2},{1,3},{2,0},{3,1},{4,6},{5,7},{6,4},{7,5},{8,10},{9,11},{10,... | collective-permute-start | bytes 1572872 | tf_op jit(solution)/shard_map/ppermute | solution.py:432
  53.2 16.9 %collective-permute-start.9 = (bf16[2,128,1024]{2,1,0:T(8,128)(2,1)}, bf16[2,128,1024]{2,1,0:T(8,128)(2,1)}, u32[]{:S(2)}, u32[]{:S(2)}) collective-permute-start(bf16[2,128,1024]{2,1,0:T(8,128)(2,1)} %get-tuple-element.38.refs_7_), channel_id=1, source_target_pairs={{0,1},{1,0},{2,3},{3,2},{4,5},{5,4},{6,7},{7,6},{8,9},{9,8},{10,11... | collective-permute-start | bytes 1572872 | tf_op jit(solution)/shard_map/ppermute | solution.py:432
  58.1 20.7 %collective-permute-start.15 = (bf16[64,2048]{1,0:T(8,128)(2,1)}, bf16[64,2048]{1,0:T(8,128)(2,1)}, u32[]{:S(2)}, u32[]{:S(2)}) collective-permute-start(bf16[64,2048]{1,0:T(8,128)(2,1)} %get-tuple-element.52), channel_id=1, source_target_pairs={{0,16},{4,20},{8,24},{12,28},{16,0},{20,4},{24,8},{28,12},{1,17},{... | collective-permute-start | bytes 786440 | tf_op jit(solution)/shard_map/ppermute | solution.py:438
  59.7 19.1 %collective-permute-start.16 = (bf16[64,2048]{1,0:T(8,128)(2,1)S(1)}, bf16[64,2048]{1,0:T(8,128)(2,1)}, u32[]{:S(2)}, u32[]{:S(2)}) collective-permute-start(bf16[64,2048]{1,0:T(8,128)(2,1)S(1)} %get-tuple-element.53), channel_id=1, source_target_pairs={{0,24},{4,28},{8,16},{12,20},{16,8},{20,12},{24,0},{28,4},{1,25},{... | collective-permute-start | bytes 786440 | tf_op jit(solution)/shard_map/ppermute | solution.py:438
  61.0 18.7 %collective-permute-start.14 = (bf16[64,2048]{1,0:T(8,128)(2,1)S(1)}, bf16[64,2048]{1,0:T(8,128)(2,1)}, u32[]{:S(2)}, u32[]{:S(2)}) collective-permute-start(bf16[64,2048]{1,0:T(8,128)(2,1)S(1)} %get-tuple-element.48.refs_4_), channel_id=1, source_target_pairs={{0,8},{4,12},{8,0},{12,4},{16,24},{20,28},{24,16},{28,20},{1,9},{5... | collective-permute-start | bytes 786440 | tf_op jit(solution)/shard_map/ppermute | solution.py:438
  66.4 32.2 %all-to-all-start.1 = ((bf16[4,3,128,512]{3,2,1,0:T(8,128)(2,1)}), bf16[4,3,128,512]{3,2,1,0:T(8,128)(2,1)S(1)}, u32[]{:S(2)}, u32[]{:S(2)}) async-start(bf16[4,3,128,512]{3,2,1,0:T(8,128)(2,1)} %backward.1.refs_4_), calls=%async_computation.1 | async-start | bytes 3145728 | tf_op jit(solution)/shard_map/all_to_all | solution.py:441
  70.2 26.2 %copy-start.3 = (bf16[128,2048]{1,0:T(8,128)(2,1)S(1)}, bf16[128,2048]{1,0:T(8,128)(2,1)}, u32[]{:S(2)}) copy-start(bf16[128,2048]{1,0:T(8,128)(2,1)} %copy-done.2) | copy-start | bytes 1572868
  71.6 22.8 %collective-permute-start.12 = (bf16[128,1024]{1,0:T(8,128)(2,1)S(1)}, bf16[128,1024]{1,0:T(8,128)(2,1)S(1)}, u32[]{:S(2)}, u32[]{:S(2)}) collective-permute-start(bf16[128,1024]{1,0:T(8,128)(2,1)S(1)} %get-tuple-element.49), channel_id=1, source_target_pairs={{0,2},{1,3},{2,0},{3,1},{4,6},{5,7},{6,4},{7,5},{8,10},{9,11},{10,... | collective-permute-start | bytes 786440 | tf_op jit(solution)/shard_map/ppermute | solution.py:432
  73.6 22.8 %collective-permute-start.13 = (bf16[128,1024]{1,0:T(8,128)(2,1)S(1)}, bf16[128,1024]{1,0:T(8,128)(2,1)S(1)}, u32[]{:S(2)}, u32[]{:S(2)}) collective-permute-start(bf16[128,1024]{1,0:T(8,128)(2,1)S(1)} %get-tuple-element.50), channel_id=1, source_target_pairs={{0,1},{1,0},{2,3},{3,2},{4,5},{5,4},{6,7},{7,6},{8,9},{9,8},{10,11... | collective-permute-start | bytes 786440 | tf_op jit(solution)/shard_map/ppermute | solution.py:432
  81.0 19.7 %collective-permute-start.20 = (bf16[64,2048]{1,0:T(8,128)(2,1)S(1)}, bf16[64,2048]{1,0:T(8,128)(2,1)S(1)}, u32[]{:S(2)}, u32[]{:S(2)}) collective-permute-start(bf16[64,2048]{1,0:T(8,128)(2,1)S(1)} %add_convert_fusion.refs_2_), channel_id=1, source_target_pairs={{0,3},{1,2},{2,5},{3,4},{4,1},{5,0},{6,7},{7,6},{8,11},{9,10},{10,... | collective-permute-start | bytes 786440 | tf_op jit(solution)/shard_map/ppermute | solution.py:491
  82.5 18.1 %collective-permute-start.19 = (bf16[64,2048]{1,0:T(8,128)(2,1)S(1)}, bf16[64,2048]{1,0:T(8,128)(2,1)S(1)}, u32[]{:S(2)}, u32[]{:S(2)}) collective-permute-start(bf16[64,2048]{1,0:T(8,128)(2,1)S(1)} %add_convert_fusion.refs_2_), channel_id=1, source_target_pairs={{0,2},{1,3},{2,4},{3,5},{4,0},{5,1},{6,6},{7,7},{8,10},{9,11},{10,... | collective-permute-start | bytes 786440 | tf_op jit(solution)/shard_map/ppermute | solution.py:491
  84.5 21.3 %collective-permute-start.18 = (bf16[64,2048]{1,0:T(8,128)(2,1)S(1)}, bf16[64,2048]{1,0:T(8,128)(2,1)S(1)}, u32[]{:S(2)}, u32[]{:S(2)}) collective-permute-start(bf16[64,2048]{1,0:T(8,128)(2,1)S(1)} %add_convert_fusion.refs_2_), channel_id=1, source_target_pairs={{0,1},{1,0},{2,7},{3,6},{4,3},{5,2},{6,5},{7,4},{8,9},{9,8},{10,15... | collective-permute-start | bytes 786440 | tf_op jit(solution)/shard_map/ppermute | solution.py:491
  94.4 11.3 %collective-permute-start.17 = (bf16[64,2048]{1,0:T(8,128)(2,1)S(1)}, bf16[64,2048]{1,0:T(8,128)(2,1)S(1)}, u32[]{:S(2)}, u32[]{:S(2)}) collective-permute-start(bf16[64,2048]{1,0:T(8,128)(2,1)S(1)} %add_convert_fusion.refs_2_), channel_id=1, source_target_pairs={{0,0},{1,1},{2,6},{3,7},{4,2},{5,3},{6,4},{7,5},{8,8},{9,9},{10,14... | collective-permute-start | bytes 786440 | tf_op jit(solution)/shard_map/ppermute | solution.py:491
  (10 other events, 35.5 us)

commit v4 on v3

--- a/solution.py
+++ b/solution.py
@@ -13,7 +13,7 @@
 F32 = jnp.float32
 BF16 = jnp.bfloat16
 VMEM_BYTES = 20 * 1024 * 1024
-HINT = 0
+HINT = 2_000_000_000
 
 
 SMEM = pl.BlockSpec(memory_space=pltpu.SMEM)
@@ -91,6 +91,8 @@
 
 
 def merge_kernel(place, blocks, *outs):
+    *outs, token = outs
+    token[...] = jnp.zeros_like(token)
     for column in range(4):
         for index, target in enumerate(outs):
             for h in range(4):
@@ -100,7 +102,8 @@
 def merge_heads(place, blocks, after=()):
     _, _, tokens, part = blocks.shape
     out = jax.ShapeDtypeStruct((tokens, 4 * part), BF16)
-    return call(merge_kernel, "merge_heads", (place, blocks), [SMEM, VMEM], [out] * 3, [VMEM] * 3, after=after)
+    token = jax.ShapeDtypeStruct((8, DH), F32)
+    return call(merge_kernel, "merge_heads", (place, blocks), [SMEM, VMEM], [out] * 3 + [token], [VMEM] * 4, after=after)
 
 
 def dot(a, b, a_dim, b_dim):
@@ -489,8 +492,8 @@
                     to_core, to_column = t // 2, t ^ (2 * c) ^ k
                     pairs.append(((2 * plane_at + c) * 4 + t, (2 * plane_at + to_core) * 4 + to_column))
         pieces.append(lax.ppermute(summed, ("dp", "seq"), pairs))
-    merged = merge_heads(place, outs, after=(summed, mixed))
-    grad_weight = weight_out(place, pieces, after=(merged[0],))
+    *merged, token = merge_heads(place, outs, after=(summed, mixed))
+    grad_weight = weight_out(place, pieces, after=(token,))
     return (mixed[None],) + tuple(g[None] for g in merged) + (grad_weight,)
 
 

time: 109 us -> 107 us (0.982)
  local copies, waits for them, and re-layouts: 3.31 us -> 1.58 us
    unnamed x22 -> x20, local copies, waits for them, and re-layouts: 1.78 us -> 0.05 us
where the time goes in v4:
time: 107 us
  starting transfers between devices  35.9 us (34%)
  waiting for transfers between devices  34.4 us (32%)
  Pallas kernels  29.8 us (28%)
  other arithmetic  3.91 us (4%)
  local copies, waits for them, and re-layouts  1.58 us (1%)
    pallas_call x12, Pallas kernels, call(): pl.pallas_call(body, in_specs=list(in_specs) + [HBM] * extra, out_specs=l...  29.8 us
    ppermute x8, starting transfers between devices, plane(): return lax.ppermute(array, 'seq', [(i, i ^ flip) for i in range(4)])  13.1 us
    ppermute x8, waiting for transfers between devices, plane(): return lax.ppermute(array, 'seq', [(i, i ^ flip) for i in range(4)])  10.6 us
    ppermute x2, waiting for transfers between devices, in_dp(): lax.ppermute(array, 'dp', [(2 * a + c, target(a, c)) for a in range(4) fo...  8.67 us
    all_to_all x2, starting transfers between devices, columns(): return lax.all_to_all(array, 'seq', 0, 0, tiled=True)  7.27 us
    ppermute x4, starting transfers between devices, column_shards(): pieces.append(lax.ppermute(summed, ('dp', 'seq'), pairs))  5.57 us
    all_to_all x2, waiting for transfers between devices, columns(): return lax.all_to_all(array, 'seq', 0, 0, tiled=True)  5.31 us
    ppermute x4, waiting for transfers between devices, column_shards(): pieces.append(lax.ppermute(summed, ('dp', 'seq'), pairs))  5.07 us
  transfers between devices with their start and end apart: 23, of which 8 were waited for; matrix products, arithmetic and copies ran while one was open for 5% of the time, Pallas kernels for 19%

profile of v4, /device:TPU:0, one launch (start us, length us, event | category | flops | bytes accessed | tf_op | source)
XLA Modules:
  0.0 106.5 jit_solution(2900575090728594995)
XLA Ops:
  1.1 2.6 %collective-permute-start.6 = (bf16[128,2048]{1,0:T(8,128)(2,1)}, bf16[128,2048]{1,0:T(8,128)(2,1)S(1)}, u32[]{:S(2)}, u32[]{:S(2)}) collective-permute-start(bf16[128,2048]{1,0:T(8,128)(2,1)} %bitcast.22), channel_id=1, source_target_pairs={{0,2},{1,3},{2,0},{3,1},{4,6},{5,7},{6,4},{7,5},{8,10},{9,11},{10,... | collective-permute-start | bytes 1572872 | tf_op jit(solution)/shard_map/ppermute | solution.py:435
  5.8 3.5 %split_heads.1.refs_3_ = bf16[4,3,128,512]{3,2,1,0:T(8,128)(2,1)} custom-call(s32[3]{0:T(128)} %pad_add_fusion.refs_0_, bf16[128,2048]{1,0:T(8,128)(2,1)} %bitcast.28, bf16[128,2048]{1,0:T(8,128)(2,1)} %bitcast.29, bf16[128,2048]{1,0:T(8,128)(2,1)} %bitcast.30), custom_call_target="tpu_custom_call" | custom-call | bytes 1024 | tf_op jit(solution)/shard_map/split_heads/pallas_call | solution.py:31
  10.7 1.6 %collective-permute-start.1 = (bf16[128,2048]{1,0:T(8,128)(2,1)S(1)}, bf16[128,2048]{1,0:T(8,128)(2,1)}, u32[]{:S(2)}, u32[]{:S(2)}) collective-permute-start(bf16[128,2048]{1,0:T(8,128)(2,1)S(1)} %get-tuple-element.32.refs_1_), channel_id=1, source_target_pairs={{0,8},{4,20},{8,0},{12,28},{16,24},{20,4},{24,16},{28,12},{1,9},{5... | collective-permute-start | bytes 1572872 | tf_op jit(solution)/shard_map/ppermute | solution.py:452
  12.3 2.5 %collective-permute-start.3 = (bf16[64,2048]{1,0:T(8,128)(2,1)}, bf16[64,2048]{1,0:T(8,128)(2,1)S(1)}, u32[]{:S(2)}, u32[]{:S(2)}) collective-permute-start(bf16[64,2048]{1,0:T(8,128)(2,1)} %get-tuple-element.33), channel_id=1, source_target_pairs={{0,24},{4,28},{8,16},{12,20},{16,8},{20,12},{24,0},{28,4},{1,25},{... | collective-permute-start | bytes 786440 | tf_op jit(solution)/shard_map/ppermute | solution.py:452
  14.8 3.6 %all-to-all-start = ((bf16[4,3,128,512]{3,2,1,0:T(8,128)(2,1)}), bf16[4,3,128,512]{3,2,1,0:T(8,128)(2,1)S(1)}, u32[]{:S(2)}, u32[]{:S(2)}) async-start(bf16[4,3,128,512]{3,2,1,0:T(8,128)(2,1)} %split_heads.1.refs_3_), calls=%async_computation | async-start | bytes 3145728 | tf_op jit(solution)/shard_map/all_to_all | solution.py:444
  19.2 2.0 %collective-permute-start.7 = (bf16[64,2048]{1,0:T(8,128)(2,1)}, bf16[64,2048]{1,0:T(8,128)(2,1)}, u32[]{:S(2)}, u32[]{:S(2)}) collective-permute-start(bf16[64,2048]{1,0:T(8,128)(2,1)} %slice.24), channel_id=1, source_target_pairs={{0,1},{1,0},{2,3},{3,2},{4,5},{5,4},{6,7},{7,6},{8,9},{9,8},{10,11... | collective-permute-start | bytes 786440 | tf_op jit(solution)/shard_map/ppermute | solution.py:435
  23.3 8.7 %collective-permute-done.3.refs_4_ = bf16[64,2048]{1,0:T(8,128)(2,1)S(1)} collective-permute-done((bf16[64,2048]{1,0:T(8,128)(2,1)}, bf16[64,2048]{1,0:T(8,128)(2,1)S(1)}, u32[]{:S(2)}, u32[]{:S(2)}) %collective-permute-start.3) | collective-permute-done | bytes 262176 | tf_op jit(solution)/shard_map/ppermute | solution.py:452
  32.0 1.7 %collective-permute-start.2 = (bf16[128,2048]{1,0:T(8,128)(2,1)}, bf16[128,2048]{1,0:T(8,128)(2,1)}, u32[]{:S(2)}, u32[]{:S(2)}) collective-permute-start(bf16[128,2048]{1,0:T(8,128)(2,1)} %collective-permute-done.1.refs_2_), channel_id=1, source_target_pairs={{0,4},{4,0},{8,12},{12,8},{16,20},{20,16},{24,28},{28,24},{1,5},{5... | collective-permute-start | bytes 1572872 | tf_op jit(solution)/shard_map/ppermute | solution.py:438
  33.7 5.3 %all-to-all-done.refs_1_.refs_3_ = bf16[4,3,128,512]{3,2,1,0:T(8,128)(2,1)S(1)} async-done(((bf16[4,3,128,512]{3,2,1,0:T(8,128)(2,1)}), bf16[4,3,128,512]{3,2,1,0:T(8,128)(2,1)S(1)}, u32[]{:S(2)}, u32[]{:S(2)}) %all-to-all-start) | async-done | bytes 1572896 | tf_op jit(solution)/shard_map/all_to_all | solution.py:444
  39.0 3.2 %forward.1 = (bf16[512,512]{1,0:T(8,128)(2,1)S(1)}, bf16[512,512]{1,0:T(8,128)(2,1)S(1)}, f32[4,512]{1,0:T(4,128)S(1)}) custom-call(s32[16]{0:T(128)S(1)} %reshape.48.refs_0_, bf16[4,3,128,512]{3,2,1,0:T(8,128)(2,1)S(1)} %all-to-all-done.refs_1_.refs_3_, f32[8,128]{1,0:T(8,128)S(1)} %arrived.1.refs_2_), custom_call_target="tpu_custom_call" | custom-call | bytes 1024 | tf_op jit(solution)/shard_map/forward/pallas_call | solution.py:31
  43.0 4.0 %mixed_parts.1 = (bf16[2,128,1024]{2,1,0:T(8,128)(2,1)}, bf16[2,128,1024]{2,1,0:T(8,128)(2,1)}, bf16[128,2048]{1,0:T(8,128)(2,1)S(1)}, bf16[128,1024]{1,0:T(8,128)(2,1)S(1)}, bf16[128,1024]{1,0:T(8,128)(2,1)S(1)}) custom-call(s32[3]{0:T(128)S(1)} %copy-done.4, bf16[128,2048]{1,0:T(8,128)(2,1)S(1)} %get-tuple-element.32.refs_1_, ...), custom_call_target="tpu_custom_call" | custom-call | bytes 1024 | tf_op jit(solution)/shard_map/mixed_parts/pallas_call | solution.py:31
  47.1 3.8 %weight_parts.1 = (bf16[4,64,2048]{2,1,0:T(8,128)(2,1)S(1)}, bf16[4,64,2048]{2,1,0:T(8,128)(2,1)S(1)}) custom-call(s32[3]{0:T(128)S(1)} %copy-done.4, bf16[512,512]{1,0:T(8,128)(2,1)S(1)} %get-tuple-element.46.refs_1_, bf16[128,2048]{1,0:T(8,128)(2,1)S(1)} %bitcast.24, bf16[128,2048]{1,0:T(8,128)(2,1)S(1)} %collective-permute-done.5.refs_0_.refs_3_.refs_7_, ...), custom_call_target="tpu_custom_call" | custom-call | bytes 1024 | tf_op jit(solution)/shard_map/weight_parts/pallas_call | solution.py:31
  51.0 1.5 %collective-permute-start.10 = (bf16[2,128,1024]{2,1,0:T(8,128)(2,1)}, bf16[2,128,1024]{2,1,0:T(8,128)(2,1)}, u32[]{:S(2)}, u32[]{:S(2)}) collective-permute-start(bf16[2,128,1024]{2,1,0:T(8,128)(2,1)} %get-tuple-element.42), channel_id=1, source_target_pairs={{0,2},{1,3},{2,0},{3,1},{4,6},{5,7},{6,4},{7,5},{8,10},{9,11},{10,... | collective-permute-start | bytes 1572872 | tf_op jit(solution)/shard_map/ppermute | solution.py:435
  53.1 3.4 %attended_grads.1.refs_2_ = bf16[512,512]{1,0:T(8,128)(2,1)S(1)} custom-call(s32[3]{0:T(128)S(1)} %copy-done.4, bf16[128,2048]{1,0:T(8,128)(2,1)S(1)} %get-tuple-element.32.refs_1_, bf16[128,2048]{1,0:T(8,128)(2,1)} %collective-permute-done.1.refs_2_, bf16[128,2048]{1,0:T(8,128)(2,1)} %collective-permute-done.2.refs_3_, ...), custom_call_target="tpu_custom_call" | custom-call | bytes 1024 | tf_op jit(solution)/shard_map/attended_grads/pallas_call | solution.py:31
  56.8 1.7 %collective-permute-start.15 = (bf16[64,2048]{1,0:T(8,128)(2,1)S(1)}, bf16[64,2048]{1,0:T(8,128)(2,1)S(1)}, u32[]{:S(2)}, u32[]{:S(2)}) collective-permute-start(bf16[64,2048]{1,0:T(8,128)(2,1)S(1)} %get-tuple-element.53), channel_id=1, source_target_pairs={{0,16},{4,20},{8,24},{12,28},{16,0},{20,4},{24,8},{28,12},{1,17},{... | collective-permute-start | bytes 786440 | tf_op jit(solution)/shard_map/ppermute | solution.py:441
  60.3 4.8 %backward.1.refs_4_ = bf16[4,3,128,512]{3,2,1,0:T(8,128)(2,1)} custom-call(s32[16]{0:T(128)S(1)} %reshape.48.refs_0_, f32[4,512]{1,0:T(4,128)S(1)} %get-tuple-element.43.refs_1_, bf16[512,512]{1,0:T(8,128)(2,1)S(1)} %attended_grads.1.refs_2_, bf16[4,3,128,512]{3,2,1,0:T(8,128)(2,1)S(1)} %all-to-all-done.refs_1_.refs_3_, ...), custom_call_target="tpu_custom_call" | custom-call | bytes 1024 | tf_op jit(solution)/shard_map/backward/pallas_call | solution.py:31
  65.2 3.7 %all-to-all-start.1 = ((bf16[4,3,128,512]{3,2,1,0:T(8,128)(2,1)}), bf16[4,3,128,512]{3,2,1,0:T(8,128)(2,1)S(1)}, u32[]{:S(2)}, u32[]{:S(2)}) async-start(bf16[4,3,128,512]{3,2,1,0:T(8,128)(2,1)} %backward.1.refs_4_), calls=%async_computation.1 | async-start | bytes 3145728 | tf_op jit(solution)/shard_map/all_to_all | solution.py:444
  70.3 2.0 %collective-permute-start.12 = (bf16[128,1024]{1,0:T(8,128)(2,1)S(1)}, bf16[128,1024]{1,0:T(8,128)(2,1)S(1)}, u32[]{:S(2)}, u32[]{:S(2)}) collective-permute-start(bf16[128,1024]{1,0:T(8,128)(2,1)S(1)} %get-tuple-element.50), channel_id=1, source_target_pairs={{0,2},{1,3},{2,0},{3,1},{4,6},{5,7},{6,4},{7,5},{8,10},{9,11},{10,... | collective-permute-start | bytes 786440 | tf_op jit(solution)/shard_map/ppermute | solution.py:435
  73.8 3.5 %collective-permute-done.15 = bf16[64,2048]{1,0:T(8,128)(2,1)S(1)} collective-permute-done((bf16[64,2048]{1,0:T(8,128)(2,1)S(1)}, bf16[64,2048]{1,0:T(8,128)(2,1)S(1)}, u32[]{:S(2)}, u32[]{:S(2)}) %collective-permute-start.15) | collective-permute-done | bytes 262176 | tf_op jit(solution)/shard_map/ppermute | solution.py:441
  81.2 1.9 %collective-permute-start.19 = (bf16[64,2048]{1,0:T(8,128)(2,1)S(1)}, bf16[64,2048]{1,0:T(8,128)(2,1)S(1)}, u32[]{:S(2)}, u32[]{:S(2)}) collective-permute-start(bf16[64,2048]{1,0:T(8,128)(2,1)S(1)} %add_convert_fusion.refs_2_), channel_id=1, source_target_pairs={{0,2},{1,3},{2,4},{3,5},{4,0},{5,1},{6,6},{7,7},{8,10},{9,11},{10,... | collective-permute-start | bytes 786440 | tf_op jit(solution)/shard_map/ppermute | solution.py:494
  84.6 8.6 %collective-permute-done.12 = bf16[128,1024]{1,0:T(8,128)(2,1)S(1)} collective-permute-done((bf16[128,1024]{1,0:T(8,128)(2,1)S(1)}, bf16[128,1024]{1,0:T(8,128)(2,1)S(1)}, u32[]{:S(2)}, u32[]{:S(2)}) %collective-permute-start.12) | collective-permute-done | bytes 262176 | tf_op jit(solution)/shard_map/ppermute | solution.py:435
  97.4 2.1 %merge_heads.1 = (bf16[128,2048]{1,0:T(8,128)(2,1)}, bf16[128,2048]{1,0:T(8,128)(2,1)}, bf16[128,2048]{1,0:T(8,128)(2,1)}, f32[8,128]{1,0:T(8,128)S(1)}) custom-call(s32[3]{0:T(128)S(1)} %copy-done.4, bf16[4,3,128,512]{3,2,1,0:T(8,128)(2,1)S(1)} %all-to-all-done.1.refs_1_, bf16[64,2048]{1,0:T(8,128)(2,1)S(1)} %add_convert_fusion.refs_2_, ...), custom_call_target="tpu_custom_call" | custom-call | bytes 1024 | tf_op jit(solution)/shard_map/merge_heads/pallas_call | solution.py:31
  99.5 5.1 %collective-permute-done.18.refs_2_ = bf16[64,2048]{1,0:T(8,128)(2,1)S(1)} collective-permute-done((bf16[64,2048]{1,0:T(8,128)(2,1)S(1)}, bf16[64,2048]{1,0:T(8,128)(2,1)S(1)}, u32[]{:S(2)}, u32[]{:S(2)}) %collective-permute-start.18) | collective-permute-done | bytes 262176 | tf_op jit(solution)/shard_map/ppermute | solution.py:494
  104.5 2.0 %weight_out.1 = f32[256,2048]{1,0:T(8,128)} custom-call(s32[3]{0:T(128)S(1)} %copy-done.4, bf16[64,2048]{1,0:T(8,128)(2,1)S(1)} %collective-permute-done.17.refs_1_, bf16[64,2048]{1,0:T(8,128)(2,1)S(1)} %collective-permute-done.18.refs_2_, bf16[64,2048]{1,0:T(8,128)(2,1)S(1)} %collective-permute-done.19.refs_3_, ...), custom_call_target="tpu_custom_call" | custom-call | bytes 1024 | tf_op jit(solution)/shard_map/weight_out/pallas_call | solution.py:31
  (62 shorter events, 22.8 us)
Async XLA Ops:
  0.6 8.7 %collective-permute-start = (bf16[256,2048]{1,0:T(8,128)(2,1)}, bf16[256,2048]{1,0:T(8,128)(2,1)S(1)}, u32[]{:S(2)}, u32[]{:S(2)}) collective-permute-start(bf16[256,2048]{1,0:T(8,128)(2,1)} %refs_1_.1), channel_id=1, source_target_pairs={{0,4},{4,0},{8,12},{12,8},{16,20},{20,16},{24,28},{28,24},{1,5},{5... | collective-permute-start | bytes 3145736 | tf_op jit(solution)/shard_map/ppermute | solution.py:438
  1.1 17.3 %collective-permute-start.6 = (bf16[128,2048]{1,0:T(8,128)(2,1)}, bf16[128,2048]{1,0:T(8,128)(2,1)S(1)}, u32[]{:S(2)}, u32[]{:S(2)}) collective-permute-start(bf16[128,2048]{1,0:T(8,128)(2,1)} %bitcast.22), channel_id=1, source_target_pairs={{0,2},{1,3},{2,0},{3,1},{4,6},{5,7},{6,4},{7,5},{8,10},{9,11},{10,... | collective-permute-start | bytes 1572872 | tf_op jit(solution)/shard_map/ppermute | solution.py:435
  3.7 17.4 %collective-permute-start.5 = (bf16[128,2048]{1,0:T(8,128)(2,1)}, bf16[128,2048]{1,0:T(8,128)(2,1)S(1)}, u32[]{:S(2)}, u32[]{:S(2)}) collective-permute-start(bf16[128,2048]{1,0:T(8,128)(2,1)} %bitcast.23), channel_id=1, source_target_pairs={{0,1},{1,0},{2,3},{3,2},{4,5},{5,4},{6,7},{7,6},{8,9},{9,8},{10,11... | collective-permute-start | bytes 1572872 | tf_op jit(solution)/shard_map/ppermute | solution.py:435
  10.7 21.4 %collective-permute-start.1 = (bf16[128,2048]{1,0:T(8,128)(2,1)S(1)}, bf16[128,2048]{1,0:T(8,128)(2,1)}, u32[]{:S(2)}, u32[]{:S(2)}) collective-permute-start(bf16[128,2048]{1,0:T(8,128)(2,1)S(1)} %get-tuple-element.32.refs_1_), channel_id=1, source_target_pairs={{0,8},{4,20},{8,0},{12,28},{16,24},{20,4},{24,16},{28,12},{1,9},{5... | collective-permute-start | bytes 1572872 | tf_op jit(solution)/shard_map/ppermute | solution.py:452
  12.3 19.7 %collective-permute-start.3 = (bf16[64,2048]{1,0:T(8,128)(2,1)}, bf16[64,2048]{1,0:T(8,128)(2,1)S(1)}, u32[]{:S(2)}, u32[]{:S(2)}) collective-permute-start(bf16[64,2048]{1,0:T(8,128)(2,1)} %get-tuple-element.33), channel_id=1, source_target_pairs={{0,24},{4,28},{8,16},{12,20},{16,8},{20,12},{24,0},{28,4},{1,25},{... | collective-permute-start | bytes 786440 | tf_op jit(solution)/shard_map/ppermute | solution.py:452
  14.8 24.2 %all-to-all-start = ((bf16[4,3,128,512]{3,2,1,0:T(8,128)(2,1)}), bf16[4,3,128,512]{3,2,1,0:T(8,128)(2,1)S(1)}, u32[]{:S(2)}, u32[]{:S(2)}) async-start(bf16[4,3,128,512]{3,2,1,0:T(8,128)(2,1)} %split_heads.1.refs_3_), calls=%async_computation | async-start | bytes 3145728 | tf_op jit(solution)/shard_map/all_to_all | solution.py:444
  19.2 23.8 %collective-permute-start.7 = (bf16[64,2048]{1,0:T(8,128)(2,1)}, bf16[64,2048]{1,0:T(8,128)(2,1)}, u32[]{:S(2)}, u32[]{:S(2)}) collective-permute-start(bf16[64,2048]{1,0:T(8,128)(2,1)} %slice.24), channel_id=1, source_target_pairs={{0,1},{1,0},{2,3},{3,2},{4,5},{5,4},{6,7},{7,6},{8,9},{9,8},{10,11... | collective-permute-start | bytes 786440 | tf_op jit(solution)/shard_map/ppermute | solution.py:435
  21.9 21.1 %collective-permute-start.8 = (bf16[64,2048]{1,0:T(8,128)(2,1)}, bf16[64,2048]{1,0:T(8,128)(2,1)}, u32[]{:S(2)}, u32[]{:S(2)}) collective-permute-start(bf16[64,2048]{1,0:T(8,128)(2,1)} %slice.25), channel_id=1, source_target_pairs={{0,2},{1,3},{2,0},{3,1},{4,6},{5,7},{6,4},{7,5},{8,10},{9,11},{10,... | collective-permute-start | bytes 786440 | tf_op jit(solution)/shard_map/ppermute | solution.py:435
  32.0 11.0 %collective-permute-start.4 = (bf16[64,2048]{1,0:T(8,128)(2,1)S(1)}, bf16[64,2048]{1,0:T(8,128)(2,1)}, u32[]{:S(2)}, u32[]{:S(2)}) collective-permute-start(bf16[64,2048]{1,0:T(8,128)(2,1)S(1)} %collective-permute-done.3.refs_4_), channel_id=1, source_target_pairs={{0,4},{4,0},{8,12},{12,8},{16,20},{20,16},{24,28},{28,24},{1,5},{5... | collective-permute-start | bytes 786440 | tf_op jit(solution)/shard_map/ppermute | solution.py:438
  32.0 11.0 %collective-permute-start.2 = (bf16[128,2048]{1,0:T(8,128)(2,1)}, bf16[128,2048]{1,0:T(8,128)(2,1)}, u32[]{:S(2)}, u32[]{:S(2)}) collective-permute-start(bf16[128,2048]{1,0:T(8,128)(2,1)} %collective-permute-done.1.refs_2_), channel_id=1, source_target_pairs={{0,4},{4,0},{8,12},{12,8},{16,20},{20,16},{24,28},{28,24},{1,5},{5... | collective-permute-start | bytes 1572872 | tf_op jit(solution)/shard_map/ppermute | solution.py:438
  51.0 5.6 %collective-permute-start.11 = (bf16[4,64,2048]{2,1,0:T(8,128)(2,1)S(1)}, bf16[4,64,2048]{2,1,0:T(8,128)(2,1)S(1)}, u32[]{:S(2)}, u32[]{:S(2)}) collective-permute-start(bf16[4,64,2048]{2,1,0:T(8,128)(2,1)S(1)} %get-tuple-element.48), channel_id=1, source_target_pairs={{0,4},{4,0},{8,12},{12,8},{16,20},{20,16},{24,28},{28,24},{1,5},{5... | collective-permute-start | bytes 3145736 | tf_op jit(solution)/shard_map/ppermute | solution.py:438
  51.0 17.9 %collective-permute-start.10 = (bf16[2,128,1024]{2,1,0:T(8,128)(2,1)}, bf16[2,128,1024]{2,1,0:T(8,128)(2,1)}, u32[]{:S(2)}, u32[]{:S(2)}) collective-permute-start(bf16[2,128,1024]{2,1,0:T(8,128)(2,1)} %get-tuple-element.42), channel_id=1, source_target_pairs={{0,2},{1,3},{2,0},{3,1},{4,6},{5,7},{6,4},{7,5},{8,10},{9,11},{10,... | collective-permute-start | bytes 1572872 | tf_op jit(solution)/shard_map/ppermute | solution.py:435
  52.6 16.4 %collective-permute-start.9 = (bf16[2,128,1024]{2,1,0:T(8,128)(2,1)}, bf16[2,128,1024]{2,1,0:T(8,128)(2,1)}, u32[]{:S(2)}, u32[]{:S(2)}) collective-permute-start(bf16[2,128,1024]{2,1,0:T(8,128)(2,1)} %get-tuple-element.39.refs_7_), channel_id=1, source_target_pairs={{0,1},{1,0},{2,3},{3,2},{4,5},{5,4},{6,7},{7,6},{8,9},{9,8},{10,11... | collective-permute-start | bytes 1572872 | tf_op jit(solution)/shard_map/ppermute | solution.py:435
  56.8 20.5 %collective-permute-start.15 = (bf16[64,2048]{1,0:T(8,128)(2,1)S(1)}, bf16[64,2048]{1,0:T(8,128)(2,1)S(1)}, u32[]{:S(2)}, u32[]{:S(2)}) collective-permute-start(bf16[64,2048]{1,0:T(8,128)(2,1)S(1)} %get-tuple-element.53), channel_id=1, source_target_pairs={{0,16},{4,20},{8,24},{12,28},{16,0},{20,4},{24,8},{28,12},{1,17},{... | collective-permute-start | bytes 786440 | tf_op jit(solution)/shard_map/ppermute | solution.py:441
  58.5 18.8 %collective-permute-start.16 = (bf16[64,2048]{1,0:T(8,128)(2,1)S(1)}, bf16[64,2048]{1,0:T(8,128)(2,1)}, u32[]{:S(2)}, u32[]{:S(2)}) collective-permute-start(bf16[64,2048]{1,0:T(8,128)(2,1)S(1)} %get-tuple-element.54), channel_id=1, source_target_pairs={{0,24},{4,28},{8,16},{12,20},{16,8},{20,12},{24,0},{28,4},{1,25},{... | collective-permute-start | bytes 786440 | tf_op jit(solution)/shard_map/ppermute | solution.py:441
  59.8 18.7 %collective-permute-start.14 = (bf16[64,2048]{1,0:T(8,128)(2,1)S(1)}, bf16[64,2048]{1,0:T(8,128)(2,1)}, u32[]{:S(2)}, u32[]{:S(2)}) collective-permute-start(bf16[64,2048]{1,0:T(8,128)(2,1)S(1)} %get-tuple-element.49.refs_4_), channel_id=1, source_target_pairs={{0,8},{4,12},{8,0},{12,4},{16,24},{20,28},{24,16},{28,20},{1,9},{5... | collective-permute-start | bytes 786440 | tf_op jit(solution)/shard_map/ppermute | solution.py:441
  65.2 32.2 %all-to-all-start.1 = ((bf16[4,3,128,512]{3,2,1,0:T(8,128)(2,1)}), bf16[4,3,128,512]{3,2,1,0:T(8,128)(2,1)S(1)}, u32[]{:S(2)}, u32[]{:S(2)}) async-start(bf16[4,3,128,512]{3,2,1,0:T(8,128)(2,1)} %backward.1.refs_4_), calls=%async_computation.1 | async-start | bytes 3145728 | tf_op jit(solution)/shard_map/all_to_all | solution.py:444
  70.3 24.9 %copy-start.3 = (bf16[128,2048]{1,0:T(8,128)(2,1)S(1)}, bf16[128,2048]{1,0:T(8,128)(2,1)}, u32[]{:S(2)}) copy-start(bf16[128,2048]{1,0:T(8,128)(2,1)} %copy-done.2) | copy-start | bytes 1572868
  70.3 22.9 %collective-permute-start.12 = (bf16[128,1024]{1,0:T(8,128)(2,1)S(1)}, bf16[128,1024]{1,0:T(8,128)(2,1)S(1)}, u32[]{:S(2)}, u32[]{:S(2)}) collective-permute-start(bf16[128,1024]{1,0:T(8,128)(2,1)S(1)} %get-tuple-element.50), channel_id=1, source_target_pairs={{0,2},{1,3},{2,0},{3,1},{4,6},{5,7},{6,4},{7,5},{8,10},{9,11},{10,... | collective-permute-start | bytes 786440 | tf_op jit(solution)/shard_map/ppermute | solution.py:435
  72.3 22.9 %collective-permute-start.13 = (bf16[128,1024]{1,0:T(8,128)(2,1)S(1)}, bf16[128,1024]{1,0:T(8,128)(2,1)S(1)}, u32[]{:S(2)}, u32[]{:S(2)}) collective-permute-start(bf16[128,1024]{1,0:T(8,128)(2,1)S(1)} %get-tuple-element.51), channel_id=1, source_target_pairs={{0,1},{1,0},{2,3},{3,2},{4,5},{5,4},{6,7},{7,6},{8,9},{9,8},{10,11... | collective-permute-start | bytes 786440 | tf_op jit(solution)/shard_map/ppermute | solution.py:435
  79.7 19.7 %collective-permute-start.20 = (bf16[64,2048]{1,0:T(8,128)(2,1)S(1)}, bf16[64,2048]{1,0:T(8,128)(2,1)S(1)}, u32[]{:S(2)}, u32[]{:S(2)}) collective-permute-start(bf16[64,2048]{1,0:T(8,128)(2,1)S(1)} %add_convert_fusion.refs_2_), channel_id=1, source_target_pairs={{0,3},{1,2},{2,5},{3,4},{4,1},{5,0},{6,7},{7,6},{8,11},{9,10},{10,... | collective-permute-start | bytes 786440 | tf_op jit(solution)/shard_map/ppermute | solution.py:494
  81.2 18.2 %collective-permute-start.19 = (bf16[64,2048]{1,0:T(8,128)(2,1)S(1)}, bf16[64,2048]{1,0:T(8,128)(2,1)S(1)}, u32[]{:S(2)}, u32[]{:S(2)}) collective-permute-start(bf16[64,2048]{1,0:T(8,128)(2,1)S(1)} %add_convert_fusion.refs_2_), channel_id=1, source_target_pairs={{0,2},{1,3},{2,4},{3,5},{4,0},{5,1},{6,6},{7,7},{8,10},{9,11},{10,... | collective-permute-start | bytes 786440 | tf_op jit(solution)/shard_map/ppermute | solution.py:494
  83.2 21.4 %collective-permute-start.18 = (bf16[64,2048]{1,0:T(8,128)(2,1)S(1)}, bf16[64,2048]{1,0:T(8,128)(2,1)S(1)}, u32[]{:S(2)}, u32[]{:S(2)}) collective-permute-start(bf16[64,2048]{1,0:T(8,128)(2,1)S(1)} %add_convert_fusion.refs_2_), channel_id=1, source_target_pairs={{0,1},{1,0},{2,7},{3,6},{4,3},{5,2},{6,5},{7,4},{8,9},{9,8},{10,15... | collective-permute-start | bytes 786440 | tf_op jit(solution)/shard_map/ppermute | solution.py:494
  93.2 11.3 %collective-permute-start.17 = (bf16[64,2048]{1,0:T(8,128)(2,1)S(1)}, bf16[64,2048]{1,0:T(8,128)(2,1)S(1)}, u32[]{:S(2)}, u32[]{:S(2)}) collective-permute-start(bf16[64,2048]{1,0:T(8,128)(2,1)S(1)} %add_convert_fusion.refs_2_), channel_id=1, source_target_pairs={{0,0},{1,1},{2,6},{3,7},{4,2},{5,3},{6,4},{7,5},{8,8},{9,9},{10,14... | collective-permute-start | bytes 786440 | tf_op jit(solution)/shard_map/ppermute | solution.py:494
  (9 other events, 37.0 us)

commit v5 on v4

--- a/solution.py
+++ b/solution.py
@@ -13,7 +13,7 @@
 F32 = jnp.float32
 BF16 = jnp.bfloat16
 VMEM_BYTES = 20 * 1024 * 1024
-HINT = 2_000_000_000
+HINT = 1_000_000_000
 
 
 SMEM = pl.BlockSpec(memory_space=pltpu.SMEM)
@@ -341,18 +341,22 @@
     return call(sum_kernel, "sum_planes", parts, [VMEM] * 4, [out], [VMEM], hint=0)[0]
 
 
-def weight_out_kernel(place, p0, p1, p2, p3, out):
+def weight_out_kernel(place, p0, p1, p2, p3, out, held, sems):
+    copies = []
     for k, piece in enumerate((p0, p1, p2, p3)):
         head = jnp.bitwise_xor(place[0] % 2, k % 2)
         half = jnp.bitwise_xor(jnp.bitwise_xor(place[1], place[0] // 2), k // 2)
         start = pl.multiple_of(head * DH + half * HALF, HALF)
-        out[pl.ds(start, HALF), :] = piece[...].astype(F32) * 0.125
+        held[k] = piece[...].astype(F32) * 0.125
+        copies += run_copies([(held.at[k], out.at[pl.ds(start, HALF), :])], sems, k)
+    wait_all(copies)
 
 
 def weight_out(place, pieces, after=()):
     rows, width = pieces[0].shape
     out = jax.ShapeDtypeStruct((4 * rows, width), F32)
-    return call(weight_out_kernel, "weight_out", (place, *pieces), [SMEM] + [VMEM] * 4, [out], [VMEM], after=after)[0]
+    scratch = [pltpu.VMEM((4, rows, width), F32), pltpu.SemaphoreType.DMA((4,))]
+    return call(weight_out_kernel, "weight_out", (place, *pieces), [SMEM] + [VMEM] * 4, [out], [HBM], scratch, after=after)[0]
 
 
 def grads_kernel(place, w0, w1, w2, w3, w4, c0, c1, c2, c3, c4, grads, slab, cots, sems):
@@ -459,8 +463,7 @@
     cot_blocks = (cot, cot_x, cot_y, plane(cot_y[:half], 1), plane(cot_x[half:], 2))
     attended, attended_t, log_total = forward(mask, blocks, after=(arrived((cot_x, cot_y)),))
 
-    crossed, other, attended, far_y, far_x = lax.optimization_barrier((swap(direct), swap(part), attended, *cot_blocks[3:]))
-    cot_blocks = (*cot_blocks[:3], far_y, far_x)
+    crossed, other, attended = lax.optimization_barrier((swap(direct), swap(part), attended))
     weights = (chunk, direct, crossed, part, other)
 
     send_x, send_y, mixed_own, x_right, y_left = mixed_parts(place, weights, attended)

time: 107 us -> 106 us (level)
  transfers between devices with their start and end apart: 23 -> 23, of which waited for: 8 -> 7; matrix products, arithmetic and copies ran while one was open for 5% -> 5% of each run, Pallas kernels for 19% -> 23%
where the time goes in v5:
time: 106 us
  starting transfers between devices  36 us (34%)
  waiting for transfers between devices  33.6 us (32%)
  Pallas kernels  29.7 us (28%)
  other arithmetic  3.91 us (4%)
  local copies, waits for them, and re-layouts  1.59 us (2%)
    pallas_call x12, Pallas kernels, call(): pl.pallas_call(body, in_specs=list(in_specs) + [HBM] * extra, out_specs=l...  29.7 us
    ppermute x8, starting transfers between devices, plane(): return lax.ppermute(array, 'seq', [(i, i ^ flip) for i in range(4)])  13.1 us
    ppermute x8, waiting for transfers between devices, plane(): return lax.ppermute(array, 'seq', [(i, i ^ flip) for i in range(4)])  9.79 us
    ppermute x2, waiting for transfers between devices, in_dp(): lax.ppermute(array, 'dp', [(2 * a + c, target(a, c)) for a in range(4) fo...  8.66 us
    all_to_all x2, starting transfers between devices, columns(): return lax.all_to_all(array, 'seq', 0, 0, tiled=True)  7.27 us
    ppermute x4, starting transfers between devices, column_shards(): pieces.append(lax.ppermute(summed, ('dp', 'seq'), pairs))  5.65 us
    all_to_all x2, waiting for transfers between devices, columns(): return lax.all_to_all(array, 'seq', 0, 0, tiled=True)  5.31 us
    ppermute x4, waiting for transfers between devices, column_shards(): pieces.append(lax.ppermute(summed, ('dp', 'seq'), pairs))  5.06 us
  transfers between devices with their start and end apart: 23, of which 7 were waited for; matrix products, arithmetic and copies ran while one was open for 5% of the time, Pallas kernels for 23%

profile of v5, /device:TPU:0, one launch (start us, length us, event | category | flops | bytes accessed | tf_op | source)
XLA Modules:
  0.0 105.7 jit_solution(3164317425959490437)
XLA Ops:
  1.1 2.6 %collective-permute-start.6 = (bf16[128,2048]{1,0:T(8,128)(2,1)}, bf16[128,2048]{1,0:T(8,128)(2,1)S(1)}, u32[]{:S(2)}, u32[]{:S(2)}) collective-permute-start(bf16[128,2048]{1,0:T(8,128)(2,1)} %bitcast.22), channel_id=1, source_target_pairs={{0,2},{1,3},{2,0},{3,1},{4,6},{5,7},{6,4},{7,5},{8,10},{9,11},{10,... | collective-permute-start | bytes 1572872 | tf_op jit(solution)/shard_map/ppermute | solution.py:439
  5.8 3.5 %split_heads.1.refs_3_ = bf16[4,3,128,512]{3,2,1,0:T(8,128)(2,1)} custom-call(s32[3]{0:T(128)} %pad_add_fusion.refs_0_, bf16[128,2048]{1,0:T(8,128)(2,1)} %bitcast.28, bf16[128,2048]{1,0:T(8,128)(2,1)} %bitcast.29, bf16[128,2048]{1,0:T(8,128)(2,1)} %bitcast.30), custom_call_target="tpu_custom_call" | custom-call | bytes 1024 | tf_op jit(solution)/shard_map/split_heads/pallas_call | solution.py:31
  10.7 1.6 %collective-permute-start.1 = (bf16[128,2048]{1,0:T(8,128)(2,1)S(1)}, bf16[128,2048]{1,0:T(8,128)(2,1)}, u32[]{:S(2)}, u32[]{:S(2)}) collective-permute-start(bf16[128,2048]{1,0:T(8,128)(2,1)S(1)} %get-tuple-element.30.refs_1_), channel_id=1, source_target_pairs={{0,8},{4,20},{8,0},{12,28},{16,24},{20,4},{24,16},{28,12},{1,9},{5... | collective-permute-start | bytes 1572872 | tf_op jit(solution)/shard_map/ppermute | solution.py:456
  12.3 2.5 %collective-permute-start.3 = (bf16[64,2048]{1,0:T(8,128)(2,1)}, bf16[64,2048]{1,0:T(8,128)(2,1)S(1)}, u32[]{:S(2)}, u32[]{:S(2)}) collective-permute-start(bf16[64,2048]{1,0:T(8,128)(2,1)} %get-tuple-element.31), channel_id=1, source_target_pairs={{0,24},{4,28},{8,16},{12,20},{16,8},{20,12},{24,0},{28,4},{1,25},{... | collective-permute-start | bytes 786440 | tf_op jit(solution)/shard_map/ppermute | solution.py:456
  14.8 3.6 %all-to-all-start = ((bf16[4,3,128,512]{3,2,1,0:T(8,128)(2,1)}), bf16[4,3,128,512]{3,2,1,0:T(8,128)(2,1)S(1)}, u32[]{:S(2)}, u32[]{:S(2)}) async-start(bf16[4,3,128,512]{3,2,1,0:T(8,128)(2,1)} %split_heads.1.refs_3_), calls=%async_computation | async-start | bytes 3145728 | tf_op jit(solution)/shard_map/all_to_all | solution.py:448
  19.2 2.0 %collective-permute-start.9 = (bf16[64,2048]{1,0:T(8,128)(2,1)}, bf16[64,2048]{1,0:T(8,128)(2,1)}, u32[]{:S(2)}, u32[]{:S(2)}) collective-permute-start(bf16[64,2048]{1,0:T(8,128)(2,1)} %slice.25), channel_id=1, source_target_pairs={{0,1},{1,0},{2,3},{3,2},{4,5},{5,4},{6,7},{7,6},{8,9},{9,8},{10,11... | collective-permute-start | bytes 786440 | tf_op jit(solution)/shard_map/ppermute | solution.py:439
  23.3 8.7 %collective-permute-done.3.refs_4_ = bf16[64,2048]{1,0:T(8,128)(2,1)S(1)} collective-permute-done((bf16[64,2048]{1,0:T(8,128)(2,1)}, bf16[64,2048]{1,0:T(8,128)(2,1)S(1)}, u32[]{:S(2)}, u32[]{:S(2)}) %collective-permute-start.3) | collective-permute-done | bytes 262176 | tf_op jit(solution)/shard_map/ppermute | solution.py:456
  32.0 1.7 %collective-permute-start.2 = (bf16[128,2048]{1,0:T(8,128)(2,1)}, bf16[128,2048]{1,0:T(8,128)(2,1)}, u32[]{:S(2)}, u32[]{:S(2)}) collective-permute-start(bf16[128,2048]{1,0:T(8,128)(2,1)} %collective-permute-done.1.refs_2_), channel_id=1, source_target_pairs={{0,4},{4,0},{8,12},{12,8},{16,20},{20,16},{24,28},{28,24},{1,5},{5... | collective-permute-start | bytes 1572872 | tf_op jit(solution)/shard_map/ppermute | solution.py:442
  33.7 5.3 %all-to-all-done.refs_1_.refs_3_ = bf16[4,3,128,512]{3,2,1,0:T(8,128)(2,1)S(1)} async-done(((bf16[4,3,128,512]{3,2,1,0:T(8,128)(2,1)}), bf16[4,3,128,512]{3,2,1,0:T(8,128)(2,1)S(1)}, u32[]{:S(2)}, u32[]{:S(2)}) %all-to-all-start) | async-done | bytes 1572896 | tf_op jit(solution)/shard_map/all_to_all | solution.py:448
  39.0 3.2 %forward.1 = (bf16[512,512]{1,0:T(8,128)(2,1)S(1)}, bf16[512,512]{1,0:T(8,128)(2,1)S(1)}, f32[4,512]{1,0:T(4,128)S(1)}) custom-call(s32[16]{0:T(128)S(1)} %reshape.48.refs_0_, bf16[4,3,128,512]{3,2,1,0:T(8,128)(2,1)S(1)} %all-to-all-done.refs_1_.refs_3_, f32[8,128]{1,0:T(8,128)S(1)} %arrived.1.refs_2_), custom_call_target="tpu_custom_call" | custom-call | bytes 1024 | tf_op jit(solution)/shard_map/forward/pallas_call | solution.py:31
  42.3 4.0 %mixed_parts.1 = (bf16[2,128,1024]{2,1,0:T(8,128)(2,1)}, bf16[2,128,1024]{2,1,0:T(8,128)(2,1)}, bf16[128,2048]{1,0:T(8,128)(2,1)S(1)}, bf16[128,1024]{1,0:T(8,128)(2,1)S(1)}, bf16[128,1024]{1,0:T(8,128)(2,1)S(1)}) custom-call(s32[3]{0:T(128)S(1)} %copy-done.4, bf16[128,2048]{1,0:T(8,128)(2,1)S(1)} %get-tuple-element.30.refs_1_, ...), custom_call_target="tpu_custom_call" | custom-call | bytes 1024 | tf_op jit(solution)/shard_map/mixed_parts/pallas_call | solution.py:31
  46.4 3.8 %weight_parts.1 = (bf16[4,64,2048]{2,1,0:T(8,128)(2,1)S(1)}, bf16[4,64,2048]{2,1,0:T(8,128)(2,1)S(1)}) custom-call(s32[3]{0:T(128)S(1)} %copy-done.4, bf16[512,512]{1,0:T(8,128)(2,1)S(1)} %get-tuple-element.42.refs_1_, bf16[128,2048]{1,0:T(8,128)(2,1)S(1)} %bitcast.24, bf16[128,2048]{1,0:T(8,128)(2,1)S(1)} %collective-permute-done.5.refs_0_.refs_3_.refs_7_, ...), custom_call_target="tpu_custom_call" | custom-call | bytes 1024 | tf_op jit(solution)/shard_map/weight_parts/pallas_call | solution.py:31
  52.4 3.4 %attended_grads.1.refs_2_ = bf16[512,512]{1,0:T(8,128)(2,1)S(1)} custom-call(s32[3]{0:T(128)S(1)} %copy-done.4, bf16[128,2048]{1,0:T(8,128)(2,1)S(1)} %get-tuple-element.30.refs_1_, bf16[128,2048]{1,0:T(8,128)(2,1)} %collective-permute-done.1.refs_2_, bf16[128,2048]{1,0:T(8,128)(2,1)} %collective-permute-done.2.refs_3_, ...), custom_call_target="tpu_custom_call" | custom-call | bytes 1024 | tf_op jit(solution)/shard_map/attended_grads/pallas_call | solution.py:31
  56.3 2.9 %collective-permute-start.16 = (bf16[64,2048]{1,0:T(8,128)(2,1)S(1)}, bf16[64,2048]{1,0:T(8,128)(2,1)}, u32[]{:S(2)}, u32[]{:S(2)}) collective-permute-start(bf16[64,2048]{1,0:T(8,128)(2,1)S(1)} %get-tuple-element.50), channel_id=1, source_target_pairs={{0,24},{4,28},{8,16},{12,20},{16,8},{20,12},{24,0},{28,4},{1,25},{... | collective-permute-start | bytes 786440 | tf_op jit(solution)/shard_map/ppermute | solution.py:445
  59.6 4.8 %backward.1.refs_4_ = bf16[4,3,128,512]{3,2,1,0:T(8,128)(2,1)} custom-call(s32[16]{0:T(128)S(1)} %reshape.48.refs_0_, f32[4,512]{1,0:T(4,128)S(1)} %get-tuple-element.41.refs_1_, bf16[512,512]{1,0:T(8,128)(2,1)S(1)} %attended_grads.1.refs_2_, bf16[4,3,128,512]{3,2,1,0:T(8,128)(2,1)S(1)} %all-to-all-done.refs_1_.refs_3_, ...), custom_call_target="tpu_custom_call" | custom-call | bytes 1024 | tf_op jit(solution)/shard_map/backward/pallas_call | solution.py:31
  64.5 3.7 %all-to-all-start.1 = ((bf16[4,3,128,512]{3,2,1,0:T(8,128)(2,1)}), bf16[4,3,128,512]{3,2,1,0:T(8,128)(2,1)S(1)}, u32[]{:S(2)}, u32[]{:S(2)}) async-start(bf16[4,3,128,512]{3,2,1,0:T(8,128)(2,1)} %backward.1.refs_4_), calls=%async_computation.1 | async-start | bytes 3145728 | tf_op jit(solution)/shard_map/all_to_all | solution.py:448
  69.6 2.0 %collective-permute-start.12 = (bf16[128,1024]{1,0:T(8,128)(2,1)S(1)}, bf16[128,1024]{1,0:T(8,128)(2,1)S(1)}, u32[]{:S(2)}, u32[]{:S(2)}) collective-permute-start(bf16[128,1024]{1,0:T(8,128)(2,1)S(1)} %get-tuple-element.46), channel_id=1, source_target_pairs={{0,2},{1,3},{2,0},{3,1},{4,6},{5,7},{6,4},{7,5},{8,10},{9,11},{10,... | collective-permute-start | bytes 786440 | tf_op jit(solution)/shard_map/ppermute | solution.py:439
  73.1 3.5 %collective-permute-done.15 = bf16[64,2048]{1,0:T(8,128)(2,1)S(1)} collective-permute-done((bf16[64,2048]{1,0:T(8,128)(2,1)S(1)}, bf16[64,2048]{1,0:T(8,128)(2,1)S(1)}, u32[]{:S(2)}, u32[]{:S(2)}) %collective-permute-start.15) | collective-permute-done | bytes 262176 | tf_op jit(solution)/shard_map/ppermute | solution.py:445
  79.0 1.5 %collective-permute-start.20 = (bf16[64,2048]{1,0:T(8,128)(2,1)S(1)}, bf16[64,2048]{1,0:T(8,128)(2,1)S(1)}, u32[]{:S(2)}, u32[]{:S(2)}) collective-permute-start(bf16[64,2048]{1,0:T(8,128)(2,1)S(1)} %add_convert_fusion.refs_2_), channel_id=1, source_target_pairs={{0,3},{1,2},{2,5},{3,4},{4,1},{5,0},{6,7},{7,6},{8,11},{9,10},{10,... | collective-permute-start | bytes 786440 | tf_op jit(solution)/shard_map/ppermute | solution.py:497
  80.5 2.0 %collective-permute-start.19 = (bf16[64,2048]{1,0:T(8,128)(2,1)S(1)}, bf16[64,2048]{1,0:T(8,128)(2,1)S(1)}, u32[]{:S(2)}, u32[]{:S(2)}) collective-permute-start(bf16[64,2048]{1,0:T(8,128)(2,1)S(1)} %add_convert_fusion.refs_2_), channel_id=1, source_target_pairs={{0,2},{1,3},{2,4},{3,5},{4,0},{5,1},{6,6},{7,7},{8,10},{9,11},{10,... | collective-permute-start | bytes 786440 | tf_op jit(solution)/shard_map/ppermute | solution.py:497
  84.0 8.5 %collective-permute-done.12 = bf16[128,1024]{1,0:T(8,128)(2,1)S(1)} collective-permute-done((bf16[128,1024]{1,0:T(8,128)(2,1)S(1)}, bf16[128,1024]{1,0:T(8,128)(2,1)S(1)}, u32[]{:S(2)}, u32[]{:S(2)}) %collective-permute-start.12) | collective-permute-done | bytes 262176 | tf_op jit(solution)/shard_map/ppermute | solution.py:439
  96.6 2.1 %merge_heads.1 = (bf16[128,2048]{1,0:T(8,128)(2,1)}, bf16[128,2048]{1,0:T(8,128)(2,1)}, bf16[128,2048]{1,0:T(8,128)(2,1)}, f32[8,128]{1,0:T(8,128)S(1)}) custom-call(s32[3]{0:T(128)S(1)} %copy-done.4, bf16[4,3,128,512]{3,2,1,0:T(8,128)(2,1)S(1)} %all-to-all-done.1.refs_1_, bf16[64,2048]{1,0:T(8,128)(2,1)S(1)} %add_convert_fusion.refs_2_, ...), custom_call_target="tpu_custom_call" | custom-call | bytes 1024 | tf_op jit(solution)/shard_map/merge_heads/pallas_call | solution.py:31
  98.8 5.1 %collective-permute-done.18.refs_2_ = bf16[64,2048]{1,0:T(8,128)(2,1)S(1)} collective-permute-done((bf16[64,2048]{1,0:T(8,128)(2,1)S(1)}, bf16[64,2048]{1,0:T(8,128)(2,1)S(1)}, u32[]{:S(2)}, u32[]{:S(2)}) %collective-permute-start.18) | collective-permute-done | bytes 262176 | tf_op jit(solution)/shard_map/ppermute | solution.py:497
  103.8 1.9 %weight_out.1 = f32[256,2048]{1,0:T(8,128)} custom-call(s32[3]{0:T(128)S(1)} %copy-done.4, bf16[64,2048]{1,0:T(8,128)(2,1)S(1)} %collective-permute-done.17.refs_1_, bf16[64,2048]{1,0:T(8,128)(2,1)S(1)} %collective-permute-done.18.refs_2_, bf16[64,2048]{1,0:T(8,128)(2,1)S(1)} %collective-permute-done.19.refs_3_, ...), custom_call_target="tpu_custom_call" | custom-call | bytes 1024 | tf_op jit(solution)/shard_map/weight_out/pallas_call | solution.py:31
  (62 shorter events, 20.9 us)
Async XLA Ops:
  0.6 8.7 %collective-permute-start = (bf16[256,2048]{1,0:T(8,128)(2,1)}, bf16[256,2048]{1,0:T(8,128)(2,1)S(1)}, u32[]{:S(2)}, u32[]{:S(2)}) collective-permute-start(bf16[256,2048]{1,0:T(8,128)(2,1)} %refs_1_.1), channel_id=1, source_target_pairs={{0,4},{4,0},{8,12},{12,8},{16,20},{20,16},{24,28},{28,24},{1,5},{5... | collective-permute-start | bytes 3145736 | tf_op jit(solution)/shard_map/ppermute | solution.py:442
  1.1 17.3 %collective-permute-start.6 = (bf16[128,2048]{1,0:T(8,128)(2,1)}, bf16[128,2048]{1,0:T(8,128)(2,1)S(1)}, u32[]{:S(2)}, u32[]{:S(2)}) collective-permute-start(bf16[128,2048]{1,0:T(8,128)(2,1)} %bitcast.22), channel_id=1, source_target_pairs={{0,2},{1,3},{2,0},{3,1},{4,6},{5,7},{6,4},{7,5},{8,10},{9,11},{10,... | collective-permute-start | bytes 1572872 | tf_op jit(solution)/shard_map/ppermute | solution.py:439
  3.7 17.4 %collective-permute-start.5 = (bf16[128,2048]{1,0:T(8,128)(2,1)}, bf16[128,2048]{1,0:T(8,128)(2,1)S(1)}, u32[]{:S(2)}, u32[]{:S(2)}) collective-permute-start(bf16[128,2048]{1,0:T(8,128)(2,1)} %bitcast.23), channel_id=1, source_target_pairs={{0,1},{1,0},{2,3},{3,2},{4,5},{5,4},{6,7},{7,6},{8,9},{9,8},{10,11... | collective-permute-start | bytes 1572872 | tf_op jit(solution)/shard_map/ppermute | solution.py:439
  10.7 21.4 %collective-permute-start.1 = (bf16[128,2048]{1,0:T(8,128)(2,1)S(1)}, bf16[128,2048]{1,0:T(8,128)(2,1)}, u32[]{:S(2)}, u32[]{:S(2)}) collective-permute-start(bf16[128,2048]{1,0:T(8,128)(2,1)S(1)} %get-tuple-element.30.refs_1_), channel_id=1, source_target_pairs={{0,8},{4,20},{8,0},{12,28},{16,24},{20,4},{24,16},{28,12},{1,9},{5... | collective-permute-start | bytes 1572872 | tf_op jit(solution)/shard_map/ppermute | solution.py:456
  12.3 19.7 %collective-permute-start.3 = (bf16[64,2048]{1,0:T(8,128)(2,1)}, bf16[64,2048]{1,0:T(8,128)(2,1)S(1)}, u32[]{:S(2)}, u32[]{:S(2)}) collective-permute-start(bf16[64,2048]{1,0:T(8,128)(2,1)} %get-tuple-element.31), channel_id=1, source_target_pairs={{0,24},{4,28},{8,16},{12,20},{16,8},{20,12},{24,0},{28,4},{1,25},{... | collective-permute-start | bytes 786440 | tf_op jit(solution)/shard_map/ppermute | solution.py:456
  14.8 24.2 %all-to-all-start = ((bf16[4,3,128,512]{3,2,1,0:T(8,128)(2,1)}), bf16[4,3,128,512]{3,2,1,0:T(8,128)(2,1)S(1)}, u32[]{:S(2)}, u32[]{:S(2)}) async-start(bf16[4,3,128,512]{3,2,1,0:T(8,128)(2,1)} %split_heads.1.refs_3_), calls=%async_computation | async-start | bytes 3145728 | tf_op jit(solution)/shard_map/all_to_all | solution.py:448
  19.2 27.2 %collective-permute-start.9 = (bf16[64,2048]{1,0:T(8,128)(2,1)}, bf16[64,2048]{1,0:T(8,128)(2,1)}, u32[]{:S(2)}, u32[]{:S(2)}) collective-permute-start(bf16[64,2048]{1,0:T(8,128)(2,1)} %slice.25), channel_id=1, source_target_pairs={{0,1},{1,0},{2,3},{3,2},{4,5},{5,4},{6,7},{7,6},{8,9},{9,8},{10,11... | collective-permute-start | bytes 786440 | tf_op jit(solution)/shard_map/ppermute | solution.py:439
  21.9 24.5 %collective-permute-start.10 = (bf16[64,2048]{1,0:T(8,128)(2,1)}, bf16[64,2048]{1,0:T(8,128)(2,1)}, u32[]{:S(2)}, u32[]{:S(2)}) collective-permute-start(bf16[64,2048]{1,0:T(8,128)(2,1)} %slice.26), channel_id=1, source_target_pairs={{0,2},{1,3},{2,0},{3,1},{4,6},{5,7},{6,4},{7,5},{8,10},{9,11},{10,... | collective-permute-start | bytes 786440 | tf_op jit(solution)/shard_map/ppermute | solution.py:439
  32.0 10.2 %collective-permute-start.4 = (bf16[64,2048]{1,0:T(8,128)(2,1)S(1)}, bf16[64,2048]{1,0:T(8,128)(2,1)}, u32[]{:S(2)}, u32[]{:S(2)}) collective-permute-start(bf16[64,2048]{1,0:T(8,128)(2,1)S(1)} %collective-permute-done.3.refs_4_), channel_id=1, source_target_pairs={{0,4},{4,0},{8,12},{12,8},{16,20},{20,16},{24,28},{28,24},{1,5},{5... | collective-permute-start | bytes 786440 | tf_op jit(solution)/shard_map/ppermute | solution.py:442
  32.0 10.2 %collective-permute-start.2 = (bf16[128,2048]{1,0:T(8,128)(2,1)}, bf16[128,2048]{1,0:T(8,128)(2,1)}, u32[]{:S(2)}, u32[]{:S(2)}) collective-permute-start(bf16[128,2048]{1,0:T(8,128)(2,1)} %collective-permute-done.1.refs_2_), channel_id=1, source_target_pairs={{0,4},{4,0},{8,12},{12,8},{16,20},{20,16},{24,28},{28,24},{1,5},{5... | collective-permute-start | bytes 1572872 | tf_op jit(solution)/shard_map/ppermute | solution.py:442
  50.2 5.6 %collective-permute-start.11 = (bf16[4,64,2048]{2,1,0:T(8,128)(2,1)S(1)}, bf16[4,64,2048]{2,1,0:T(8,128)(2,1)S(1)}, u32[]{:S(2)}, u32[]{:S(2)}) collective-permute-start(bf16[4,64,2048]{2,1,0:T(8,128)(2,1)S(1)} %get-tuple-element.44), channel_id=1, source_target_pairs={{0,4},{4,0},{8,12},{12,8},{16,20},{20,16},{24,28},{28,24},{1,5},{5... | collective-permute-start | bytes 3145736 | tf_op jit(solution)/shard_map/ppermute | solution.py:442
  50.3 17.9 %collective-permute-start.8 = (bf16[2,128,1024]{2,1,0:T(8,128)(2,1)}, bf16[2,128,1024]{2,1,0:T(8,128)(2,1)}, u32[]{:S(2)}, u32[]{:S(2)}) collective-permute-start(bf16[2,128,1024]{2,1,0:T(8,128)(2,1)} %get-tuple-element.40), channel_id=1, source_target_pairs={{0,2},{1,3},{2,0},{3,1},{4,6},{5,7},{6,4},{7,5},{8,10},{9,11},{10,... | collective-permute-start | bytes 1572872 | tf_op jit(solution)/shard_map/ppermute | solution.py:439
  51.8 16.4 %collective-permute-start.7 = (bf16[2,128,1024]{2,1,0:T(8,128)(2,1)}, bf16[2,128,1024]{2,1,0:T(8,128)(2,1)}, u32[]{:S(2)}, u32[]{:S(2)}) collective-permute-start(bf16[2,128,1024]{2,1,0:T(8,128)(2,1)} %get-tuple-element.37.refs_7_), channel_id=1, source_target_pairs={{0,1},{1,0},{2,3},{3,2},{4,5},{5,4},{6,7},{7,6},{8,9},{9,8},{10,11... | collective-permute-start | bytes 1572872 | tf_op jit(solution)/shard_map/ppermute | solution.py:439
  56.1 20.5 %collective-permute-start.15 = (bf16[64,2048]{1,0:T(8,128)(2,1)S(1)}, bf16[64,2048]{1,0:T(8,128)(2,1)S(1)}, u32[]{:S(2)}, u32[]{:S(2)}) collective-permute-start(bf16[64,2048]{1,0:T(8,128)(2,1)S(1)} %get-tuple-element.49), channel_id=1, source_target_pairs={{0,16},{4,20},{8,24},{12,28},{16,0},{20,4},{24,8},{28,12},{1,17},{... | collective-permute-start | bytes 786440 | tf_op jit(solution)/shard_map/ppermute | solution.py:445
  56.3 20.3 %collective-permute-start.16 = (bf16[64,2048]{1,0:T(8,128)(2,1)S(1)}, bf16[64,2048]{1,0:T(8,128)(2,1)}, u32[]{:S(2)}, u32[]{:S(2)}) collective-permute-start(bf16[64,2048]{1,0:T(8,128)(2,1)S(1)} %get-tuple-element.50), channel_id=1, source_target_pairs={{0,24},{4,28},{8,16},{12,20},{16,8},{20,12},{24,0},{28,4},{1,25},{... | collective-permute-start | bytes 786440 | tf_op jit(solution)/shard_map/ppermute | solution.py:445
  59.2 18.7 %collective-permute-start.14 = (bf16[64,2048]{1,0:T(8,128)(2,1)S(1)}, bf16[64,2048]{1,0:T(8,128)(2,1)}, u32[]{:S(2)}, u32[]{:S(2)}) collective-permute-start(bf16[64,2048]{1,0:T(8,128)(2,1)S(1)} %get-tuple-element.45.refs_4_), channel_id=1, source_target_pairs={{0,8},{4,12},{8,0},{12,4},{16,24},{20,28},{24,16},{28,20},{1,9},{5... | collective-permute-start | bytes 786440 | tf_op jit(solution)/shard_map/ppermute | solution.py:445
  64.5 32.2 %all-to-all-start.1 = ((bf16[4,3,128,512]{3,2,1,0:T(8,128)(2,1)}), bf16[4,3,128,512]{3,2,1,0:T(8,128)(2,1)S(1)}, u32[]{:S(2)}, u32[]{:S(2)}) async-start(bf16[4,3,128,512]{3,2,1,0:T(8,128)(2,1)} %backward.1.refs_4_), calls=%async_computation.1 | async-start | bytes 3145728 | tf_op jit(solution)/shard_map/all_to_all | solution.py:448
  69.6 24.9 %copy-start.3 = (bf16[128,2048]{1,0:T(8,128)(2,1)S(1)}, bf16[128,2048]{1,0:T(8,128)(2,1)}, u32[]{:S(2)}) copy-start(bf16[128,2048]{1,0:T(8,128)(2,1)} %copy-done.2) | copy-start | bytes 1572868
  69.6 22.9 %collective-permute-start.12 = (bf16[128,1024]{1,0:T(8,128)(2,1)S(1)}, bf16[128,1024]{1,0:T(8,128)(2,1)S(1)}, u32[]{:S(2)}, u32[]{:S(2)}) collective-permute-start(bf16[128,1024]{1,0:T(8,128)(2,1)S(1)} %get-tuple-element.46), channel_id=1, source_target_pairs={{0,2},{1,3},{2,0},{3,1},{4,6},{5,7},{6,4},{7,5},{8,10},{9,11},{10,... | collective-permute-start | bytes 786440 | tf_op jit(solution)/shard_map/ppermute | solution.py:439
  71.6 22.9 %collective-permute-start.13 = (bf16[128,1024]{1,0:T(8,128)(2,1)S(1)}, bf16[128,1024]{1,0:T(8,128)(2,1)S(1)}, u32[]{:S(2)}, u32[]{:S(2)}) collective-permute-start(bf16[128,1024]{1,0:T(8,128)(2,1)S(1)} %get-tuple-element.47), channel_id=1, source_target_pairs={{0,1},{1,0},{2,3},{3,2},{4,5},{5,4},{6,7},{7,6},{8,9},{9,8},{10,11... | collective-permute-start | bytes 786440 | tf_op jit(solution)/shard_map/ppermute | solution.py:439
  79.0 19.7 %collective-permute-start.20 = (bf16[64,2048]{1,0:T(8,128)(2,1)S(1)}, bf16[64,2048]{1,0:T(8,128)(2,1)S(1)}, u32[]{:S(2)}, u32[]{:S(2)}) collective-permute-start(bf16[64,2048]{1,0:T(8,128)(2,1)S(1)} %add_convert_fusion.refs_2_), channel_id=1, source_target_pairs={{0,3},{1,2},{2,5},{3,4},{4,1},{5,0},{6,7},{7,6},{8,11},{9,10},{10,... | collective-permute-start | bytes 786440 | tf_op jit(solution)/shard_map/ppermute | solution.py:497
  80.5 18.2 %collective-permute-start.19 = (bf16[64,2048]{1,0:T(8,128)(2,1)S(1)}, bf16[64,2048]{1,0:T(8,128)(2,1)S(1)}, u32[]{:S(2)}, u32[]{:S(2)}) collective-permute-start(bf16[64,2048]{1,0:T(8,128)(2,1)S(1)} %add_convert_fusion.refs_2_), channel_id=1, source_target_pairs={{0,2},{1,3},{2,4},{3,5},{4,0},{5,1},{6,6},{7,7},{8,10},{9,11},{10,... | collective-permute-start | bytes 786440 | tf_op jit(solution)/shard_map/ppermute | solution.py:497
  82.5 21.3 %collective-permute-start.18 = (bf16[64,2048]{1,0:T(8,128)(2,1)S(1)}, bf16[64,2048]{1,0:T(8,128)(2,1)S(1)}, u32[]{:S(2)}, u32[]{:S(2)}) collective-permute-start(bf16[64,2048]{1,0:T(8,128)(2,1)S(1)} %add_convert_fusion.refs_2_), channel_id=1, source_target_pairs={{0,1},{1,0},{2,7},{3,6},{4,3},{5,2},{6,5},{7,4},{8,9},{9,8},{10,15... | collective-permute-start | bytes 786440 | tf_op jit(solution)/shard_map/ppermute | solution.py:497
  92.5 11.3 %collective-permute-start.17 = (bf16[64,2048]{1,0:T(8,128)(2,1)S(1)}, bf16[64,2048]{1,0:T(8,128)(2,1)S(1)}, u32[]{:S(2)}, u32[]{:S(2)}) collective-permute-start(bf16[64,2048]{1,0:T(8,128)(2,1)S(1)} %add_convert_fusion.refs_2_), channel_id=1, source_target_pairs={{0,0},{1,1},{2,6},{3,7},{4,2},{5,3},{6,4},{7,5},{8,8},{9,9},{10,14... | collective-permute-start | bytes 786440 | tf_op jit(solution)/shard_map/ppermute | solution.py:497
  (9 other events, 36.4 us)
